TPU v7x, 32 devices: a whole 2x2x4 slice. The times are simulated.
32 devices in a mesh: groups: 2 (over y), ctx: 4 (over z), tp: 4 (over x, core).
Axes of the slice: x: 2, y: 2, z: 4, core: 2. Of those that a mesh axis runs over, the one named last changes fastest.
Arguments:
- queries: bfloat16 [1152, 8192], P(('groups', 'ctx'), 'tp'), parts along dimension 0, may hold values from -6 to 6
- keys: bfloat16 [1152, 1024], P(('groups', 'ctx'), 'tp'), parts along dimension 0, may hold values from -6 to 6
- values: bfloat16 [1152, 1024], P(('groups', 'ctx'), 'tp'), parts along dimension 0, may hold values from -6 to 6
- residual: bfloat16 [1152, 8192], P(('groups', 'ctx'), 'tp'), parts along dimension 0, may hold values from -4 to 4
- out_weight: bfloat16 [8192, 8192], P('tp', 'ctx'), may hold values from -0.0625 to 0.0625
- value_head: bfloat16 [8192], P('tp'), may hold values from -0.5 to 0.5
- segment_ids: int32 [1152], P(('groups', 'ctx')), parts along dimension 0, may hold values from 0 to 3, as said below
- positions: int32 [1152], P(('groups', 'ctx')), parts along dimension 0, may hold values from 0 to 251, as said below
- turn_ids: int32 [1152], P(('groups', 'ctx')), parts along dimension 0, may hold values from 0 to 15, as said below
Outputs:
- hidden_out: bfloat16 [1152, 8192], P(('groups', 'ctx'), 'tp'), parts along dimension 0
- turn_means: float32 [32], P('groups'), parts along dimension 0
There are 2 independent parts, one for each index of `groups`. A program takes and returns all parts, laid end to end along the dimension named above; an argument that names none is the same for every part. Nothing has to cross between parts.
Inputs may be any that keep to these rules, and one draw needn't show every extreme that they name: `segment_ids`: in token order (the stored order reverted) segment ids never fall; the sequence holds 4 rollouts of 36 to 252 tokens, one of exactly 252. `positions`: A row's position is its token's offset from the first token of its rollout. `turn_ids`: A row's turn id is 4 times its segment id plus how many of its rollout's three turn starts lie at or before its position; turn starts lie at positions 1 to the rollout's length minus 1 and may coincide.
All inputs are finite; a program needn't handle non-finite values.
Results may differ from a plain program's by a relative error of at most 0.013.
Values may be sent and summed in bfloat16 or wider, within the bound.
No kernel may reach another device: no remote copies, remote signals or barrier semaphores. Data moves between devices by JAX's collectives and lax.ppermute only.
A program may use at most 64 MiB of HBM per device.

v0:
```python
import math

import jax
import jax.numpy as jnp
from jax import lax
from jax.sharding import PartitionSpec as P

HEAD_SIZE = 128
TURNS = 16


def shards(
    queries, keys, values, residual, out_weight, value_head, segment_ids, positions, turn_ids
):
    tok_rows = queries.shape[0]
    kv_heads = keys.shape[1] // HEAD_SIZE
    query_head_group = queries.shape[1] // keys.shape[1]
    query_rows = query_head_group * tok_rows
    score_scale = 1.0 / math.sqrt(HEAD_SIZE)
    grouped = (
        queries.reshape(tok_rows, kv_heads, query_head_group, HEAD_SIZE)
        .transpose(1, 2, 0, 3)
        .reshape(kv_heads, query_rows, HEAD_SIZE)
    )
    seg_rows = jnp.tile(segment_ids, query_head_group)
    pos_rows = jnp.tile(positions, query_head_group)

    def update(running, key_block, value_block, seg_block, pos_block):
        allowed = (seg_rows[:, None] == seg_block[None, :]) & (
            pos_block[None, :] <= pos_rows[:, None]
        )
        numerator, row_max, denominator = running
        scores = (
            jnp.einsum("hqd,khd->hqk", grouped, key_block, preferred_element_type=jnp.float32)
            * score_scale
        )
        scores = jnp.where(allowed[None], scores, -1e30)
        new_max = jnp.maximum(row_max, jnp.max(scores, axis=2))
        weights = jnp.where(allowed[None], jnp.exp(scores - new_max[..., None]), 0.0)
        factor = jnp.exp(row_max - new_max)
        denominator = denominator * factor + jnp.sum(weights, axis=2)
        product = jnp.einsum(
            "hqk,khd->hqd",
            weights.astype(jnp.bfloat16),
            value_block,
            preferred_element_type=jnp.float32,
        )
        numerator = numerator * factor[..., None] + product
        return (numerator, new_max, denominator)

    initial = (
        jnp.zeros((kv_heads, query_rows, HEAD_SIZE), jnp.float32),
        jnp.full((kv_heads, query_rows), -1e30, jnp.float32),
        jnp.zeros((kv_heads, query_rows), jnp.float32),
    )
    running = initial
    key_piece = lax.all_gather(keys, "ctx", axis=0, tiled=True)
    value_piece = lax.all_gather(values, "ctx", axis=0, tiled=True)
    seg_piece = lax.all_gather(segment_ids, "ctx", axis=0, tiled=True)
    pos_piece = lax.all_gather(positions, "ctx", axis=0, tiled=True)
    row_count = key_piece.shape[0]
    key_piece = key_piece.reshape(row_count, kv_heads, HEAD_SIZE)
    value_piece = value_piece.reshape(row_count, kv_heads, HEAD_SIZE)
    block_width = math.gcd(row_count, 512)
    block_steps = row_count // block_width
    stacked = (
        key_piece.reshape(block_steps, block_width, kv_heads, HEAD_SIZE),
        value_piece.reshape(block_steps, block_width, kv_heads, HEAD_SIZE),
        seg_piece.reshape(block_steps, block_width),
        pos_piece.reshape(block_steps, block_width),
    )

    def block_step(running_state, block_set):
        return (update(running_state, block_set[0], block_set[1], block_set[2], block_set[3]), None)

    running, _ = lax.scan(block_step, running, stacked)
    numerator, row_max, denominator = running
    attention = (numerator / denominator[..., None]).reshape(
        kv_heads, query_head_group, tok_rows, HEAD_SIZE
    )
    attention = (
        attention.transpose(2, 0, 1, 3)
        .reshape(tok_rows, kv_heads * query_head_group * HEAD_SIZE)
        .astype(jnp.bfloat16)
    )
    partial_value = jnp.dot(
        lax.all_gather(attention, "ctx", axis=0, tiled=True),
        out_weight,
        preferred_element_type=jnp.float32,
    ).astype(jnp.bfloat16)
    term_rows = lax.all_to_all(
        partial_value, "ctx", split_axis=0, concat_axis=1, tiled=True
    ).astype(jnp.float32)
    summed = lax.psum_scatter(
        term_rows.astype(jnp.bfloat16), "tp", scatter_dimension=1, tiled=True
    ).astype(jnp.float32)
    hidden_out = (residual.astype(jnp.float32) + summed).astype(jnp.bfloat16)
    token_score = jnp.dot(hidden_out, value_head, preferred_element_type=jnp.float32)
    one_hot = (turn_ids[:, None] == jnp.arange(TURNS, dtype=jnp.int32)[None, :]).astype(jnp.float32)
    local_sum = jnp.dot(token_score, one_hot, precision=lax.Precision.HIGHEST)
    local_count = jnp.where(lax.axis_index("tp") == 0, jnp.sum(one_hot, axis=0), 0.0)
    totals, counts = lax.psum((local_sum, local_count), ("ctx", "tp"))
    turn_means = totals / jnp.maximum(counts, 1.0)
    return (hidden_out, turn_means)


def solution(mesh):
    return jax.shard_map(
        shards,
        mesh=mesh,
        in_specs=(
            P(("groups", "ctx"), "tp"),
            P(("groups", "ctx"), "tp"),
            P(("groups", "ctx"), "tp"),
            P(("groups", "ctx"), "tp"),
            P("tp", "ctx"),
            P("tp"),
            P(("groups", "ctx")),
            P(("groups", "ctx")),
            P(("groups", "ctx")),
        ),
        out_specs=(P(("groups", "ctx"), "tp"), P("groups")),
        check_vma=False,
    )
```

profile of v0, /device:TPU:0, one launch (start us, length us, event | category | flops | bytes accessed | tf_op | source)
XLA Modules:
  0.0 259.5 jit_solution(10053838486972242503)
XLA Ops:
  7.3 1.2 dynamic-slice
  9.2 0.9 dynamic-update-slice
  10.0 0.9 dynamic-update-slice.1
  10.9 10.0 %all-reduce.2 = (s32[576]{0:T(1024)S(1)}, s32[576]{0:T(1024)S(1)}) all-reduce(s32[576]{0:T(1024)S(1)} %dynamic-update-slice, s32[576]{0:T(1024)S(1)} %dynamic-update-slice.1), channel_id=1, replica_groups=mesh['groups'=2,'ctx'=4,'tp'=4] {'ctx'}, use_global_device_ids=true, to_apply=%add | all-reduce | flops 1152 | bytes 9216
  21.0 1.2 copy.26
  22.3 0.2 copy.18
  22.5 14.0 %all_gather.17 = bf16[576,256]{1,0:T(8,128)(2,1)S(1)} all-gather(bf16[144,256]{1,0:T(8,128)(2,1)S(1)} %copy-done.2), channel_id=1, replica_groups=mesh['groups'=2,'ctx'=4,'tp'=4] {'ctx'}, dimensions={0}, use_global_device_ids=true | all-gather | bytes 368640 | tf_op jit(solution)/shard_map/all_gather | solution.py:57
  36.5 14.3 %all_gather.18 = bf16[576,256]{1,0:T(8,128)(2,1)S(1)} all-gather(bf16[144,256]{1,0:T(8,128)(2,1)S(1)} %copy-done.3), channel_id=1, replica_groups=mesh['groups'=2,'ctx'=4,'tp'=4] {'ctx'}, dimensions={0}, use_global_device_ids=true | all-gather | bytes 368640 | tf_op jit(solution)/shard_map/all_gather | solution.py:58
  50.9 16.4 %while.15 = (s32[]{:T(128)}, f32[2,1152,128]{2,1,0:T(8,128)S(1)}, f32[2,1152]{1,0:T(2,128)S(1)}, f32[2,1152]{1,0:T(2,128)S(1)}, s32[9,64]{1,0:T(8,128)S(1)}, /*i...) while((s32[]{:T(128)}, f32[2,1152,128]{2,1,0:T(8,128)S(1)}, ...), condition=%wide.region_3.4_spmd.clone, body=%wide.region_0.3_spmd.clone.sunk | while | flops 77942016 | bytes 5397265 | solution.py:76
  51.4 0.4 fusion.35
  51.8 0.1 fusion.37
  51.9 0.8 convolution_add_fusion.2
  53.2 0.4 fusion.35
  53.6 0.1 fusion.37
  53.8 0.8 convolution_add_fusion.2
  55.0 0.4 fusion.35
  55.4 0.1 fusion.37
  55.6 0.8 convolution_add_fusion.2
  56.9 0.4 fusion.35
  57.2 0.1 fusion.37
  57.4 0.8 convolution_add_fusion.2
  58.7 0.4 fusion.35
  59.1 0.1 fusion.37
  59.3 0.8 convolution_add_fusion.2
  60.5 0.4 fusion.35
  60.9 0.1 fusion.37
  61.1 0.8 convolution_add_fusion.2
  62.3 0.4 fusion.35
  62.7 0.1 fusion.37
  62.9 0.8 convolution_add_fusion.2
  64.2 0.4 fusion.35
  64.6 0.1 fusion.37
  64.7 0.8 convolution_add_fusion.2
  66.0 0.4 fusion.35
  66.6 0.8 convolution_add_fusion.2
  67.4 0.4 divide_convert_fusion
  67.8 0.2 copy.21
  67.9 1.0 copy.35
  69.0 50.6 %all-gather.2.cloned.1.call-done = bf16[576,2048]{1,0:T(8,128)(2,1)} async-done(((bf16[144,2048]{1,0:T(8,128)(2,1)}), bf16[576,2048]{1,0:T(8,128)(2,1)}) %all-gather.2.cloned.1.call-update) | async-done | bytes 2359312 | tf_op jit(solution)/shard_map/all_gather | solution.py:87
  119.6 8.2 %convolution_convert_fusion = bf16[576,2048]{1,0:T(8,128)(2,1)S(1)} fusion(bf16[576,2048]{1,0:T(8,128)(2,1)} %all-gather.2.cloned.1.call-done, bf16[2048,2048]{1,0:T(8,128)(2,1)} %param.15), kind=kOutput, calls=%fused_computation.28 | convolution fusion | flops 4833017856 | bytes 13107200 | tf_op jit(solution)/shard_map/dot_general | solution.py:86
  127.8 56.5 %all_to_all.19 = bf16[4,144,2048]{2,1,0:T(8,128)(2,1)S(1)} all-to-all(bf16[4,144,2048]{2,1,0:T(8,128)(2,1)S(1)} %bitcast.57), channel_id=1, replica_groups=mesh['groups'=2,'ctx'=4,'tp'=4] {'ctx'}, dimensions={0} | all-to-all | bytes 4718592 | tf_op jit(solution)/shard_map/all_to_all | solution.py:91
  184.4 1.6 copy.25
  186.0 0.7 copy-done.6
  186.8 31.5 %reduce-scatter.2.cloned.1.call-done = bf16[144,2048]{1,0:T(8,128)(2,1)} async-done(((bf16[144,8192]{1,0:T(8,128)(2,1)}), bf16[144,2048]{1,0:T(8,128)(2,1)}) %reduce-scatter.2.cloned.1.call-update) | async-done | bytes 589840 | tf_op jit(solution)/shard_map/reduce_scatter | solution.py:94
  218.3 1.2 add_convert_fusion
  219.5 0.3 convolution_bitcast_fusion
  219.9 32.2 %all-reduce.3 = (f32[16]{0:T(128)S(1)}, f32[16]{0:T(128)S(1)}) all-reduce(f32[16]{0:T(128)S(1)} %convolution_bitcast_fusion.1, f32[16]{0:T(128)S(1)} %broadcast_select_fusion.1), channel_id=1, replica_groups=mesh['groups'=2,'ctx'=4,'tp'=4] {'ctx','tp'}, use_global_device_ids=true, to_apply=%region_5.6 | all-reduce | flops 32 | bytes 256 | tf_op jit(solution)/shard_map/psum | solution.py:102
  252.1 0.5 maximum_divide_fusion
  (123 shorter events, 4.5 us)
Async XLA Ops:
  7.2 112.5 %all-gather.2.cloned.1.call-start = ((), (), s32[]{:S(2)}) async-start(), calls=%async_computation.2 | async-start | bytes 2949120 | tf_op jit(solution)/shard_map/all_gather | solution.py:87
  21.0 1.4 copy-start.2
  22.2 14.3 %copy-start.3 = (bf16[144,256]{1,0:T(8,128)(2,1)S(1)}, bf16[144,256]{1,0:T(8,128)(2,1)}, u32[]{:S(2)}) copy-start(bf16[144,256]{1,0:T(8,128)(2,1)} %param.13) | copy-start | bytes 221188
  22.4 28.5 %copy-start.4 = (s32[144]{0:T(256)S(1)}, s32[144]{0:T(256)}, u32[]{:S(2)}) copy-start(s32[144]{0:T(256)} %param.17) | copy-start | bytes 1732
  22.4 28.5 %copy-start.5 = (s32[144]{0:T(256)S(1)}, s32[144]{0:T(256)}, u32[]{:S(2)}) copy-start(s32[144]{0:T(256)} %param.18) | copy-start | bytes 1732
  68.9 149.3 %reduce-scatter.2.cloned.1.call-start = ((), (), s32[]{:S(2)}) async-start(), calls=%async_computation.3 | async-start | bytes 2949120 | tf_op jit(solution)/shard_map/reduce_scatter | solution.py:94
  185.9 0.7 copy-start.6
  185.9 0.7 copy-start.7
  185.9 32.3 %copy-start.1 = (bf16[144,2048]{1,0:T(8,128)(2,1)S(1)}, bf16[144,2048]{1,0:T(8,128)(2,1)}, u32[]{:S(2)}) copy-start(bf16[144,2048]{1,0:T(8,128)(2,1)} %param.14) | copy-start | bytes 1769476
  219.5 33.2 %copy-start = (bf16[144,2048]{1,0:T(8,128)(2,1)}, bf16[144,2048]{1,0:T(8,128)(2,1)S(1)}, u32[]{:S(2)}) copy-start(bf16[144,2048]{1,0:T(8,128)(2,1)S(1)} %add_convert_fusion) | copy-start | bytes 1769476
Sparse Core Ops, SparseCore 0:
  69.1 50.5 all-gather.1
  186.1 32.1 reduce-scatter.1
where the time goes:
time: 260 us; the launch traced here: 259 us
  blocking collectives  127 us (49%)
  waiting for transfers between devices  82.2 us (32%)
  matrix products  19.2 us (7%)
  between operations  14.9 us (6%)
  local copies, waits for them, and re-layouts  10.1 us (4%)
  other arithmetic  5.05 us (2%)
    all_to_all x1, blocking collectives, shards(): lax.all_to_all(partial_value, 'ctx', split_axis=0, concat_axis=1, tiled=T...  56.5 us
    all_gather x1, waiting for transfers between devices, shards(): lax.all_gather(attention, 'ctx', axis=0, tiled=True)  50.6 us
    psum x1, blocking collectives, shards(): totals, counts = lax.psum((local_sum, local_count), ('ctx', 'tp'))  32.2 us
    reduce_scatter x1, waiting for transfers between devices, shards(): lax.psum_scatter(term_rows.astype(jnp.bfloat16), 'tp', scatter_dimension=...  31.5 us
    all_gather x1, blocking collectives, shards(): value_piece = lax.all_gather(values, 'ctx', axis=0, tiled=True)  14.3 us
    all_gather x1, blocking collectives, shards(): key_piece = lax.all_gather(keys, 'ctx', axis=0, tiled=True)  14 us
    unnamed x1, blocking collectives  9.99 us
    dot_general x1, matrix products, shards(): jnp.dot(lax.all_gather(attention, 'ctx', axis=0, tiled=True), out_weight,...  8.18 us
  transfers between devices with their start and end apart: 2, of which 2 were waited for; matrix products, arithmetic and copies ran while one was open for 0% of the time, Pallas kernels for 0%

commit v1 on v0

v1 whole, which is shorter than its diff:
```python
import functools
import math

import jax
import jax.numpy as jnp
from jax import lax
from jax.experimental import pallas as pl
from jax.experimental.pallas import tpu as pltpu
from jax.sharding import PartitionSpec as P

HEAD_SIZE = 128
TURNS = 16
MASKED = -1e30


def row_tokens(index, n_ctx, tok_rows):
    half = tok_rows // 2
    row = jnp.arange(tok_rows, dtype=jnp.int32)
    return jnp.where(row < half, index * half + row, (2 * n_ctx - 2 - index) * half + row)


def attention_kernel(q_ref, kv_ref, bias_ref, out_ref, *, kv_heads, group, scale):
    bias = bias_ref[...]
    for g in range(kv_heads):
        key = kv_ref[:, g * HEAD_SIZE : (g + 1) * HEAD_SIZE]
        value = kv_ref[:, (kv_heads + g) * HEAD_SIZE : (kv_heads + g + 1) * HEAD_SIZE]
        for h in range(g * group, (g + 1) * group):
            cols = slice(h * HEAD_SIZE, (h + 1) * HEAD_SIZE)
            scores = lax.dot_general(
                q_ref[:, cols], key, (((1,), (1,)), ((), ())), preferred_element_type=jnp.float32
            )
            scores = scores * scale + bias
            weights = jnp.exp(scores - jnp.max(scores, axis=1, keepdims=True))
            denominator = jnp.sum(weights, axis=1, keepdims=True)
            numerator = jnp.dot(
                weights.astype(jnp.bfloat16), value, preferred_element_type=jnp.float32
            )
            out_ref[:, cols] = (numerator / denominator).astype(jnp.bfloat16)


def attend(queries, kv, bias):
    kv_heads = kv.shape[1] // (2 * HEAD_SIZE)
    heads = queries.shape[1] // HEAD_SIZE
    rows, keys = bias.shape
    return pl.pallas_call(
        functools.partial(
            attention_kernel,
            kv_heads=kv_heads,
            group=heads // kv_heads,
            scale=1.0 / math.sqrt(HEAD_SIZE),
        ),
        out_shape=jax.ShapeDtypeStruct(queries.shape, jnp.bfloat16),
        in_specs=[pl.BlockSpec(memory_space=pltpu.VMEM)] * 3,
        out_specs=pl.BlockSpec(memory_space=pltpu.VMEM),
        compiler_params=pltpu.CompilerParams(vmem_limit_bytes=40 * 1024 * 1024),
        cost_estimate=pl.CostEstimate(
            flops=4 * heads * rows * keys * HEAD_SIZE,
            bytes_accessed=2 * (2 * queries.size + kv.size) + 4 * bias.size,
            transcendentals=heads * rows * keys,
        ),
        name="attention",
    )(queries, kv, bias)


def butterfly_sum(x, axes, sizes):
    total = math.prod(sizes)
    if total & (total - 1):
        return lax.psum(x, axes)
    bit = 1
    while bit < total:
        x = x + lax.ppermute(x, axes, [(i, i ^ bit) for i in range(total)])
        bit *= 2
    return x


def shards(
    n_ctx,
    n_tp,
    queries,
    keys,
    values,
    residual,
    out_weight,
    value_head,
    segment_ids,
    positions,
    turn_ids,
):
    tok_rows = queries.shape[0]
    ctx = lax.axis_index("ctx")

    def ring(x, step):
        return lax.ppermute(x, "ctx", [(i, (i + step) % n_ctx) for i in range(n_ctx)])

    own_kv = jnp.concatenate([keys, values], axis=1)
    kv = jnp.concatenate([own_kv] + [ring(own_kv, s) for s in range(1, n_ctx)], axis=0)
    key_tokens = jnp.concatenate(
        [row_tokens((ctx - s) % n_ctx, n_ctx, tok_rows) for s in range(n_ctx)]
    )
    tokens = row_tokens(ctx, n_ctx, tok_rows)
    allowed = (key_tokens[None, :] <= tokens[:, None]) & (
        key_tokens[None, :] >= (tokens - positions)[:, None]
    )
    bias = jnp.where(allowed, 0.0, MASKED).astype(jnp.float32)
    piece = attend(queries, kv, bias)

    def project(rows):
        return jnp.dot(rows, out_weight, preferred_element_type=jnp.float32)

    both = ("ctx", "tp")
    if n_ctx == n_tp and n_tp & (n_tp - 1) == 0:
        summed = None
        for s in range(n_ctx):
            following = ring(piece, 1) if s + 1 < n_ctx else None
            part = project(piece)
            bit = 1
            while bit < n_tp:
                pairs = []
                for c in range(n_ctx):
                    for t in range(n_tp):
                        if (t ^ c) & bit and (t ^ c) & (bit - 1) == 0:
                            pairs.append((c * n_tp + t, c * n_tp + (t ^ bit)))
                arrived = lax.ppermute(part.astype(jnp.bfloat16), both, pairs)
                part = part + arrived.astype(jnp.float32)
                bit *= 2
            if s == 0:
                mine = lax.axis_index("tp") == ctx
                summed = jnp.where(mine, part, 0.0)
            else:
                pairs = [(c * n_tp + c, ((c - s) % n_ctx) * n_tp + c) for c in range(n_ctx)]
                summed = summed + lax.ppermute(part.astype(jnp.bfloat16), both, pairs).astype(
                    jnp.float32
                )
            piece = following
    else:
        partial_value = project(lax.all_gather(piece, "ctx", axis=0, tiled=True))
        term_rows = lax.all_to_all(
            partial_value.astype(jnp.bfloat16), "ctx", split_axis=0, concat_axis=1, tiled=True
        )
        summed = lax.psum_scatter(term_rows, "tp", scatter_dimension=1, tiled=True)
        summed = summed.astype(jnp.float32)
    hidden_out = (residual.astype(jnp.float32) + summed).astype(jnp.bfloat16)
    token_score = jnp.dot(hidden_out, value_head, preferred_element_type=jnp.float32)
    one_hot = (turn_ids[:, None] == jnp.arange(TURNS, dtype=jnp.int32)[None, :]).astype(jnp.float32)
    local_sum = jnp.dot(token_score, one_hot, precision=lax.Precision.HIGHEST)
    local_count = jnp.where(lax.axis_index("tp") == 0, jnp.sum(one_hot, axis=0), 0.0)
    totals = butterfly_sum(jnp.stack([local_sum, local_count]), both, (n_ctx, n_tp))
    turn_means = totals[0] / jnp.maximum(totals[1], 1.0)
    return (hidden_out, turn_means)


def solution(mesh):
    return jax.shard_map(
        functools.partial(shards, mesh.shape["ctx"], mesh.shape["tp"]),
        mesh=mesh,
        in_specs=(
            P(("groups", "ctx"), "tp"),
            P(("groups", "ctx"), "tp"),
            P(("groups", "ctx"), "tp"),
            P(("groups", "ctx"), "tp"),
            P("tp", "ctx"),
            P("tp"),
            P(("groups", "ctx")),
            P(("groups", "ctx")),
            P(("groups", "ctx")),
        ),
        out_specs=(P(("groups", "ctx"), "tp"), P("groups")),
        check_vma=False,
    )
```

time: 260 us -> 131 us (0.50)
  blocking collectives: 127 us -> 0 us
  starting transfers between devices: 0.08 us -> 36.6 us
  between operations: 14.9 us -> 0.94 us
  waiting for transfers between devices: 82.2 us -> 69.2 us
  matrix products: 19.2 us -> 9.82 us
  local copies, waits for them, and re-layouts: 10.1 us -> 1.88 us
  Pallas kernels: 0 us -> 5.25 us
    ppermute x0 -> x21, waiting for transfers between devices: none -> 69.2 us  [the longest x6 42.9 us: ring(): lax.ppermute(x, 'ctx', [(i, (i + step) % n_ctx) for i in range(n_ctx)])]
    all_to_all x1 -> x0, blocking collectives: 56.5 us -> none  [shards(): lax.all_to_all(partial_value, 'ctx', split_axis=0, concat_axis=1, tiled=T...]
    all_gather x1 -> x0, waiting for transfers between devices: 50.6 us -> none  [shards(): lax.all_gather(attention, 'ctx', axis=0, tiled=True)]
    ppermute x0 -> x21, starting transfers between devices: none -> 36.6 us  [the longest x4 12.8 us: butterfly_sum(): x = x + lax.ppermute(x, axes, [(i, i ^ bit) for i in range(total)])]
    psum x1 -> x0, blocking collectives: 32.2 us -> none  [shards(): totals, counts = lax.psum((local_sum, local_count), ('ctx', 'tp'))]
    reduce_scatter x1 -> x0, waiting for transfers between devices: 31.5 us -> none  [shards(): lax.psum_scatter(term_rows.astype(jnp.bfloat16), 'tp', scatter_dimension=...]
    all_gather x2 -> x0, blocking collectives: 28.3 us -> none  [the longest x1 14.3 us: shards(): value_piece = lax.all_gather(values, 'ctx', axis=0, tiled=True)]
    unnamed x1 -> x0, blocking collectives: 9.99 us -> none
  transfers between devices with their start and end apart: 2 -> 21, of which waited for: 2 -> 14; matrix products, arithmetic and copies ran while one was open for 0% -> 11% of each run, Pallas kernels for 0% -> 0%
where the time goes in v1:
time: 131 us
  waiting for transfers between devices  69.2 us (53%)
  starting transfers between devices  36.6 us (28%)
  matrix products  9.82 us (7%)
  other arithmetic  7.3 us (6%)
  Pallas kernels  5.25 us (4%)
  local copies, waits for them, and re-layouts  1.88 us (1%)
    ppermute x6, waiting for transfers between devices, ring(): lax.ppermute(x, 'ctx', [(i, (i + step) % n_ctx) for i in range(n_ctx)])  42.9 us
    ppermute x8, waiting for transfers between devices, shards(): arrived = lax.ppermute(part.astype(jnp.bfloat16), both, pairs)  13.8 us
    ppermute x4, starting transfers between devices, butterfly_sum(): x = x + lax.ppermute(x, axes, [(i, i ^ bit) for i in range(total)])  12.8 us
    ppermute x8, starting transfers between devices, shards(): arrived = lax.ppermute(part.astype(jnp.bfloat16), both, pairs)  10.3 us
    dot_general x4, matrix products, project(): return jnp.dot(rows, out_weight, preferred_element_type=jnp.float32)  9.43 us
    ppermute x6, starting transfers between devices, ring(): lax.ppermute(x, 'ctx', [(i, (i + step) % n_ctx) for i in range(n_ctx)])  7.01 us
    ppermute x3, waiting for transfers between devices, shards(): lax.ppermute(part.astype(jnp.bfloat16), both, pairs).astype(jnp.float32)  6.83 us
    ppermute x3, starting transfers between devices, shards(): lax.ppermute(part.astype(jnp.bfloat16), both, pairs).astype(jnp.float32)  6.48 us
  transfers between devices with their start and end apart: 21, of which 14 were waited for; matrix products, arithmetic and copies ran while one was open for 11% of the time, Pallas kernels for 0%

profile of v1, /device:TPU:0, one launch (start us, length us, event | category | flops | bytes accessed | tf_op | source)
XLA Modules:
  0.0 131.0 jit_solution(5027871193015552911)
XLA Ops:
  0.6 1.0 constant_dynamic-update-slice_fusion.1
  1.6 0.9 constant_dynamic-update-slice_fusion
  2.5 5.0 %collective-permute-start.2 = (bf16[144,512]{1,0:T(8,128)(2,1)S(1)}, bf16[144,512]{1,0:T(8,128)(2,1)S(1)}, u32[]{:S(2)}, u32[]{:S(2)}) collective-permute-start(bf16[144,512]{1,0:T(8,128)(2,1)S(1)} %constant_dynamic-update-slice_fusion), channel_id=1, source_target_pairs={{0,12},{4,0},{8,4},{12,8},{1,13},{5,1},{9,5},{13,9},{2,14},{6,2},{... | collective-permute-start | bytes 442376 | tf_op jit(solution)/shard_map/ppermute | solution.py:93
  7.5 1.0 collective-permute-start
  8.5 0.7 add_select_fusion
  9.4 2.4 %collective-permute-done.2 = bf16[144,512]{1,0:T(8,128)(2,1)S(1)} collective-permute-done((bf16[144,512]{1,0:T(8,128)(2,1)S(1)}, bf16[144,512]{1,0:T(8,128)(2,1)S(1)}, u32[]{:S(2)}, u32[]{:S(2)}) %collective-permute-start.2) | collective-permute-done | bytes 147488 | tf_op jit(solution)/shard_map/ppermute | solution.py:93
  11.8 8.2 %collective-permute-done.1 = bf16[144,512]{1,0:T(8,128)(2,1)S(1)} collective-permute-done((bf16[144,512]{1,0:T(8,128)(2,1)S(1)}, bf16[144,512]{1,0:T(8,128)(2,1)S(1)}, u32[]{:S(2)}, u32[]{:S(2)}) %collective-permute-start.1) | collective-permute-done | bytes 147488 | tf_op jit(solution)/shard_map/ppermute | solution.py:93
  20.1 5.3 %attention.1 = bf16[144,2048]{1,0:T(8,128)(2,1)S(1)} custom-call(bf16[144,2048]{1,0:T(8,128)(2,1)S(1)} %copy-done, bf16[576,512]{1,0:T(8,128)(2,1)S(1)} %pad_maximum_fusion.kv_ref, f32[144,576]{1,0:T(8,128)S(1)} %and_select_fusion.bias_ref), custom_call_target="tpu_custom_call" | custom-call | flops 679477248 | bytes 2101248 | tf_op jit(solution)/shard_map/attention/pallas_call | solution.py:45
  25.3 0.9 collective-permute-start.5
  26.3 5.1 %fusion.13 = (bf16[144,2048]{1,0:T(8,128)(2,1)S(1)}, f32[144,2048]{1,0:T(8,128)S(1)}) fusion(bf16[144,2048]{1,0:T(8,128)(2,1)S(1)} %attention.1, bf16[2048,2048]{1,0:T(8,128)(2,1)} %param.13), kind=kOutput, calls=%fused_computation.38 | convolution fusion | flops 1208254464 | bytes 10747904 | tf_op jit(solution)/shard_map/dot_general | solution.py:108
  31.4 10.4 %collective-permute-done.5 = bf16[144,2048]{1,0:T(8,128)(2,1)S(1)} collective-permute-done((bf16[144,2048]{1,0:T(8,128)(2,1)S(1)}, bf16[144,2048]{1,0:T(8,128)(2,1)S(1)}, u32[]{:S(2)}, u32[]{:S(2)}) %collective-permute-start.5) | collective-permute-done | bytes 589856 | tf_op jit(solution)/shard_map/ppermute | solution.py:93
  41.8 1.3 collective-permute-start.3
  43.2 1.4 %fusion.12 = (bf16[144,2048]{1,0:T(8,128)(2,1)S(1)}, f32[144,2048]{1,0:T(8,128)S(1)}) fusion(bf16[144,2048]{1,0:T(8,128)(2,1)S(1)} %collective-permute-done.5, bf16[2048,2048]{1,0:T(8,128)(2,1)S(1)} %bitcast.20), kind=kOutput, calls=%fused_computation.37 | convolution fusion | flops 1208254464 | bytes 10747904 | tf_op jit(solution)/shard_map/dot_general | solution.py:108
  44.6 1.3 collective-permute-start.6
  45.9 11.4 %collective-permute-done.9 = bf16[144,2048]{1,0:T(8,128)(2,1)S(1)} collective-permute-done((bf16[144,2048]{1,0:T(8,128)(2,1)S(1)}, bf16[144,2048]{1,0:T(8,128)(2,1)S(1)}, u32[]{:S(2)}, u32[]{:S(2)}) %collective-permute-start.9) | collective-permute-done | bytes 589856 | tf_op jit(solution)/shard_map/ppermute | solution.py:93
  57.4 0.1 fusion
  57.5 1.3 collective-permute-start.4
  58.8 1.4 %fusion.11 = (bf16[144,2048]{1,0:T(8,128)(2,1)S(1)}, f32[144,2048]{1,0:T(8,128)S(1)}) fusion(bf16[144,2048]{1,0:T(8,128)(2,1)S(1)} %collective-permute-done.9, bf16[2048,2048]{1,0:T(8,128)(2,1)S(1)} %bitcast.20), kind=kOutput, calls=%fused_computation.36 | convolution fusion | flops 1208254464 | bytes 10747904 | tf_op jit(solution)/shard_map/dot_general | solution.py:108
  60.2 1.3 collective-permute-start.10
  61.5 10.4 %collective-permute-done.13 = bf16[144,2048]{1,0:T(8,128)(2,1)S(1)} collective-permute-done((bf16[144,2048]{1,0:T(8,128)(2,1)S(1)}, bf16[144,2048]{1,0:T(8,128)(2,1)S(1)}, u32[]{:S(2)}, u32[]{:S(2)}) %collective-permute-start.13) | collective-permute-done | bytes 589856 | tf_op jit(solution)/shard_map/ppermute | solution.py:93
  72.0 1.4 %fusion.10 = (bf16[144,2048]{1,0:T(8,128)(2,1)S(1)}, f32[144,2048]{1,0:T(8,128)S(1)}) fusion(bf16[144,2048]{1,0:T(8,128)(2,1)S(1)} %collective-permute-done.13, bf16[2048,2048]{1,0:T(8,128)(2,1)S(1)} %bitcast.20), kind=kOutput, calls=%fused_computation.35 | convolution fusion | flops 1208254464 | bytes 10747904 | tf_op jit(solution)/shard_map/dot_general | solution.py:108
  73.4 1.3 collective-permute-start.14
  74.7 0.1 fusion.1
  74.8 1.3 collective-permute-start.7
  76.3 1.3 collective-permute-start.11
  77.7 1.3 collective-permute-start.15
  79.0 7.6 %collective-permute-done.7 = bf16[144,2048]{1,0:T(8,128)(2,1)S(1)} collective-permute-done((bf16[144,2048]{1,0:T(8,128)(2,1)S(1)}, bf16[144,2048]{1,0:T(8,128)(2,1)S(1)}, u32[]{:S(2)}, u32[]{:S(2)}) %collective-permute-start.7) | collective-permute-done | bytes 589856 | tf_op jit(solution)/shard_map/ppermute | solution.py:123
  86.6 1.1 add_convert_fusion.3
  87.7 2.1 %collective-permute-start.8 = (bf16[144,2048]{1,0:T(8,128)(2,1)}, bf16[144,2048]{1,0:T(8,128)(2,1)}, u32[]{:S(2)}, u32[]{:S(2)}) collective-permute-start(bf16[144,2048]{1,0:T(8,128)(2,1)} %add_convert_fusion.3), channel_id=1, source_target_pairs={{0,12},{5,1},{10,6},{15,11},{16,28},{21,17},{26,22},{31,27}} | collective-permute-start | bytes 1769480 | tf_op jit(solution)/shard_map/ppermute | solution.py:131
  89.8 3.1 %collective-permute-done.11 = bf16[144,2048]{1,0:T(8,128)(2,1)S(1)} collective-permute-done((bf16[144,2048]{1,0:T(8,128)(2,1)S(1)}, bf16[144,2048]{1,0:T(8,128)(2,1)S(1)}, u32[]{:S(2)}, u32[]{:S(2)}) %collective-permute-start.11) | collective-permute-done | bytes 589856 | tf_op jit(solution)/shard_map/ppermute | solution.py:123
  92.9 1.1 add_convert_fusion.2
  94.0 2.2 %collective-permute-start.12 = (bf16[144,2048]{1,0:T(8,128)(2,1)}, bf16[144,2048]{1,0:T(8,128)(2,1)}, u32[]{:S(2)}, u32[]{:S(2)}) collective-permute-start(bf16[144,2048]{1,0:T(8,128)(2,1)} %add_convert_fusion.2), channel_id=1, source_target_pairs={{0,8},{5,13},{10,2},{15,7},{16,24},{21,29},{26,18},{31,23}} | collective-permute-start | bytes 1769480 | tf_op jit(solution)/shard_map/ppermute | solution.py:131
  96.2 3.0 %collective-permute-done.15 = bf16[144,2048]{1,0:T(8,128)(2,1)S(1)} collective-permute-done((bf16[144,2048]{1,0:T(8,128)(2,1)S(1)}, bf16[144,2048]{1,0:T(8,128)(2,1)S(1)}, u32[]{:S(2)}, u32[]{:S(2)}) %collective-permute-start.15) | collective-permute-done | bytes 589856 | tf_op jit(solution)/shard_map/ppermute | solution.py:123
  99.3 1.0 add_convert_fusion.1
  100.3 2.1 %collective-permute-start.16 = (bf16[144,2048]{1,0:T(8,128)(2,1)}, bf16[144,2048]{1,0:T(8,128)(2,1)}, u32[]{:S(2)}, u32[]{:S(2)}) collective-permute-start(bf16[144,2048]{1,0:T(8,128)(2,1)} %add_convert_fusion.1), channel_id=1, source_target_pairs={{0,4},{5,9},{10,14},{15,3},{16,20},{21,25},{26,30},{31,19}} | collective-permute-start | bytes 1769480 | tf_op jit(solution)/shard_map/ppermute | solution.py:131
  102.6 0.5 collective-permute-done.12
  103.1 6.3 %collective-permute-done.16 = bf16[144,2048]{1,0:T(8,128)(2,1)} collective-permute-done((bf16[144,2048]{1,0:T(8,128)(2,1)}, bf16[144,2048]{1,0:T(8,128)(2,1)}, u32[]{:S(2)}, u32[]{:S(2)}) %collective-permute-start.16) | collective-permute-done | bytes 589856 | tf_op jit(solution)/shard_map/ppermute | solution.py:131
  109.4 2.0 %add_convert_fusion = bf16[144,2048]{1,0:T(8,128)(2,1)S(1)} fusion(bf16[144,2048]{1,0:T(8,128)(2,1)} %collective-permute-done.16, bf16[144,2048]{1,0:T(8,128)(2,1)} %collective-permute-done.12, bf16[144,2048]{1,0:T(8,128)(2,1)} %collective-permute-done.8, bf16[144,2048]{1,0:T(8,128)(2,1)S(1)} %collective-permute-done.4, bf16[144,2048]{1,0:T(8,128)(2,1)S(1)} %copy-done.2, ...), kind=kLoop, calls=%fused_computation | loop fusion | flops 4128768 | bytes 5308417 | tf_op jit(solution)/shard_map/convert_element_type | solution.py:142
  111.5 0.3 convolution_bitcast_fusion
  111.7 0.1 fusion.4
  112.0 1.1 collective-permute-done.17
  113.1 5.1 %collective-permute-start.18 = (f32[2,16]{1,0:T(2,128)S(1)}, f32[2,16]{1,0:T(2,128)S(1)}, u32[]{:S(2)}, u32[]{:S(2)}) collective-permute-start(f32[2,16]{1,0:T(2,128)S(1)} %fusion.9), channel_id=1, source_target_pairs={{0,2},{1,3},{2,0},{3,1},{4,6},{5,7},{6,4},{7,5},{8,10},{9,11},{10,... | collective-permute-start | bytes 392 | tf_op jit(solution)/shard_map/ppermute | solution.py:71
  118.2 1.5 %collective-permute-done.18 = f32[2,16]{1,0:T(2,128)S(1)} collective-permute-done((f32[2,16]{1,0:T(2,128)S(1)}, f32[2,16]{1,0:T(2,128)S(1)}, u32[]{:S(2)}, u32[]{:S(2)}) %collective-permute-start.18) | collective-permute-done | bytes 160 | tf_op jit(solution)/shard_map/ppermute | solution.py:71
  119.8 4.0 %collective-permute-start.19 = (f32[2,16]{1,0:T(2,128)S(1)}, f32[2,16]{1,0:T(2,128)S(1)}, u32[]{:S(2)}, u32[]{:S(2)}) collective-permute-start(f32[2,16]{1,0:T(2,128)S(1)} %fusion.25), channel_id=1, source_target_pairs={{0,4},{1,5},{2,6},{3,7},{4,0},{5,1},{6,2},{7,3},{8,12},{9,13},{10,... | collective-permute-start | bytes 392 | tf_op jit(solution)/shard_map/ppermute | solution.py:71
  123.7 1.5 %collective-permute-done.19 = f32[2,16]{1,0:T(2,128)S(1)} collective-permute-done((f32[2,16]{1,0:T(2,128)S(1)}, f32[2,16]{1,0:T(2,128)S(1)}, u32[]{:S(2)}, u32[]{:S(2)}) %collective-permute-start.19) | collective-permute-done | bytes 160 | tf_op jit(solution)/shard_map/ppermute | solution.py:71
  125.3 3.6 %collective-permute-start.20 = (f32[2,16]{1,0:T(2,128)S(1)}, f32[2,16]{1,0:T(2,128)S(1)}, u32[]{:S(2)}, u32[]{:S(2)}) collective-permute-start(f32[2,16]{1,0:T(2,128)S(1)} %add.170), channel_id=1, source_target_pairs={{0,8},{1,9},{2,10},{3,11},{4,12},{5,13},{6,14},{7,15},{8,0},{9,1},... | collective-permute-start | bytes 392 | tf_op jit(solution)/shard_map/ppermute | solution.py:71
  128.9 1.5 %collective-permute-done.20 = f32[2,16]{1,0:T(2,128)S(1)} collective-permute-done((f32[2,16]{1,0:T(2,128)S(1)}, f32[2,16]{1,0:T(2,128)S(1)}, u32[]{:S(2)}, u32[]{:S(2)}) %collective-permute-start.20) | collective-permute-done | bytes 160 | tf_op jit(solution)/shard_map/ppermute | solution.py:71
  130.5 0.5 fusion.7
  (41 shorter events, 0.8 us)
Async XLA Ops:
  0.6 19.4 %copy-start = (bf16[144,2048]{1,0:T(8,128)(2,1)S(1)}, bf16[144,2048]{1,0:T(8,128)(2,1)}, u32[]{:S(2)}) copy-start(bf16[144,2048]{1,0:T(8,128)(2,1)} %q_ref.1) | copy-start | bytes 1769476
  2.5 9.3 %collective-permute-start.2 = (bf16[144,512]{1,0:T(8,128)(2,1)S(1)}, bf16[144,512]{1,0:T(8,128)(2,1)S(1)}, u32[]{:S(2)}, u32[]{:S(2)}) collective-permute-start(bf16[144,512]{1,0:T(8,128)(2,1)S(1)} %constant_dynamic-update-slice_fusion), channel_id=1, source_target_pairs={{0,12},{4,0},{8,4},{12,8},{1,13},{5,1},{9,5},{13,9},{2,14},{6,2},{... | collective-permute-start | bytes 442376 | tf_op jit(solution)/shard_map/ppermute | solution.py:93
  7.5 12.5 %collective-permute-start.1 = (bf16[144,512]{1,0:T(8,128)(2,1)S(1)}, bf16[144,512]{1,0:T(8,128)(2,1)S(1)}, u32[]{:S(2)}, u32[]{:S(2)}) collective-permute-start(bf16[144,512]{1,0:T(8,128)(2,1)S(1)} %constant_dynamic-update-slice_fusion), channel_id=1, source_target_pairs={{0,8},{4,12},{8,0},{12,4},{1,9},{5,13},{9,1},{13,5},{2,10},{6,14},... | collective-permute-start | bytes 442376 | tf_op jit(solution)/shard_map/ppermute | solution.py:93
  7.5 12.5 %collective-permute-start = (bf16[144,512]{1,0:T(8,128)(2,1)S(1)}, bf16[144,512]{1,0:T(8,128)(2,1)S(1)}, u32[]{:S(2)}, u32[]{:S(2)}) collective-permute-start(bf16[144,512]{1,0:T(8,128)(2,1)S(1)} %constant_dynamic-update-slice_fusion), channel_id=1, source_target_pairs={{0,4},{4,8},{8,12},{12,0},{1,5},{5,9},{9,13},{13,1},{2,6},{6,10},{... | collective-permute-start | bytes 442376 | tf_op jit(solution)/shard_map/ppermute | solution.py:93
  20.1 23.1 %slice-start = ((s8[8388608]{0:T(1024)(128)(4,1)}), s8[4194304]{0:T(1024)(128)(4,1)S(1)}, s32[]{:S(2)}) async-start(s8[8388608]{0:T(1024)(128)(4,1)} %bitcast.19), calls=%async_computation | async-start | bytes 8388608
  25.3 17.8 %slice-start.1 = ((s8[8388608]{0:T(1024)(128)(4,1)}), s8[4194304]{0:T(1024)(128)(4,1)S(1)}, s32[]{:S(2)}) async-start(s8[8388608]{0:T(1024)(128)(4,1)} %bitcast.19), calls=%async_computation.1 | async-start | bytes 8388608
  25.3 16.5 %collective-permute-start.5 = (bf16[144,2048]{1,0:T(8,128)(2,1)S(1)}, bf16[144,2048]{1,0:T(8,128)(2,1)S(1)}, u32[]{:S(2)}, u32[]{:S(2)}) collective-permute-start(bf16[144,2048]{1,0:T(8,128)(2,1)S(1)} %attention.1), channel_id=1, source_target_pairs={{0,4},{4,8},{8,12},{12,0},{1,5},{5,9},{9,13},{13,1},{2,6},{6,10},{... | collective-permute-start | bytes 1769480 | tf_op jit(solution)/shard_map/ppermute | solution.py:93
  41.8 15.5 %collective-permute-start.9 = (bf16[144,2048]{1,0:T(8,128)(2,1)S(1)}, bf16[144,2048]{1,0:T(8,128)(2,1)S(1)}, u32[]{:S(2)}, u32[]{:S(2)}) collective-permute-start(bf16[144,2048]{1,0:T(8,128)(2,1)S(1)} %collective-permute-done.5), channel_id=1, source_target_pairs={{0,4},{4,8},{8,12},{12,0},{1,5},{5,9},{9,13},{13,1},{2,6},{6,10},{... | collective-permute-start | bytes 1769480 | tf_op jit(solution)/shard_map/ppermute | solution.py:93
  41.8 15.5 %collective-permute-start.3 = (bf16[144,2048]{1,0:T(8,128)(2,1)S(1)}, bf16[144,2048]{1,0:T(8,128)(2,1)S(1)}, u32[]{:S(2)}, u32[]{:S(2)}) collective-permute-start(bf16[144,2048]{1,0:T(8,128)(2,1)S(1)} %get-tuple-element.8), channel_id=1, source_target_pairs={{1,0},{3,2},{4,5},{6,7},{9,8},{11,10},{12,13},{14,15},{17,16},{19,... | collective-permute-start | bytes 1769480 | tf_op jit(solution)/shard_map/ppermute | solution.py:123
  44.6 30.1 %collective-permute-start.6 = (bf16[144,2048]{1,0:T(8,128)(2,1)S(1)}, bf16[144,2048]{1,0:T(8,128)(2,1)S(1)}, u32[]{:S(2)}, u32[]{:S(2)}) collective-permute-start(bf16[144,2048]{1,0:T(8,128)(2,1)S(1)} %get-tuple-element.6), channel_id=1, source_target_pairs={{1,0},{3,2},{4,5},{6,7},{9,8},{11,10},{12,13},{14,15},{17,16},{19,... | collective-permute-start | bytes 1769480 | tf_op jit(solution)/shard_map/ppermute | solution.py:123
  57.4 14.6 %collective-permute-start.13 = (bf16[144,2048]{1,0:T(8,128)(2,1)S(1)}, bf16[144,2048]{1,0:T(8,128)(2,1)S(1)}, u32[]{:S(2)}, u32[]{:S(2)}) collective-permute-start(bf16[144,2048]{1,0:T(8,128)(2,1)S(1)} %collective-permute-done.9), channel_id=1, source_target_pairs={{0,4},{4,8},{8,12},{12,0},{1,5},{5,9},{9,13},{13,1},{2,6},{6,10},{... | collective-permute-start | bytes 1769480 | tf_op jit(solution)/shard_map/ppermute | solution.py:93
  57.5 45.1 %collective-permute-start.4 = (bf16[144,2048]{1,0:T(8,128)(2,1)S(1)}, bf16[144,2048]{1,0:T(8,128)(2,1)S(1)}, u32[]{:S(2)}, u32[]{:S(2)}) collective-permute-start(bf16[144,2048]{1,0:T(8,128)(2,1)S(1)} %fusion), channel_id=1, source_target_pairs={{2,0},{7,5},{8,10},{13,15},{18,16},{23,21},{24,26},{29,31}} | collective-permute-start | bytes 1769480 | tf_op jit(solution)/shard_map/ppermute | solution.py:123
  60.2 15.9 %collective-permute-start.10 = (bf16[144,2048]{1,0:T(8,128)(2,1)S(1)}, bf16[144,2048]{1,0:T(8,128)(2,1)S(1)}, u32[]{:S(2)}, u32[]{:S(2)}) collective-permute-start(bf16[144,2048]{1,0:T(8,128)(2,1)S(1)} %get-tuple-element.4), channel_id=1, source_target_pairs={{1,0},{3,2},{4,5},{6,7},{9,8},{11,10},{12,13},{14,15},{17,16},{19,... | collective-permute-start | bytes 1769480 | tf_op jit(solution)/shard_map/ppermute | solution.py:123
  73.4 4.2 %collective-permute-start.14 = (bf16[144,2048]{1,0:T(8,128)(2,1)S(1)}, bf16[144,2048]{1,0:T(8,128)(2,1)S(1)}, u32[]{:S(2)}, u32[]{:S(2)}) collective-permute-start(bf16[144,2048]{1,0:T(8,128)(2,1)S(1)} %get-tuple-element.2), channel_id=1, source_target_pairs={{1,0},{3,2},{4,5},{6,7},{9,8},{11,10},{12,13},{14,15},{17,16},{19,... | collective-permute-start | bytes 1769480 | tf_op jit(solution)/shard_map/ppermute | solution.py:123
  74.8 11.8 %collective-permute-start.7 = (bf16[144,2048]{1,0:T(8,128)(2,1)S(1)}, bf16[144,2048]{1,0:T(8,128)(2,1)S(1)}, u32[]{:S(2)}, u32[]{:S(2)}) collective-permute-start(bf16[144,2048]{1,0:T(8,128)(2,1)S(1)} %fusion.1), channel_id=1, source_target_pairs={{2,0},{7,5},{8,10},{13,15},{18,16},{23,21},{24,26},{29,31}} | collective-permute-start | bytes 1769480 | tf_op jit(solution)/shard_map/ppermute | solution.py:123
  76.3 16.7 %collective-permute-start.11 = (bf16[144,2048]{1,0:T(8,128)(2,1)S(1)}, bf16[144,2048]{1,0:T(8,128)(2,1)S(1)}, u32[]{:S(2)}, u32[]{:S(2)}) collective-permute-start(bf16[144,2048]{1,0:T(8,128)(2,1)S(1)} %fusion.2), channel_id=1, source_target_pairs={{2,0},{7,5},{8,10},{13,15},{18,16},{23,21},{24,26},{29,31}} | collective-permute-start | bytes 1769480 | tf_op jit(solution)/shard_map/ppermute | solution.py:123
  77.7 21.5 %collective-permute-start.15 = (bf16[144,2048]{1,0:T(8,128)(2,1)S(1)}, bf16[144,2048]{1,0:T(8,128)(2,1)S(1)}, u32[]{:S(2)}, u32[]{:S(2)}) collective-permute-start(bf16[144,2048]{1,0:T(8,128)(2,1)S(1)} %fusion.3), channel_id=1, source_target_pairs={{2,0},{7,5},{8,10},{13,15},{18,16},{23,21},{24,26},{29,31}} | collective-permute-start | bytes 1769480 | tf_op jit(solution)/shard_map/ppermute | solution.py:123
  87.7 14.9 %collective-permute-start.8 = (bf16[144,2048]{1,0:T(8,128)(2,1)}, bf16[144,2048]{1,0:T(8,128)(2,1)}, u32[]{:S(2)}, u32[]{:S(2)}) collective-permute-start(bf16[144,2048]{1,0:T(8,128)(2,1)} %add_convert_fusion.3), channel_id=1, source_target_pairs={{0,12},{5,1},{10,6},{15,11},{16,28},{21,17},{26,22},{31,27}} | collective-permute-start | bytes 1769480 | tf_op jit(solution)/shard_map/ppermute | solution.py:131
  94.0 8.4 %copy-start.3 = (bf16[2048]{0:T(1024)(128)(2,1)S(1)}, bf16[2048]{0:T(1024)(128)(2,1)}, u32[]{:S(2)}) copy-start(bf16[2048]{0:T(1024)(128)(2,1)} %param.14) | copy-start | bytes 12292
  94.0 8.5 %copy-start.4 = (s32[144]{0:T(256)S(1)}, s32[144]{0:T(256)}, u32[]{:S(2)}) copy-start(s32[144]{0:T(256)} %param.16) | copy-start | bytes 1732
  94.0 15.4 %copy-start.2 = (bf16[144,2048]{1,0:T(8,128)(2,1)S(1)}, bf16[144,2048]{1,0:T(8,128)(2,1)}, u32[]{:S(2)}) copy-start(bf16[144,2048]{1,0:T(8,128)(2,1)} %param.12) | copy-start | bytes 1769476
  94.0 9.1 %collective-permute-start.12 = (bf16[144,2048]{1,0:T(8,128)(2,1)}, bf16[144,2048]{1,0:T(8,128)(2,1)}, u32[]{:S(2)}, u32[]{:S(2)}) collective-permute-start(bf16[144,2048]{1,0:T(8,128)(2,1)} %add_convert_fusion.2), channel_id=1, source_target_pairs={{0,8},{5,13},{10,2},{15,7},{16,24},{21,29},{26,18},{31,23}} | collective-permute-start | bytes 1769480 | tf_op jit(solution)/shard_map/ppermute | solution.py:131
  100.3 9.1 %collective-permute-start.16 = (bf16[144,2048]{1,0:T(8,128)(2,1)}, bf16[144,2048]{1,0:T(8,128)(2,1)}, u32[]{:S(2)}, u32[]{:S(2)}) collective-permute-start(bf16[144,2048]{1,0:T(8,128)(2,1)} %add_convert_fusion.1), channel_id=1, source_target_pairs={{0,4},{5,9},{10,14},{15,3},{16,20},{21,25},{26,30},{31,19}} | collective-permute-start | bytes 1769480 | tf_op jit(solution)/shard_map/ppermute | solution.py:131
  111.5 19.5 %copy-start.1 = (bf16[144,2048]{1,0:T(8,128)(2,1)}, bf16[144,2048]{1,0:T(8,128)(2,1)S(1)}, u32[]{:S(2)}) copy-start(bf16[144,2048]{1,0:T(8,128)(2,1)S(1)} %add_convert_fusion) | copy-start | bytes 1769476
  111.9 1.2 collective-permute-start.17
  113.1 6.7 %collective-permute-start.18 = (f32[2,16]{1,0:T(2,128)S(1)}, f32[2,16]{1,0:T(2,128)S(1)}, u32[]{:S(2)}, u32[]{:S(2)}) collective-permute-start(f32[2,16]{1,0:T(2,128)S(1)} %fusion.9), channel_id=1, source_target_pairs={{0,2},{1,3},{2,0},{3,1},{4,6},{5,7},{6,4},{7,5},{8,10},{9,11},{10,... | collective-permute-start | bytes 392 | tf_op jit(solution)/shard_map/ppermute | solution.py:71
  119.8 5.5 %collective-permute-start.19 = (f32[2,16]{1,0:T(2,128)S(1)}, f32[2,16]{1,0:T(2,128)S(1)}, u32[]{:S(2)}, u32[]{:S(2)}) collective-permute-start(f32[2,16]{1,0:T(2,128)S(1)} %fusion.25), channel_id=1, source_target_pairs={{0,4},{1,5},{2,6},{3,7},{4,0},{5,1},{6,2},{7,3},{8,12},{9,13},{10,... | collective-permute-start | bytes 392 | tf_op jit(solution)/shard_map/ppermute | solution.py:71
  125.3 5.2 %collective-permute-start.20 = (f32[2,16]{1,0:T(2,128)S(1)}, f32[2,16]{1,0:T(2,128)S(1)}, u32[]{:S(2)}, u32[]{:S(2)}) collective-permute-start(f32[2,16]{1,0:T(2,128)S(1)} %add.170), channel_id=1, source_target_pairs={{0,8},{1,9},{2,10},{3,11},{4,12},{5,13},{6,14},{7,15},{8,0},{9,1},... | collective-permute-start | bytes 392 | tf_op jit(solution)/shard_map/ppermute | solution.py:71

commit v2 on v1

v2 whole, which is shorter than its diff:
```python
import functools
import math

import jax
import jax.numpy as jnp
from jax import lax
from jax.experimental import pallas as pl
from jax.experimental.pallas import tpu as pltpu
from jax.sharding import PartitionSpec as P

HEAD_SIZE = 128
TURNS = 16
MASKED = -1e30


def row_tokens(index, n_ctx, tok_rows):
    half = tok_rows // 2
    row = jnp.arange(tok_rows, dtype=jnp.int32)
    return jnp.where(row < half, index * half + row, (2 * n_ctx - 2 - index) * half + row)


def attention(q_ref, kv_ref, token_ref, span_ref, out_ref):
    kv_heads = kv_ref.shape[1] // (2 * HEAD_SIZE)
    group = q_ref.shape[1] // (kv_heads * HEAD_SIZE)
    scale = math.log2(math.e) / math.sqrt(HEAD_SIZE)
    token = token_ref[...]
    allowed = (token >= span_ref[:, 0:1]) & (token <= span_ref[:, 1:2])
    bias = jnp.where(allowed, 0.0, MASKED)
    for g in range(kv_heads):
        key = kv_ref[:, g * HEAD_SIZE : (g + 1) * HEAD_SIZE]
        value = kv_ref[:, (kv_heads + g) * HEAD_SIZE : (kv_heads + g + 1) * HEAD_SIZE]
        value = jnp.concatenate([value, jnp.ones_like(value)], axis=1)
        for h in range(g * group, (g + 1) * group):
            cols = slice(h * HEAD_SIZE, (h + 1) * HEAD_SIZE)
            scores = lax.dot_general(
                q_ref[:, cols], key, (((1,), (1,)), ((), ())), preferred_element_type=jnp.float32
            )
            scores = scores + bias
            weights = jnp.exp2((scores - jnp.max(scores, axis=1, keepdims=True)) * scale)
            sums = jnp.dot(weights.astype(jnp.bfloat16), value, preferred_element_type=jnp.float32)
            out_ref[:, cols] = (sums[:, :HEAD_SIZE] / sums[:, HEAD_SIZE:]).astype(jnp.bfloat16)


VMEM = pl.BlockSpec(memory_space=pltpu.VMEM)


def attend(queries, kv, tokens, span):
    rows, keys = queries.shape[0], kv.shape[0]
    return pl.pallas_call(
        attention,
        out_shape=jax.ShapeDtypeStruct(queries.shape, jnp.bfloat16),
        in_specs=[VMEM] * 4,
        out_specs=VMEM,
        compiler_params=pltpu.CompilerParams(
            vmem_limit_bytes=2**22 + 4 * (2 * queries.size + kv.size) + 32 * rows * keys
        ),
        name="attention",
    )(queries, kv, tokens, span)


def pack_kernel(key_ref, value_ref, line_ref, out_ref):
    rows, cols = key_ref.shape
    width = out_ref.shape[1]
    out_ref[:rows, :cols] = key_ref[...]
    out_ref[:rows, cols:] = value_ref[...]
    extra = out_ref.shape[0] - rows
    at = lax.broadcasted_iota(jnp.int32, (extra, width), 0)
    lines = jnp.zeros((extra, width), jnp.float32)
    for r in range(line_ref.shape[0]):
        lines = jnp.where(at == r, line_ref[r : r + 1, :].astype(jnp.float32), lines)
    out_ref[rows:, :] = lines.astype(out_ref.dtype)


def pack(keys, values, lines):
    rows, width = keys.shape[0], keys.shape[1] + values.shape[1]
    extra = lines.shape[0]
    return pl.pallas_call(
        pack_kernel,
        out_shape=jax.ShapeDtypeStruct((rows + extra + -extra % 16, width), keys.dtype),
        in_specs=[VMEM] * 3,
        out_specs=VMEM,
        name="pack",
    )(keys, values, lines)


def shards(
    n_ctx,
    n_tp,
    queries,
    keys,
    values,
    residual,
    out_weight,
    value_head,
    segment_ids,
    positions,
    turn_ids,
):
    tok_rows = queries.shape[0]
    ctx = lax.axis_index("ctx")

    def ring(x, step):
        return lax.ppermute(x, "ctx", [(i, (i + step) % n_ctx) for i in range(n_ctx)])

    width = keys.shape[1] + values.shape[1]
    per_number = -(-tok_rows // width)
    packed = pack(keys, values, jnp.pad(turn_ids, (0, per_number * width - tok_rows)).reshape(-1, width))
    with jax.named_scope("kv"):
        packed = [packed] + [ring(packed, s) for s in range(1, n_ctx)]
    kv = jnp.concatenate([block[:tok_rows] for block in packed], axis=0)
    key_tokens = jnp.concatenate(
        [row_tokens((ctx - s) % n_ctx, n_ctx, tok_rows) for s in range(n_ctx)]
    )
    tokens = row_tokens(ctx, n_ctx, tok_rows)
    span = jnp.stack([tokens - positions, tokens], axis=1)
    piece = attend(queries, kv, key_tokens[None, :], span)
    both = ("ctx", "tp")
    wide = jnp.float32

    def one_hot(turns):
        return (jnp.arange(TURNS, dtype=turns.dtype)[:, None] == turns[None, :]).astype(jnp.bfloat16)

    if n_ctx != n_tp or n_tp != 4:
        partial_value = jnp.dot(
            lax.all_gather(piece, "ctx", axis=0, tiled=True), out_weight, preferred_element_type=wide
        )
        term_rows = lax.all_to_all(
            partial_value.astype(jnp.bfloat16), "ctx", split_axis=0, concat_axis=1, tiled=True
        )
        summed = lax.psum_scatter(term_rows, "tp", scatter_dimension=1, tiled=True)
        hidden_out = (residual.astype(wide) + summed.astype(wide)).astype(jnp.bfloat16)
        token_score = jnp.dot(hidden_out, value_head, preferred_element_type=wide)
        sums = jnp.sum(one_hot(turn_ids).astype(wide) * token_score[None, :], axis=1)
        counts = jnp.sum(one_hot(turn_ids).astype(wide), axis=1)
        counts = jnp.where(lax.axis_index("tp") == 0, counts, 0.0)
        totals = lax.psum(jnp.stack([sums, counts]), both)
        return (hidden_out, totals[0] / jnp.maximum(totals[1], 1.0))

    ctx_tp = [(c, t) for c in range(n_ctx) for t in range(n_tp)]

    def send(name, x, route):
        pairs = []
        for c, t in ctx_tp:
            target = route(c, t)
            if target is not None:
                pairs.append((c * n_tp + t, target[0] % n_ctx * n_tp + target[1]))
        with jax.named_scope(name):
            return lax.ppermute(x, both, pairs)

    def add(*terms):
        return sum(term.astype(wide) for term in terms).astype(jnp.bfloat16)

    def sibling(name, x):
        return send(name, x, lambda c, t: (c, t ^ 1))

    def across(name, x, bit):
        return send(
            name, x, lambda c, t: (c, t ^ bit) if (t ^ c) & bit and not (t ^ c) & (bit - 2) else None
        )

    def to_rows(name, x, step, differ):
        return send(
            name, x, lambda c, t: (c - step, c & -2 | t & 1) if (t ^ c) & -2 == differ else None
        )

    barrier = lax.optimization_barrier
    top = n_tp // 2
    columns = out_weight.shape[1] // 2
    tp = lax.axis_index("tp")
    second = tp % 2 == 1

    head_block = send("head", value_head, lambda c, t: (t, c))
    token_score = jnp.dot(residual, value_head, preferred_element_type=wide)
    sums = jnp.sum(one_hot(turn_ids).astype(wide) * token_score[None, :], axis=1)
    turns = [block[tok_rows : tok_rows + per_number].reshape(-1)[:tok_rows] for block in packed]
    hots = [one_hot(block) for block in turns]
    counts = sum(jnp.sum(hot.astype(wide), axis=1) for hot in hots)
    through = jnp.zeros((TURNS, out_weight.shape[1]), wide)

    def project(piece):
        part = jnp.dot(piece, out_weight, preferred_element_type=wide).astype(jnp.bfloat16)
        low, high = part[:, :columns], part[:, columns:]
        return part, jnp.where(second, high, low), jnp.where(second, low, high)

    def per_turn(s, part):
        return jnp.dot(hots[s], part, preferred_element_type=wide)

    def core_sum(keep, give, pieces):
        cut = columns // pieces
        return add(
            keep,
            jnp.concatenate(
                [sibling("core", give[:, i * cut : (i + 1) * cut]) for i in range(pieces)], axis=1
            ),
        )

    def ring_on(piece):
        with jax.named_scope("heads"):
            return ring(piece, 1)

    following = ring_on(piece)
    part, keep, give = project(piece)
    through = through + per_turn(0, part)
    piece, keep, give, through = barrier((following, keep, give, through))

    following = ring_on(piece)
    first = core_sum(keep, give, 1)
    crossed = across("x", first, top)
    piece, first = barrier((piece, first))
    part, keep, give = project(piece)
    through = through + per_turn(1, part)
    piece, keep, give, crossed, through = barrier((following, keep, give, crossed, through))

    following = ring_on(piece)
    chip = core_sum(keep, give, 1)
    even = jnp.where((tp ^ ctx) & -2 == 0, add(first, crossed), 0.0)
    crossed = across("x", chip, top)
    piece, chip, even = barrier((piece, chip, even))
    part, keep, give = project(piece)
    through = through + per_turn(2, part)
    piece, keep, give, crossed, through = barrier((following, keep, give, crossed, through))

    odd = to_rows("rows1", add(chip, crossed), 1, 0)
    chip = core_sum(keep, give, 1)
    back = [to_rows("rows2", chip, 2, differ) for differ in (0, top)]
    piece, chip = barrier((piece, chip))
    part = jnp.dot(piece, out_weight, preferred_element_type=wide).astype(jnp.bfloat16)
    arrived = send("core", part, lambda c, t: (c, t ^ 1) if (t ^ c) & 1 else None)
    through = through + per_turn(3, part)
    sums = sums + jnp.sum(through * head_block.astype(wide)[None, :], axis=1)
    bit = 1
    while bit < n_tp:
        with jax.named_scope("turns_tp"):
            sums = sums + lax.ppermute(sums, "tp", [(t, t ^ bit) for t in range(n_tp)])
        bit *= 2
    chip = add(part, arrived)
    last = [
        send("rows3", chip, lambda c, t: (c + 1, c) if t ^ c == differ else None)
        for differ in (0, top)
    ]
    even = add(even, *back)
    mine = (tp ^ ctx) & 1 == 0
    other = sibling("swap", jnp.where(mine, odd, even))
    same = jnp.where(mine, even, odd)
    sums, chip = barrier((sums, chip))
    with jax.named_scope("turns_ctx"):
        sums = sum([ring(sums, step) for step in range(1, n_ctx)], sums)
    low, high = jnp.where(second, other, same), jnp.where(second, same, other)
    hidden_out = add(residual, jnp.concatenate([low, high], axis=1), *last)
    return (hidden_out, sums / jnp.maximum(counts, 1.0))


def solution(mesh):
    return jax.shard_map(
        functools.partial(shards, mesh.shape["ctx"], mesh.shape["tp"]),
        mesh=mesh,
        in_specs=(
            P(("groups", "ctx"), "tp"),
            P(("groups", "ctx"), "tp"),
            P(("groups", "ctx"), "tp"),
            P(("groups", "ctx"), "tp"),
            P("tp", "ctx"),
            P("tp"),
            P(("groups", "ctx")),
            P(("groups", "ctx")),
            P(("groups", "ctx")),
        ),
        out_specs=(P(("groups", "ctx"), "tp"), P("groups")),
        check_vma=False,
    )
```

time: 131 us -> 116 us (0.89)
  the two profiles are of different devices: /device:TPU:0 before, /device:TPU:1 now
where the time goes in v2:
time: 116 us; the launch traced here: 115 us
  waiting for transfers between devices  43.5 us (38%)
  starting transfers between devices  42.9 us (37%)
  matrix products  15.3 us (13%)
  other arithmetic  4.34 us (4%)
  Pallas kernels  4.16 us (4%)
  local copies, waits for them, and re-layouts  3.96 us (3%)
  between operations  1.2 us (1%)
    ppermute x9, waiting for transfers between devices, ring(): lax.ppermute(x, 'ctx', [(i, (i + step) % n_ctx) for i in range(n_ctx)])  33.3 us
    ppermute x13, starting transfers between devices, send(): return lax.ppermute(x, both, pairs)  25.7 us
    ppermute x9, starting transfers between devices, ring(): lax.ppermute(x, 'ctx', [(i, (i + step) % n_ctx) for i in range(n_ctx)])  17.2 us
    dot_general x3, matrix products, project(): jnp.dot(piece, out_weight, preferred_element_type=wide).astype(jnp.bfloat16)  11.8 us
    ppermute x13, waiting for transfers between devices, send(): return lax.ppermute(x, both, pairs)  9.13 us
    pallas_call x1, Pallas kernels, attend(): pl.pallas_call(attention, out_shape=jax.ShapeDtypeStruct(queries.shape, j...  2.55 us
  transfers between devices with their start and end apart: 24, of which 12 were waited for; matrix products, arithmetic and copies ran while one was open for 18% of the time, Pallas kernels for 2%

profile of v2, /device:TPU:1, one launch (start us, length us, event | category | flops | bytes accessed | tf_op | source)
XLA Modules:
  0.0 115.3 jit_solution(10698992783889755264)
XLA Ops:
  0.6 1.3 %pad.4 = s32[512]{0:T(512)} pad(s32[144]{0:T(256)} %param.16, s32[]{:T(128)} %constant.49.clone.1), padding=0_368 | pad | bytes 2628 | tf_op jit(solution)/shard_map/jit(_pad)/pad | solution.py:107
  2.0 1.6 %pack.1 = bf16[160,512]{1,0:T(8,128)(2,1)} custom-call(bf16[144,256]{1,0:T(8,128)(2,1)} %key_ref.1, bf16[144,256]{1,0:T(8,128)(2,1)} %value_ref.1, s32[1,512]{1,0:T(1,128)} %bitcast.19), custom_call_target="tpu_custom_call" | custom-call | tf_op jit(solution)/shard_map/pack/pallas_call | solution.py:77
  3.6 4.2 %collective-permute-start.2 = (bf16[160,512]{1,0:T(8,128)(2,1)}, bf16[160,512]{1,0:T(8,128)(2,1)S(1)}, u32[]{:S(2)}, u32[]{:S(2)}) collective-permute-start(bf16[160,512]{1,0:T(8,128)(2,1)} %pack.1), channel_id=1, source_target_pairs={{0,12},{4,0},{8,4},{12,8},{1,13},{5,1},{9,5},{13,9},{2,14},{6,2},{... | collective-permute-start | bytes 491528 | tf_op jit(solution)/shard_map/kv/ppermute | solution.py:103
  7.7 0.5 collective-permute-start
  8.2 5.5 %collective-permute-start.18 = (bf16[2048]{0:T(1024)(128)(2,1)}, bf16[2048]{0:T(1024)(128)(2,1)S(1)}, u32[]{:S(2)}, u32[]{:S(2)}) collective-permute-start(bf16[2048]{0:T(1024)(128)(2,1)} %param.14), channel_id=1, source_target_pairs={{0,0},{1,4},{2,8},{3,12},{4,1},{5,5},{6,9},{7,13},{8,2},{9,6},{10,... | collective-permute-start | bytes 12296 | tf_op jit(solution)/shard_map/head/ppermute | solution.py:148
  13.8 0.7 reshape.46
  14.5 0.7 slice_reduce_fusion.3
  15.2 0.7 select_subtract_fusion
  15.9 1.3 %fusion.10 = f32[1,144]{1,0:T(1,128)S(1)} fusion(bf16[144,2048]{1,0:T(8,128)(2,1)} %param.12, bf16[2048,1]{0,1:T(2,128)(2,1)S(1)} %reshape.46), kind=kOutput, calls=%fused_computation.58 | convolution fusion | flops 589824 | bytes 594496 | tf_op jit(solution)/shard_map/dot_general | solution.py:173
  17.3 1.0 slice.68
  18.6 3.3 %collective-permute-done.1 = bf16[160,512]{1,0:T(8,128)(2,1)S(1)} collective-permute-done((bf16[160,512]{1,0:T(8,128)(2,1)}, bf16[160,512]{1,0:T(8,128)(2,1)S(1)}, u32[]{:S(2)}, u32[]{:S(2)}) %collective-permute-start.1) | collective-permute-done | bytes 163872 | tf_op jit(solution)/shard_map/kv/ppermute | solution.py:103
  22.0 2.6 %attention.1 = bf16[144,2048]{1,0:T(8,128)(2,1)S(1)} custom-call(bf16[144,2048]{1,0:T(8,128)(2,1)S(1)} %copy-done, bf16[576,512]{1,0:T(8,128)(2,1)S(1)} %pad_maximum_fusion.kv_ref, s32[1,576]{1,0:T(1,128)S(1)} %broadcast_in_dim.5.token_ref, s32[144,2]{1,0:T(8,128)S(1)} %copy.12.span_ref), custom_call_target="tpu_custom_call" | custom-call | tf_op jit(solution)/shard_map/attention/pallas_call | solution.py:49
  24.6 0.3 collective-permute-start.3
  24.9 4.8 %convolution_convert_fusion.3 = bf16[144,2048]{1,0:T(8,128)(2,1)S(1)} fusion(bf16[144,2048]{1,0:T(8,128)(2,1)S(1)} %attention.1, bf16[2048,2048]{1,0:T(8,128)(2,1)} %param.13), kind=kOutput, calls=%fused_computation.3 | convolution fusion | flops 1208254464 | bytes 9568256 | tf_op jit(solution)/shard_map/dot_general | solution.py:181
  29.7 0.2 fusion.5
  29.9 10.3 %collective-permute-done.3 = bf16[144,2048]{1,0:T(8,128)(2,1)S(1)} collective-permute-done((bf16[144,2048]{1,0:T(8,128)(2,1)S(1)}, bf16[144,2048]{1,0:T(8,128)(2,1)S(1)}, u32[]{:S(2)}, u32[]{:S(2)}) %collective-permute-start.3) | collective-permute-done | bytes 589856 | tf_op jit(solution)/shard_map/heads/ppermute | solution.py:103
  40.3 1.9 %collective-permute-start.5 = (bf16[144,1024]{1,0:T(8,128)(2,1)S(1)}, bf16[144,1024]{1,0:T(8,128)(2,1)S(1)}, u32[]{:S(2)}, u32[]{:S(2)}) collective-permute-start(bf16[144,1024]{1,0:T(8,128)(2,1)S(1)} %get-tuple-element.25), channel_id=1, source_target_pairs={{0,1},{1,0},{2,3},{3,2},{4,5},{5,4},{6,7},{7,6},{8,9},{9,8},{10,11... | collective-permute-start | bytes 884744 | tf_op jit(solution)/shard_map/core/ppermute | solution.py:148
  42.4 1.0 collective-permute-done.5
  43.5 1.6 %collective-permute-start.6 = (bf16[144,1024]{1,0:T(8,128)(2,1)S(1)}, bf16[144,1024]{1,0:T(8,128)(2,1)S(1)}, u32[]{:S(2)}, u32[]{:S(2)}) collective-permute-start(bf16[144,1024]{1,0:T(8,128)(2,1)S(1)} %add_convert_fusion.7), channel_id=1, source_target_pairs={{2,0},{3,1},{6,4},{7,5},{8,10},{9,11},{12,14},{13,15},{18,16},{19,... | collective-permute-start | bytes 884744 | tf_op jit(solution)/shard_map/x/ppermute | solution.py:148
  45.1 5.5 %convolution_convert_fusion.2 = bf16[144,2048]{1,0:T(8,128)(2,1)S(1)} fusion(bf16[144,2048]{1,0:T(8,128)(2,1)S(1)} %collective-permute-done.3, bf16[2048,2048]{1,0:T(8,128)(2,1)} %param.13), kind=kOutput, calls=%fused_computation.2 | convolution fusion | flops 1208254464 | bytes 9568256 | tf_op jit(solution)/shard_map/dot_general | solution.py:181
  50.6 0.2 fusion.4
  50.9 8.3 %collective-permute-done.4 = bf16[144,2048]{1,0:T(8,128)(2,1)S(1)} collective-permute-done((bf16[144,2048]{1,0:T(8,128)(2,1)S(1)}, bf16[144,2048]{1,0:T(8,128)(2,1)S(1)}, u32[]{:S(2)}, u32[]{:S(2)}) %collective-permute-start.4) | collective-permute-done | bytes 589856 | tf_op jit(solution)/shard_map/heads/ppermute | solution.py:103
  59.2 0.8 collective-permute-start.7
  60.2 1.0 collective-permute-done.7
  61.3 1.3 %collective-permute-start.9 = (bf16[144,1024]{1,0:T(8,128)(2,1)S(1)}, bf16[144,1024]{1,0:T(8,128)(2,1)S(1)}, u32[]{:S(2)}, u32[]{:S(2)}) collective-permute-start(bf16[144,1024]{1,0:T(8,128)(2,1)S(1)} %add_convert_fusion.6), channel_id=1, source_target_pairs={{2,0},{3,1},{6,4},{7,5},{8,10},{9,11},{12,14},{13,15},{18,16},{19,... | collective-permute-start | bytes 884744 | tf_op jit(solution)/shard_map/x/ppermute | solution.py:148
  62.6 1.4 %convolution_convert_fusion.1 = bf16[144,2048]{1,0:T(8,128)(2,1)S(1)} fusion(bf16[144,2048]{1,0:T(8,128)(2,1)S(1)} %collective-permute-done.4, bf16[2048,2048]{1,0:T(8,128)(2,1)S(1)} %bitcast.18), kind=kOutput, calls=%fused_computation.1 | convolution fusion | flops 1208254464 | bytes 9568256 | tf_op jit(solution)/shard_map/dot_general | solution.py:181
  64.0 0.2 fusion.3
  64.3 7.1 %collective-permute-done.9 = bf16[144,1024]{1,0:T(8,128)(2,1)S(1)} collective-permute-done((bf16[144,1024]{1,0:T(8,128)(2,1)S(1)}, bf16[144,1024]{1,0:T(8,128)(2,1)S(1)}, u32[]{:S(2)}, u32[]{:S(2)}) %collective-permute-start.9) | collective-permute-done | bytes 294944 | tf_op jit(solution)/shard_map/x/ppermute | solution.py:148
  71.4 5.4 %collective-permute-done.8 = bf16[144,2048]{1,0:T(8,128)(2,1)S(1)} collective-permute-done((bf16[144,2048]{1,0:T(8,128)(2,1)S(1)}, bf16[144,2048]{1,0:T(8,128)(2,1)S(1)}, u32[]{:S(2)}, u32[]{:S(2)}) %collective-permute-start.8) | collective-permute-done | bytes 589856 | tf_op jit(solution)/shard_map/heads/ppermute | solution.py:103
  76.8 0.8 collective-permute-start.11
  77.8 1.9 %collective-permute-start.10 = (bf16[144,1024]{1,0:T(8,128)(2,1)S(1)}, bf16[144,1024]{1,0:T(8,128)(2,1)S(1)}, u32[]{:S(2)}, u32[]{:S(2)}) collective-permute-start(bf16[144,1024]{1,0:T(8,128)(2,1)S(1)} %add_convert_fusion.4), channel_id=1, source_target_pairs={{0,12},{1,13},{4,0},{5,1},{10,6},{11,7},{14,10},{15,11},{16,28},{1... | collective-permute-start | bytes 884744 | tf_op jit(solution)/shard_map/rows1/ppermute | solution.py:148
  79.8 0.7 collective-permute-start.13
  80.5 5.4 %collective-permute-start.12 = (bf16[144,1024]{1,0:T(8,128)(2,1)S(1)}, bf16[144,1024]{1,0:T(8,128)(2,1)S(1)}, u32[]{:S(2)}, u32[]{:S(2)}) collective-permute-start(bf16[144,1024]{1,0:T(8,128)(2,1)S(1)} %add_convert_fusion.3), channel_id=1, source_target_pairs={{0,8},{1,9},{4,12},{5,13},{10,2},{11,3},{14,6},{15,7},{16,24},{17,... | collective-permute-start | bytes 884744 | tf_op jit(solution)/shard_map/rows2/ppermute | solution.py:148
  85.9 1.4 %convolution_convert_fusion = bf16[144,2048]{1,0:T(8,128)(2,1)S(1)} fusion(bf16[144,2048]{1,0:T(8,128)(2,1)S(1)} %collective-permute-done.8, bf16[2048,2048]{1,0:T(8,128)(2,1)S(1)} %bitcast.18), kind=kOutput, calls=%fused_computation | convolution fusion | flops 1208254464 | bytes 9568256 | tf_op jit(solution)/shard_map/dot_general | solution.py:227
  87.4 2.9 %collective-permute-start.15 = (bf16[144,2048]{1,0:T(8,128)(2,1)S(1)}, bf16[144,2048]{1,0:T(8,128)(2,1)S(1)}, u32[]{:S(2)}, u32[]{:S(2)}) collective-permute-start(bf16[144,2048]{1,0:T(8,128)(2,1)S(1)} %convolution_convert_fusion), channel_id=1, source_target_pairs={{1,0},{3,2},{4,5},{6,7},{9,8},{11,10},{12,13},{14,15},{17,16},{19,... | collective-permute-start | bytes 1769480 | tf_op jit(solution)/shard_map/core/ppermute | solution.py:148
  90.3 0.2 fusion.2
  90.8 1.0 collective-permute-done.19
  91.9 0.2 broadcast_select_fusion.1
  92.1 1.4 %collective-permute-start.14 = (bf16[144,1024]{1,0:T(8,128)(2,1)S(1)}, bf16[144,1024]{1,0:T(8,128)(2,1)S(1)}, u32[]{:S(2)}, u32[]{:S(2)}) collective-permute-start(bf16[144,1024]{1,0:T(8,128)(2,1)S(1)} %get-tuple-element.44), channel_id=1, source_target_pairs={{0,1},{1,0},{2,3},{3,2},{4,5},{5,4},{6,7},{7,6},{8,9},{9,8},{10,11... | collective-permute-start | bytes 884744 | tf_op jit(solution)/shard_map/swap/ppermute | solution.py:148
  93.7 0.8 collective-permute-start.17
  94.6 0.7 collective-permute-start.16
  95.5 11.8 %collective-permute-start.23 = (f32[16]{0:T(128)S(1)}, f32[16]{0:T(128)S(1)}, u32[]{:S(2)}, u32[]{:S(2)}) collective-permute-start(f32[16]{0:T(128)S(1)} %add.217), channel_id=1, source_target_pairs={{0,12},{4,0},{8,4},{12,8},{1,13},{5,1},{9,5},{13,9},{2,14},{6,2},{... | collective-permute-start | bytes 200 | tf_op jit(solution)/shard_map/turns_ctx/ppermute | solution.py:103
  107.3 0.4 collective-permute-start.21
  107.6 0.4 collective-permute-done.23
  108.0 2.6 %collective-permute-done.22 = f32[16]{0:T(128)S(1)} collective-permute-done((f32[16]{0:T(128)S(1)}, f32[16]{0:T(128)S(1)}, u32[]{:S(2)}, u32[]{:S(2)}) %collective-permute-start.22) | collective-permute-done | bytes 96 | tf_op jit(solution)/shard_map/turns_ctx/ppermute | solution.py:103
  110.6 3.0 %collective-permute-done.21 = f32[16]{0:T(128)S(1)} collective-permute-done((f32[16]{0:T(128)S(1)}, f32[16]{0:T(128)S(1)}, u32[]{:S(2)}, u32[]{:S(2)}) %collective-permute-start.21) | collective-permute-done | bytes 96 | tf_op jit(solution)/shard_map/turns_ctx/ppermute | solution.py:103
  113.5 0.5 maximum_divide_fusion
  114.1 1.2 %add_convert_fusion = bf16[144,2048]{1,0:T(8,128)(2,1)} fusion(bf16[144,2048]{1,0:T(8,128)(2,1)S(1)} %collective-permute-done.17, bf16[144,2048]{1,0:T(8,128)(2,1)S(1)} %collective-permute-done.16, bf16[144,2048]{1,0:T(8,128)(2,1)S(1)} %copy-done.1, bf16[144,1024]{1,0:T(8,128)(2,1)S(1)} %get-tuple-element.47, bf16[144,1024]{1,0:T(8,128)(2,1)S(1)} %get-tuple-element.46), kind=kLoop, calls=%fused_computation.4 | loop fusion | flops 3244032 | bytes 2949120 | tf_op jit(solution)/shard_map/convert_element_type | solution.py:151
  (66 shorter events, 2.2 us)
Async XLA Ops:
  0.6 17.8 %copy-start.2 = (s32[144]{0:T(256)S(1)}, s32[144]{0:T(256)}, u32[]{:S(2)}) copy-start(s32[144]{0:T(256)} %param.16) | copy-start | bytes 1732
  3.6 15.0 %collective-permute-start.2 = (bf16[160,512]{1,0:T(8,128)(2,1)}, bf16[160,512]{1,0:T(8,128)(2,1)S(1)}, u32[]{:S(2)}, u32[]{:S(2)}) collective-permute-start(bf16[160,512]{1,0:T(8,128)(2,1)} %pack.1), channel_id=1, source_target_pairs={{0,12},{4,0},{8,4},{12,8},{1,13},{5,1},{9,5},{13,9},{2,14},{6,2},{... | collective-permute-start | bytes 491528 | tf_op jit(solution)/shard_map/kv/ppermute | solution.py:103
  7.7 14.2 %collective-permute-start.1 = (bf16[160,512]{1,0:T(8,128)(2,1)}, bf16[160,512]{1,0:T(8,128)(2,1)S(1)}, u32[]{:S(2)}, u32[]{:S(2)}) collective-permute-start(bf16[160,512]{1,0:T(8,128)(2,1)} %pack.1), channel_id=1, source_target_pairs={{0,8},{4,12},{8,0},{12,4},{1,9},{5,13},{9,1},{13,5},{2,10},{6,14},... | collective-permute-start | bytes 491528 | tf_op jit(solution)/shard_map/kv/ppermute | solution.py:103
  7.7 14.2 %collective-permute-start = (bf16[160,512]{1,0:T(8,128)(2,1)}, bf16[160,512]{1,0:T(8,128)(2,1)S(1)}, u32[]{:S(2)}, u32[]{:S(2)}) collective-permute-start(bf16[160,512]{1,0:T(8,128)(2,1)} %pack.1), channel_id=1, source_target_pairs={{0,4},{4,8},{8,12},{12,0},{1,5},{5,9},{9,13},{13,1},{2,6},{6,10},{... | collective-permute-start | bytes 491528 | tf_op jit(solution)/shard_map/kv/ppermute | solution.py:103
  8.2 34.1 %collective-permute-start.18 = (bf16[2048]{0:T(1024)(128)(2,1)}, bf16[2048]{0:T(1024)(128)(2,1)S(1)}, u32[]{:S(2)}, u32[]{:S(2)}) collective-permute-start(bf16[2048]{0:T(1024)(128)(2,1)} %param.14), channel_id=1, source_target_pairs={{0,0},{1,4},{2,8},{3,12},{4,1},{5,5},{6,9},{7,13},{8,2},{9,6},{10,... | collective-permute-start | bytes 12296 | tf_op jit(solution)/shard_map/head/ppermute | solution.py:148
  17.3 4.7 %copy-start = (bf16[144,2048]{1,0:T(8,128)(2,1)S(1)}, bf16[144,2048]{1,0:T(8,128)(2,1)}, u32[]{:S(2)}) copy-start(bf16[144,2048]{1,0:T(8,128)(2,1)} %q_ref.1) | copy-start | bytes 1769476
  24.6 15.7 %collective-permute-start.3 = (bf16[144,2048]{1,0:T(8,128)(2,1)S(1)}, bf16[144,2048]{1,0:T(8,128)(2,1)S(1)}, u32[]{:S(2)}, u32[]{:S(2)}) collective-permute-start(bf16[144,2048]{1,0:T(8,128)(2,1)S(1)} %attention.1), channel_id=1, source_target_pairs={{0,4},{4,8},{8,12},{12,0},{1,5},{5,9},{9,13},{13,1},{2,6},{6,10},{... | collective-permute-start | bytes 1769480 | tf_op jit(solution)/shard_map/heads/ppermute | solution.py:103
  40.3 3.1 %collective-permute-start.5 = (bf16[144,1024]{1,0:T(8,128)(2,1)S(1)}, bf16[144,1024]{1,0:T(8,128)(2,1)S(1)}, u32[]{:S(2)}, u32[]{:S(2)}) collective-permute-start(bf16[144,1024]{1,0:T(8,128)(2,1)S(1)} %get-tuple-element.25), channel_id=1, source_target_pairs={{0,1},{1,0},{2,3},{3,2},{4,5},{5,4},{6,7},{7,6},{8,9},{9,8},{10,11... | collective-permute-start | bytes 884744 | tf_op jit(solution)/shard_map/core/ppermute | solution.py:148
  42.4 16.8 %collective-permute-start.4 = (bf16[144,2048]{1,0:T(8,128)(2,1)S(1)}, bf16[144,2048]{1,0:T(8,128)(2,1)S(1)}, u32[]{:S(2)}, u32[]{:S(2)}) collective-permute-start(bf16[144,2048]{1,0:T(8,128)(2,1)S(1)} %collective-permute-done.3), channel_id=1, source_target_pairs={{0,4},{4,8},{8,12},{12,0},{1,5},{5,9},{9,13},{13,1},{2,6},{6,10},{... | collective-permute-start | bytes 1769480 | tf_op jit(solution)/shard_map/heads/ppermute | solution.py:103
  43.4 19.2 %slice-start = ((s8[8388608]{0:T(1024)(128)(4,1)}), s8[4194304]{0:T(1024)(128)(4,1)S(1)}, s32[]{:S(2)}) async-start(s8[8388608]{0:T(1024)(128)(4,1)} %bitcast.17), calls=%async_computation | async-start | bytes 8388608
  43.5 19.1 %slice-start.1 = ((s8[8388608]{0:T(1024)(128)(4,1)}), s8[4194304]{0:T(1024)(128)(4,1)S(1)}, s32[]{:S(2)}) async-start(s8[8388608]{0:T(1024)(128)(4,1)} %bitcast.17), calls=%async_computation.1 | async-start | bytes 8388608
  43.5 15.7 %collective-permute-start.6 = (bf16[144,1024]{1,0:T(8,128)(2,1)S(1)}, bf16[144,1024]{1,0:T(8,128)(2,1)S(1)}, u32[]{:S(2)}, u32[]{:S(2)}) collective-permute-start(bf16[144,1024]{1,0:T(8,128)(2,1)S(1)} %add_convert_fusion.7), channel_id=1, source_target_pairs={{2,0},{3,1},{6,4},{7,5},{8,10},{9,11},{12,14},{13,15},{18,16},{19,... | collective-permute-start | bytes 884744 | tf_op jit(solution)/shard_map/x/ppermute | solution.py:148
  59.2 2.0 %collective-permute-start.7 = (bf16[144,1024]{1,0:T(8,128)(2,1)S(1)}, bf16[144,1024]{1,0:T(8,128)(2,1)S(1)}, u32[]{:S(2)}, u32[]{:S(2)}) collective-permute-start(bf16[144,1024]{1,0:T(8,128)(2,1)S(1)} %get-tuple-element.30), channel_id=1, source_target_pairs={{0,1},{1,0},{2,3},{3,2},{4,5},{5,4},{6,7},{7,6},{8,9},{9,8},{10,11... | collective-permute-start | bytes 884744 | tf_op jit(solution)/shard_map/core/ppermute | solution.py:148
  60.0 16.8 %collective-permute-start.8 = (bf16[144,2048]{1,0:T(8,128)(2,1)S(1)}, bf16[144,2048]{1,0:T(8,128)(2,1)S(1)}, u32[]{:S(2)}, u32[]{:S(2)}) collective-permute-start(bf16[144,2048]{1,0:T(8,128)(2,1)S(1)} %collective-permute-done.4), channel_id=1, source_target_pairs={{0,4},{4,8},{8,12},{12,0},{1,5},{5,9},{9,13},{13,1},{2,6},{6,10},{... | collective-permute-start | bytes 1769480 | tf_op jit(solution)/shard_map/heads/ppermute | solution.py:103
  61.3 10.1 %collective-permute-start.9 = (bf16[144,1024]{1,0:T(8,128)(2,1)S(1)}, bf16[144,1024]{1,0:T(8,128)(2,1)S(1)}, u32[]{:S(2)}, u32[]{:S(2)}) collective-permute-start(bf16[144,1024]{1,0:T(8,128)(2,1)S(1)} %add_convert_fusion.6), channel_id=1, source_target_pairs={{2,0},{3,1},{6,4},{7,5},{8,10},{9,11},{12,14},{13,15},{18,16},{19,... | collective-permute-start | bytes 884744 | tf_op jit(solution)/shard_map/x/ppermute | solution.py:148
  76.8 2.9 %collective-permute-start.11 = (bf16[144,1024]{1,0:T(8,128)(2,1)S(1)}, bf16[144,1024]{1,0:T(8,128)(2,1)S(1)}, u32[]{:S(2)}, u32[]{:S(2)}) collective-permute-start(bf16[144,1024]{1,0:T(8,128)(2,1)S(1)} %get-tuple-element.39), channel_id=1, source_target_pairs={{0,1},{1,0},{2,3},{3,2},{4,5},{5,4},{6,7},{7,6},{8,9},{9,8},{10,11... | collective-permute-start | bytes 884744 | tf_op jit(solution)/shard_map/core/ppermute | solution.py:148
  77.8 14.1 %collective-permute-start.10 = (bf16[144,1024]{1,0:T(8,128)(2,1)S(1)}, bf16[144,1024]{1,0:T(8,128)(2,1)S(1)}, u32[]{:S(2)}, u32[]{:S(2)}) collective-permute-start(bf16[144,1024]{1,0:T(8,128)(2,1)S(1)} %add_convert_fusion.4), channel_id=1, source_target_pairs={{0,12},{1,13},{4,0},{5,1},{10,6},{11,7},{14,10},{15,11},{16,28},{1... | collective-permute-start | bytes 884744 | tf_op jit(solution)/shard_map/rows1/ppermute | solution.py:148
  79.8 12.0 %collective-permute-start.13 = (bf16[144,1024]{1,0:T(8,128)(2,1)S(1)}, bf16[144,1024]{1,0:T(8,128)(2,1)S(1)}, u32[]{:S(2)}, u32[]{:S(2)}) collective-permute-start(bf16[144,1024]{1,0:T(8,128)(2,1)S(1)} %add_convert_fusion.3), channel_id=1, source_target_pairs={{2,8},{3,9},{6,12},{7,13},{8,2},{9,3},{12,6},{13,7},{18,24},{19,25... | collective-permute-start | bytes 884744 | tf_op jit(solution)/shard_map/rows2/ppermute | solution.py:148
  80.5 11.4 %collective-permute-start.12 = (bf16[144,1024]{1,0:T(8,128)(2,1)S(1)}, bf16[144,1024]{1,0:T(8,128)(2,1)S(1)}, u32[]{:S(2)}, u32[]{:S(2)}) collective-permute-start(bf16[144,1024]{1,0:T(8,128)(2,1)S(1)} %add_convert_fusion.3), channel_id=1, source_target_pairs={{0,8},{1,9},{4,12},{5,13},{10,2},{11,3},{14,6},{15,7},{16,24},{17,... | collective-permute-start | bytes 884744 | tf_op jit(solution)/shard_map/rows2/ppermute | solution.py:148
  87.4 6.2 %collective-permute-start.15 = (bf16[144,2048]{1,0:T(8,128)(2,1)S(1)}, bf16[144,2048]{1,0:T(8,128)(2,1)S(1)}, u32[]{:S(2)}, u32[]{:S(2)}) collective-permute-start(bf16[144,2048]{1,0:T(8,128)(2,1)S(1)} %convolution_convert_fusion), channel_id=1, source_target_pairs={{1,0},{3,2},{4,5},{6,7},{9,8},{11,10},{12,13},{14,15},{17,16},{19,... | collective-permute-start | bytes 1769480 | tf_op jit(solution)/shard_map/core/ppermute | solution.py:148
  90.6 1.2 %collective-permute-start.19 = (f32[16]{0:T(128)S(1)}, f32[16]{0:T(128)S(1)}, u32[]{:S(2)}, u32[]{:S(2)}) collective-permute-start(f32[16]{0:T(128)S(1)} %add.215), channel_id=1, source_target_pairs={{0,1},{1,0},{2,3},{3,2},{4,5},{5,4},{6,7},{7,6},{8,9},{9,8},{10,11... | collective-permute-start | bytes 200 | tf_op jit(solution)/shard_map/turns_tp/ppermute | solution.py:234
  91.8 3.6 %collective-permute-start.20 = (f32[16]{0:T(128)S(1)}, f32[16]{0:T(128)S(1)}, u32[]{:S(2)}, u32[]{:S(2)}) collective-permute-start(f32[16]{0:T(128)S(1)} %add.216), channel_id=1, source_target_pairs={{0,2},{1,3},{2,0},{3,1},{4,6},{5,7},{6,4},{7,5},{8,10},{9,11},{10,... | collective-permute-start | bytes 200 | tf_op jit(solution)/shard_map/turns_tp/ppermute | solution.py:234
  92.1 3.3 %collective-permute-start.14 = (bf16[144,1024]{1,0:T(8,128)(2,1)S(1)}, bf16[144,1024]{1,0:T(8,128)(2,1)S(1)}, u32[]{:S(2)}, u32[]{:S(2)}) collective-permute-start(bf16[144,1024]{1,0:T(8,128)(2,1)S(1)} %get-tuple-element.44), channel_id=1, source_target_pairs={{0,1},{1,0},{2,3},{3,2},{4,5},{5,4},{6,7},{7,6},{8,9},{9,8},{10,11... | collective-permute-start | bytes 884744 | tf_op jit(solution)/shard_map/swap/ppermute | solution.py:148
  93.7 20.3 %copy-start.1 = (bf16[144,2048]{1,0:T(8,128)(2,1)S(1)}, bf16[144,2048]{1,0:T(8,128)(2,1)}, u32[]{:S(2)}) copy-start(bf16[144,2048]{1,0:T(8,128)(2,1)} %param.12) | copy-start | bytes 1769476
  93.7 20.3 %collective-permute-start.17 = (bf16[144,2048]{1,0:T(8,128)(2,1)S(1)}, bf16[144,2048]{1,0:T(8,128)(2,1)S(1)}, u32[]{:S(2)}, u32[]{:S(2)}) collective-permute-start(bf16[144,2048]{1,0:T(8,128)(2,1)S(1)} %add_convert_fusion.1), channel_id=1, source_target_pairs={{2,4},{7,9},{8,14},{13,3},{18,20},{23,25},{24,30},{29,19}} | collective-permute-start | bytes 1769480 | tf_op jit(solution)/shard_map/rows3/ppermute | solution.py:148
  94.6 19.5 %collective-permute-start.16 = (bf16[144,2048]{1,0:T(8,128)(2,1)S(1)}, bf16[144,2048]{1,0:T(8,128)(2,1)S(1)}, u32[]{:S(2)}, u32[]{:S(2)}) collective-permute-start(bf16[144,2048]{1,0:T(8,128)(2,1)S(1)} %add_convert_fusion.1), channel_id=1, source_target_pairs={{0,4},{5,9},{10,14},{15,3},{16,20},{21,25},{26,30},{31,19}} | collective-permute-start | bytes 1769480 | tf_op jit(solution)/shard_map/rows3/ppermute | solution.py:148
  95.5 12.5 %collective-permute-start.23 = (f32[16]{0:T(128)S(1)}, f32[16]{0:T(128)S(1)}, u32[]{:S(2)}, u32[]{:S(2)}) collective-permute-start(f32[16]{0:T(128)S(1)} %add.217), channel_id=1, source_target_pairs={{0,12},{4,0},{8,4},{12,8},{1,13},{5,1},{9,5},{13,9},{2,14},{6,2},{... | collective-permute-start | bytes 200 | tf_op jit(solution)/shard_map/turns_ctx/ppermute | solution.py:103
  107.3 3.3 %collective-permute-start.22 = (f32[16]{0:T(128)S(1)}, f32[16]{0:T(128)S(1)}, u32[]{:S(2)}, u32[]{:S(2)}) collective-permute-start(f32[16]{0:T(128)S(1)} %add.217), channel_id=1, source_target_pairs={{0,8},{4,12},{8,0},{12,4},{1,9},{5,13},{9,1},{13,5},{2,10},{6,14},... | collective-permute-start | bytes 200 | tf_op jit(solution)/shard_map/turns_ctx/ppermute | solution.py:103
  107.3 6.2 %collective-permute-start.21 = (f32[16]{0:T(128)S(1)}, f32[16]{0:T(128)S(1)}, u32[]{:S(2)}, u32[]{:S(2)}) collective-permute-start(f32[16]{0:T(128)S(1)} %add.217), channel_id=1, source_target_pairs={{0,4},{4,8},{8,12},{12,0},{1,5},{5,9},{9,13},{13,1},{2,6},{6,10},{... | collective-permute-start | bytes 200 | tf_op jit(solution)/shard_map/turns_ctx/ppermute | solution.py:103

commit v3 on v2

--- a/solution.py
+++ b/solution.py
@@ -60,15 +60,16 @@
 
 def pack_kernel(key_ref, value_ref, line_ref, out_ref):
     rows, cols = key_ref.shape
-    width = out_ref.shape[1]
     out_ref[:rows, :cols] = key_ref[...]
     out_ref[:rows, cols:] = value_ref[...]
+    count, length = line_ref.shape
     extra = out_ref.shape[0] - rows
-    at = lax.broadcasted_iota(jnp.int32, (extra, width), 0)
-    lines = jnp.zeros((extra, width), jnp.float32)
-    for r in range(line_ref.shape[0]):
+    at = lax.broadcasted_iota(jnp.int32, (extra, length), 0)
+    lines = jnp.zeros((extra, length), jnp.float32)
+    for r in range(count):
         lines = jnp.where(at == r, line_ref[r : r + 1, :].astype(jnp.float32), lines)
-    out_ref[rows:, :] = lines.astype(out_ref.dtype)
+    out_ref[rows:, :] = jnp.zeros((extra, out_ref.shape[1]), out_ref.dtype)
+    out_ref[rows:, :length] = lines.astype(out_ref.dtype)
 
 
 def pack(keys, values, lines):
@@ -102,9 +103,10 @@
     def ring(x, step):
         return lax.ppermute(x, "ctx", [(i, (i + step) % n_ctx) for i in range(n_ctx)])
 
-    width = keys.shape[1] + values.shape[1]
+    width = min(tok_rows, keys.shape[1] + values.shape[1])
     per_number = -(-tok_rows // width)
-    packed = pack(keys, values, jnp.pad(turn_ids, (0, per_number * width - tok_rows)).reshape(-1, width))
+    lines = jnp.pad(turn_ids, (0, per_number * width - tok_rows)).reshape(per_number, width)
+    packed = pack(keys, values, lines)
     with jax.named_scope("kv"):
         packed = [packed] + [ring(packed, s) for s in range(1, n_ctx)]
     kv = jnp.concatenate([block[:tok_rows] for block in packed], axis=0)
@@ -150,104 +152,70 @@
     def add(*terms):
         return sum(term.astype(wide) for term in terms).astype(jnp.bfloat16)
 
-    def sibling(name, x):
-        return send(name, x, lambda c, t: (c, t ^ 1))
-
-    def across(name, x, bit):
-        return send(
-            name, x, lambda c, t: (c, t ^ bit) if (t ^ c) & bit and not (t ^ c) & (bit - 2) else None
-        )
-
-    def to_rows(name, x, step, differ):
-        return send(
-            name, x, lambda c, t: (c - step, c & -2 | t & 1) if (t ^ c) & -2 == differ else None
-        )
-
     barrier = lax.optimization_barrier
-    top = n_tp // 2
-    columns = out_weight.shape[1] // 2
     tp = lax.axis_index("tp")
-    second = tp % 2 == 1
+    near, own_core = (tp ^ ctx) & 2 == 0, (tp ^ ctx) & 1 == 0
 
     head_block = send("head", value_head, lambda c, t: (t, c))
     token_score = jnp.dot(residual, value_head, preferred_element_type=wide)
     sums = jnp.sum(one_hot(turn_ids).astype(wide) * token_score[None, :], axis=1)
-    turns = [block[tok_rows : tok_rows + per_number].reshape(-1)[:tok_rows] for block in packed]
+    turns = [block[tok_rows : tok_rows + per_number, :width].reshape(-1)[:tok_rows] for block in packed]
     hots = [one_hot(block) for block in turns]
     counts = sum(jnp.sum(hot.astype(wide), axis=1) for hot in hots)
     through = jnp.zeros((TURNS, out_weight.shape[1]), wide)
 
     def project(piece):
-        part = jnp.dot(piece, out_weight, preferred_element_type=wide).astype(jnp.bfloat16)
-        low, high = part[:, :columns], part[:, columns:]
-        return part, jnp.where(second, high, low), jnp.where(second, low, high)
+        return jnp.dot(piece, out_weight, preferred_element_type=wide).astype(jnp.bfloat16)
 
     def per_turn(s, part):
         return jnp.dot(hots[s], part, preferred_element_type=wide)
-
-    def core_sum(keep, give, pieces):
-        cut = columns // pieces
-        return add(
-            keep,
-            jnp.concatenate(
-                [sibling("core", give[:, i * cut : (i + 1) * cut]) for i in range(pieces)], axis=1
-            ),
-        )
 
     def ring_on(piece):
         with jax.named_scope("heads"):
             return ring(piece, 1)
 
     following = ring_on(piece)
-    part, keep, give = project(piece)
-    through = through + per_turn(0, part)
-    piece, keep, give, through = barrier((following, keep, give, through))
+    zero = project(piece)
+    through = through + per_turn(0, zero)
+    piece, zero, through = barrier((following, zero, through))
 
     following = ring_on(piece)
-    first = core_sum(keep, give, 1)
-    crossed = across("x", first, top)
-    piece, first = barrier((piece, first))
-    part, keep, give = project(piece)
-    through = through + per_turn(1, part)
-    piece, keep, give, crossed, through = barrier((following, keep, give, crossed, through))
+    one = project(piece)
+    through = through + per_turn(1, one)
+    piece, zero, one, through = barrier((following, zero, one, through))
 
     following = ring_on(piece)
-    chip = core_sum(keep, give, 1)
-    even = jnp.where((tp ^ ctx) & -2 == 0, add(first, crossed), 0.0)
-    crossed = across("x", chip, top)
-    piece, chip, even = barrier((piece, chip, even))
-    part, keep, give = project(piece)
-    through = through + per_turn(2, part)
-    piece, keep, give, crossed, through = barrier((following, keep, give, crossed, through))
-
-    odd = to_rows("rows1", add(chip, crossed), 1, 0)
-    chip = core_sum(keep, give, 1)
-    back = [to_rows("rows2", chip, 2, differ) for differ in (0, top)]
+    arrived = send("core01", jnp.where(own_core, one, zero), lambda c, t: (c, t ^ 1))
+    chip = add(jnp.where(own_core, zero, one), arrived)
     piece, chip = barrier((piece, chip))
-    part = jnp.dot(piece, out_weight, preferred_element_type=wide).astype(jnp.bfloat16)
-    arrived = send("core", part, lambda c, t: (c, t ^ 1) if (t ^ c) & 1 else None)
+    crossed = send("x01", chip, lambda c, t: (c, t ^ 2) if (t ^ c) in (1, 2) else None)
+    two = project(piece)
+    through = through + per_turn(2, two)
+    piece, two, chip, crossed, through = barrier((following, two, chip, crossed, through))
+    settled = add(chip, crossed)
+
+    part = project(piece)
     through = through + per_turn(3, part)
     sums = sums + jnp.sum(through * head_block.astype(wide)[None, :], axis=1)
+    arrived = send("core23", jnp.where(own_core, two, part), lambda c, t: (c, t ^ 1))
+    chip = add(jnp.where(own_core, part, two), arrived)
+    returned = [
+        send(
+            "home",
+            jnp.where(tp ^ ctx == 3, settled, chip),
+            lambda c, t: {0: (c + 1, c), 1: (c - 2, c), 3: (c - 1, c)}.get(t ^ c),
+        ),
+        send("home2", chip, lambda c, t: {2: (c + 1, c), 3: (c - 2, c)}.get(t ^ c)),
+    ]
     bit = 1
     while bit < n_tp:
         with jax.named_scope("turns_tp"):
             sums = sums + lax.ppermute(sums, "tp", [(t, t ^ bit) for t in range(n_tp)])
         bit *= 2
-    chip = add(part, arrived)
-    last = [
-        send("rows3", chip, lambda c, t: (c + 1, c) if t ^ c == differ else None)
-        for differ in (0, top)
-    ]
-    even = add(even, *back)
-    mine = (tp ^ ctx) & 1 == 0
-    other = sibling("swap", jnp.where(mine, odd, even))
-    same = jnp.where(mine, even, odd)
-    sums, chip = barrier((sums, chip))
     with jax.named_scope("turns_ctx"):
         sums = sum([ring(sums, step) for step in range(1, n_ctx)], sums)
-    low, high = jnp.where(second, other, same), jnp.where(second, same, other)
-    hidden_out = add(residual, jnp.concatenate([low, high], axis=1), *last)
-    return (hidden_out, sums / jnp.maximum(counts, 1.0))
+    mine = jnp.where(tp == ctx, settled, 0.0)
+    return (add(residual, mine, *returned), sums / jnp.maximum(counts, 1.0))
 
 
 def solution(mesh):

time: 116 us -> 112 us (0.966)
  the two profiles are of different devices: /device:TPU:1 before, /device:TPU:2 now
where the time goes in v3:
time: 112 us; the launch traced here: 111 us
  waiting for transfers between devices  65.3 us (58%)
  starting transfers between devices  20.1 us (18%)
  matrix products  11.1 us (10%)
  other arithmetic  6.02 us (5%)
  Pallas kernels  4.41 us (4%)
  local copies, waits for them, and re-layouts  2.62 us (2%)
    ppermute x9, waiting for transfers between devices, ring(): lax.ppermute(x, 'ctx', [(i, (i + step) % n_ctx) for i in range(n_ctx)])  57.1 us
    ppermute x6, starting transfers between devices, send(): return lax.ppermute(x, both, pairs)  10.7 us
    dot_general x4, matrix products, project(): jnp.dot(piece, out_weight, preferred_element_type=wide).astype(jnp.bfloat16)  10.1 us
    ppermute x9, starting transfers between devices, ring(): lax.ppermute(x, 'ctx', [(i, (i + step) % n_ctx) for i in range(n_ctx)])  9.12 us
    ppermute x2, waiting for transfers between devices, shards(): sums = sums + lax.ppermute(sums, 'tp', [(t, t ^ bit) for t in range(n_tp)])  4.22 us
    ppermute x6, waiting for transfers between devices, send(): return lax.ppermute(x, both, pairs)  3.93 us
    pallas_call x1, Pallas kernels, attend(): pl.pallas_call(attention, out_shape=jax.ShapeDtypeStruct(queries.shape, j...  2.81 us
  transfers between devices with their start and end apart: 17, of which 9 were waited for; matrix products, arithmetic and copies ran while one was open for 16% of the time, Pallas kernels for 0%

profile of v3, /device:TPU:2, one launch (start us, length us, event | category | flops | bytes accessed | tf_op | source)
XLA Modules:
  0.0 110.5 jit_solution(14902168514951518294)
XLA Ops:
  0.6 1.6 %pack.1 = bf16[160,512]{1,0:T(8,128)(2,1)} custom-call(bf16[144,256]{1,0:T(8,128)(2,1)} %key_ref.1, bf16[144,256]{1,0:T(8,128)(2,1)} %value_ref.1, s32[1,144]{1,0:T(1,128)} %bitcast.19), custom_call_target="tpu_custom_call" | custom-call | tf_op jit(solution)/shard_map/pack/pallas_call | solution.py:78
  2.2 3.6 %collective-permute-start.2 = (bf16[160,512]{1,0:T(8,128)(2,1)}, bf16[160,512]{1,0:T(8,128)(2,1)S(1)}, u32[]{:S(2)}, u32[]{:S(2)}) collective-permute-start(bf16[160,512]{1,0:T(8,128)(2,1)} %pack.1), channel_id=1, source_target_pairs={{0,12},{4,0},{8,4},{12,8},{1,13},{5,1},{9,5},{13,9},{2,14},{6,2},{... | collective-permute-start | bytes 491528 | tf_op jit(solution)/shard_map/kv/ppermute | solution.py:104
  5.8 1.0 collective-permute-start
  6.9 0.7 select_subtract_fusion
  7.6 0.1 pad_add_fusion
  7.7 1.0 slice.32
  8.7 0.1 copy.12.span_ref
  8.8 0.7 slice_reduce_fusion.3
  9.5 1.3 %collective-permute-done.2 = bf16[160,512]{1,0:T(8,128)(2,1)S(1)} collective-permute-done((bf16[160,512]{1,0:T(8,128)(2,1)}, bf16[160,512]{1,0:T(8,128)(2,1)S(1)}, u32[]{:S(2)}, u32[]{:S(2)}) %collective-permute-start.2) | collective-permute-done | bytes 163872 | tf_op jit(solution)/shard_map/kv/ppermute | solution.py:104
  10.8 9.1 %collective-permute-done.1 = bf16[160,512]{1,0:T(8,128)(2,1)S(1)} collective-permute-done((bf16[160,512]{1,0:T(8,128)(2,1)}, bf16[160,512]{1,0:T(8,128)(2,1)S(1)}, u32[]{:S(2)}, u32[]{:S(2)}) %collective-permute-start.1) | collective-permute-done | bytes 163872 | tf_op jit(solution)/shard_map/kv/ppermute | solution.py:104
  20.0 2.8 %attention.1 = bf16[144,2048]{1,0:T(8,128)(2,1)S(1)} custom-call(bf16[144,2048]{1,0:T(8,128)(2,1)S(1)} %copy-done, bf16[576,512]{1,0:T(8,128)(2,1)S(1)} %pad_maximum_fusion.kv_ref, s32[1,576]{1,0:T(1,128)S(1)} %broadcast_in_dim.5.token_ref, s32[144,2]{1,0:T(8,128)S(1)} %copy.12.span_ref), custom_call_target="tpu_custom_call" | custom-call | tf_op jit(solution)/shard_map/attention/pallas_call | solution.py:49
  22.9 1.0 collective-permute-start.3
  23.9 4.9 %convolution_convert_fusion.3 = bf16[144,2048]{1,0:T(8,128)(2,1)S(1)} fusion(bf16[144,2048]{1,0:T(8,128)(2,1)S(1)} %attention.1, bf16[2048,2048]{1,0:T(8,128)(2,1)} %param.13), kind=kOutput, calls=%fused_computation.3 | convolution fusion | flops 1208254464 | bytes 9568256 | tf_op jit(solution)/shard_map/dot_general | solution.py:168
  28.9 0.2 fusion.4
  29.1 10.5 %collective-permute-done.3 = bf16[144,2048]{1,0:T(8,128)(2,1)S(1)} collective-permute-done((bf16[144,2048]{1,0:T(8,128)(2,1)S(1)}, bf16[144,2048]{1,0:T(8,128)(2,1)S(1)}, u32[]{:S(2)}, u32[]{:S(2)}) %collective-permute-start.3) | collective-permute-done | bytes 589856 | tf_op jit(solution)/shard_map/heads/ppermute | solution.py:104
  39.5 1.4 %convolution_convert_fusion.2 = bf16[144,2048]{1,0:T(8,128)(2,1)S(1)} fusion(bf16[144,2048]{1,0:T(8,128)(2,1)S(1)} %collective-permute-done.3, bf16[2048,2048]{1,0:T(8,128)(2,1)S(1)} %bitcast.18), kind=kOutput, calls=%fused_computation.2 | convolution fusion | flops 1208254464 | bytes 9568256 | tf_op jit(solution)/shard_map/dot_general | solution.py:168
  41.0 0.2 fusion.3
  41.2 14.0 %collective-permute-done.4 = bf16[144,2048]{1,0:T(8,128)(2,1)S(1)} collective-permute-done((bf16[144,2048]{1,0:T(8,128)(2,1)S(1)}, bf16[144,2048]{1,0:T(8,128)(2,1)S(1)}, u32[]{:S(2)}, u32[]{:S(2)}) %collective-permute-start.4) | collective-permute-done | bytes 589856 | tf_op jit(solution)/shard_map/heads/ppermute | solution.py:104
  55.2 0.1 broadcast_select_fusion.2
  55.4 1.9 %collective-permute-start.11 = (bf16[2048]{0:T(1024)(128)(2,1)S(1)}, bf16[2048]{0:T(1024)(128)(2,1)S(1)}, u32[]{:S(2)}, u32[]{:S(2)}) collective-permute-start(bf16[2048]{0:T(1024)(128)(2,1)S(1)} %copy-done.5), channel_id=1, source_target_pairs={{0,0},{1,4},{2,8},{3,12},{4,1},{5,5},{6,9},{7,13},{8,2},{9,6},{10,... | collective-permute-start | bytes 12296 | tf_op jit(solution)/shard_map/head/ppermute | solution.py:150
  57.4 0.3 add_convert_fusion.3
  57.7 4.6 %collective-permute-start.7 = (bf16[144,2048]{1,0:T(8,128)(2,1)S(1)}, bf16[144,2048]{1,0:T(8,128)(2,1)S(1)}, u32[]{:S(2)}, u32[]{:S(2)}) collective-permute-start(bf16[144,2048]{1,0:T(8,128)(2,1)S(1)} %add_convert_fusion.3), channel_id=1, source_target_pairs={{1,3},{2,0},{4,6},{7,5},{8,10},{11,9},{13,15},{14,12},{17,19},{18,... | collective-permute-start | bytes 1769480 | tf_op jit(solution)/shard_map/x01/ppermute | solution.py:150
  62.3 1.4 %convolution_convert_fusion.1 = bf16[144,2048]{1,0:T(8,128)(2,1)S(1)} fusion(bf16[144,2048]{1,0:T(8,128)(2,1)S(1)} %collective-permute-done.4, bf16[2048,2048]{1,0:T(8,128)(2,1)S(1)} %bitcast.18), kind=kOutput, calls=%fused_computation.1 | convolution fusion | flops 1208254464 | bytes 9568256 | tf_op jit(solution)/shard_map/dot_general | solution.py:168
  63.7 0.2 fusion.2
  63.9 0.7 add.182
  64.6 10.3 %collective-permute-done.5 = bf16[144,2048]{1,0:T(8,128)(2,1)S(1)} collective-permute-done((bf16[144,2048]{1,0:T(8,128)(2,1)S(1)}, bf16[144,2048]{1,0:T(8,128)(2,1)S(1)}, u32[]{:S(2)}, u32[]{:S(2)}) %collective-permute-start.5) | collective-permute-done | bytes 589856 | tf_op jit(solution)/shard_map/heads/ppermute | solution.py:104
  74.9 2.3 %broadcast_select_fusion.1 = (bf16[144,2048]{1,0:T(8,128)(2,1)}, bf16[144,2048]{1,0:T(8,128)(2,1)S(1)}) fusion(bf16[144,2048]{1,0:T(8,128)(2,1)S(1)} %convolution_convert_fusion.1, pred[]{:T(512)S(6)} %eq.96, bf16[144,2048]{1,0:T(8,128)(2,1)S(1)} %collective-permute-done.5, bf16[2048,2048]{1,0:T(8,128)(2,1)S(1)} %bitcast.18), kind=kOutput, calls=%fused_computation.10 | convolution fusion | flops 1208549376 | bytes 10747905 | tf_op jit(solution)/shard_map/dot_general | solution.py:168
  77.2 0.3 fusion.9
  77.5 0.7 multiply_reduce_fusion.1
  78.1 0.6 convert_reduce_fusion.3
  78.8 0.7 slice_reduce_fusion
  79.5 0.1 convert_reduce_fusion
  79.6 0.5 broadcast_select_fusion
  80.1 1.3 %collective-permute-start.9 = (bf16[144,2048]{1,0:T(8,128)(2,1)S(1)}, bf16[144,2048]{1,0:T(8,128)(2,1)S(1)}, u32[]{:S(2)}, u32[]{:S(2)}) collective-permute-start(bf16[144,2048]{1,0:T(8,128)(2,1)S(1)} %get-tuple-element.30), channel_id=1, source_target_pairs={{0,4},{1,8},{3,12},{4,13},{5,9},{6,1},{9,6},{10,14},{11,2},{12,11}... | collective-permute-start | bytes 1769480 | tf_op jit(solution)/shard_map/home/ppermute | solution.py:150
  81.4 2.9 %collective-permute-start.10 = (bf16[144,2048]{1,0:T(8,128)(2,1)S(1)}, bf16[144,2048]{1,0:T(8,128)(2,1)S(1)}, u32[]{:S(2)}, u32[]{:S(2)}) collective-permute-start(bf16[144,2048]{1,0:T(8,128)(2,1)S(1)} %get-tuple-element.31), channel_id=1, source_target_pairs={{2,4},{3,8},{6,13},{7,9},{8,14},{9,2},{12,7},{13,3},{18,20},{19,24... | collective-permute-start | bytes 1769480 | tf_op jit(solution)/shard_map/home2/ppermute | solution.py:150
  84.3 0.2 fusion.1
  84.5 0.1 multiply_reduce_fusion
  84.7 0.3 collective-permute-start.12
  84.9 0.1 convert_reduce_fusion.1
  85.0 0.8 collective-permute-done.12
  85.9 0.1 convert_reduce_fusion.2
  86.0 3.4 %collective-permute-done.13 = f32[16]{0:T(128)S(1)} collective-permute-done((f32[16]{0:T(128)S(1)}, f32[16]{0:T(128)S(1)}, u32[]{:S(2)}, u32[]{:S(2)}) %collective-permute-start.13) | collective-permute-done | bytes 96 | tf_op jit(solution)/shard_map/turns_tp/ppermute | solution.py:213
  89.4 2.9 %collective-permute-start.16 = (f32[16]{0:T(128)S(1)}, f32[16]{0:T(128)S(1)}, u32[]{:S(2)}, u32[]{:S(2)}) collective-permute-start(f32[16]{0:T(128)S(1)} %add.191), channel_id=1, source_target_pairs={{0,12},{4,0},{8,4},{12,8},{1,13},{5,1},{9,5},{13,9},{2,14},{6,2},{... | collective-permute-start | bytes 200 | tf_op jit(solution)/shard_map/turns_ctx/ppermute | solution.py:104
  92.3 0.6 collective-permute-start.14
  92.8 11.9 %collective-permute-done.16 = f32[16]{0:T(128)S(1)} collective-permute-done((f32[16]{0:T(128)S(1)}, f32[16]{0:T(128)S(1)}, u32[]{:S(2)}, u32[]{:S(2)}) %collective-permute-start.16) | collective-permute-done | bytes 96 | tf_op jit(solution)/shard_map/turns_ctx/ppermute | solution.py:104
  104.8 0.5 maximum_divide_fusion
  105.3 3.9 %collective-permute-done.10 = bf16[144,2048]{1,0:T(8,128)(2,1)S(1)} collective-permute-done((bf16[144,2048]{1,0:T(8,128)(2,1)S(1)}, bf16[144,2048]{1,0:T(8,128)(2,1)S(1)}, u32[]{:S(2)}, u32[]{:S(2)}) %collective-permute-start.10) | collective-permute-done | bytes 589856 | tf_op jit(solution)/shard_map/home2/ppermute | solution.py:150
  109.2 1.3 %add_convert_fusion = bf16[144,2048]{1,0:T(8,128)(2,1)} fusion(bf16[144,2048]{1,0:T(8,128)(2,1)S(1)} %collective-permute-done.10, bf16[144,2048]{1,0:T(8,128)(2,1)S(1)} %collective-permute-done.9, bf16[144,2048]{1,0:T(8,128)(2,1)S(1)} %copy-done.1, pred[]{:T(512)S(6)} %eq.87, bf16[144,2048]{1,0:T(8,128)(2,1)S(1)} %collective-permute-done.7, ...), kind=kLoop, calls=%fused_computation.4 | loop fusion | flops 3833856 | bytes 3538945 | tf_op jit(solution)/shard_map/convert_element_type | solution.py:153
  (53 shorter events, 0.4 us)
Async XLA Ops:
  2.2 8.6 %collective-permute-start.2 = (bf16[160,512]{1,0:T(8,128)(2,1)}, bf16[160,512]{1,0:T(8,128)(2,1)S(1)}, u32[]{:S(2)}, u32[]{:S(2)}) collective-permute-start(bf16[160,512]{1,0:T(8,128)(2,1)} %pack.1), channel_id=1, source_target_pairs={{0,12},{4,0},{8,4},{12,8},{1,13},{5,1},{9,5},{13,9},{2,14},{6,2},{... | collective-permute-start | bytes 491528 | tf_op jit(solution)/shard_map/kv/ppermute | solution.py:104
  5.8 14.1 %collective-permute-start.1 = (bf16[160,512]{1,0:T(8,128)(2,1)}, bf16[160,512]{1,0:T(8,128)(2,1)S(1)}, u32[]{:S(2)}, u32[]{:S(2)}) collective-permute-start(bf16[160,512]{1,0:T(8,128)(2,1)} %pack.1), channel_id=1, source_target_pairs={{0,8},{4,12},{8,0},{12,4},{1,9},{5,13},{9,1},{13,5},{2,10},{6,14},... | collective-permute-start | bytes 491528 | tf_op jit(solution)/shard_map/kv/ppermute | solution.py:104
  5.8 14.1 %collective-permute-start = (bf16[160,512]{1,0:T(8,128)(2,1)}, bf16[160,512]{1,0:T(8,128)(2,1)S(1)}, u32[]{:S(2)}, u32[]{:S(2)}) collective-permute-start(bf16[160,512]{1,0:T(8,128)(2,1)} %pack.1), channel_id=1, source_target_pairs={{0,4},{4,8},{8,12},{12,0},{1,5},{5,9},{9,13},{13,1},{2,6},{6,10},{... | collective-permute-start | bytes 491528 | tf_op jit(solution)/shard_map/kv/ppermute | solution.py:104
  7.6 12.4 %copy-start = (bf16[144,2048]{1,0:T(8,128)(2,1)S(1)}, bf16[144,2048]{1,0:T(8,128)(2,1)}, u32[]{:S(2)}) copy-start(bf16[144,2048]{1,0:T(8,128)(2,1)} %q_ref.1) | copy-start | bytes 1769476
  10.8 12.1 %copy-start.3 = (bf16[160,512]{1,0:T(8,128)(2,1)}, bf16[160,512]{1,0:T(8,128)(2,1)S(1)}, u32[]{:S(2)}) copy-start(bf16[160,512]{1,0:T(8,128)(2,1)S(1)} %collective-permute-done.2) | copy-start | bytes 491524
  20.0 19.5 %slice-start = ((s8[8388608]{0:T(1024)(128)(4,1)}), s8[4194304]{0:T(1024)(128)(4,1)S(1)}, s32[]{:S(2)}) async-start(s8[8388608]{0:T(1024)(128)(4,1)} %bitcast.17), calls=%async_computation | async-start | bytes 8388608
  22.9 16.7 %collective-permute-start.3 = (bf16[144,2048]{1,0:T(8,128)(2,1)S(1)}, bf16[144,2048]{1,0:T(8,128)(2,1)S(1)}, u32[]{:S(2)}, u32[]{:S(2)}) collective-permute-start(bf16[144,2048]{1,0:T(8,128)(2,1)S(1)} %attention.1), channel_id=1, source_target_pairs={{0,4},{4,8},{8,12},{12,0},{1,5},{5,9},{9,13},{13,1},{2,6},{6,10},{... | collective-permute-start | bytes 1769480 | tf_op jit(solution)/shard_map/heads/ppermute | solution.py:104
  23.9 15.6 %slice-start.1 = ((s8[8388608]{0:T(1024)(128)(4,1)}), s8[4194304]{0:T(1024)(128)(4,1)S(1)}, s32[]{:S(2)}) async-start(s8[8388608]{0:T(1024)(128)(4,1)} %bitcast.17), calls=%async_computation.1 | async-start | bytes 8388608
  39.5 15.7 %collective-permute-start.4 = (bf16[144,2048]{1,0:T(8,128)(2,1)S(1)}, bf16[144,2048]{1,0:T(8,128)(2,1)S(1)}, u32[]{:S(2)}, u32[]{:S(2)}) collective-permute-start(bf16[144,2048]{1,0:T(8,128)(2,1)S(1)} %collective-permute-done.3), channel_id=1, source_target_pairs={{0,4},{4,8},{8,12},{12,0},{1,5},{5,9},{9,13},{13,1},{2,6},{6,10},{... | collective-permute-start | bytes 1769480 | tf_op jit(solution)/shard_map/heads/ppermute | solution.py:104
  41.2 14.2 %copy-start.5 = (bf16[2048]{0:T(1024)(128)(2,1)S(1)}, bf16[2048]{0:T(1024)(128)(2,1)}, u32[]{:S(2)}) copy-start(bf16[2048]{0:T(1024)(128)(2,1)} %param.14) | copy-start | bytes 12292
  55.3 2.1 %collective-permute-start.6 = (bf16[144,2048]{1,0:T(8,128)(2,1)S(1)}, bf16[144,2048]{1,0:T(8,128)(2,1)S(1)}, u32[]{:S(2)}, u32[]{:S(2)}) collective-permute-start(bf16[144,2048]{1,0:T(8,128)(2,1)S(1)} %broadcast_select_fusion.2), channel_id=1, source_target_pairs={{0,1},{1,0},{2,3},{3,2},{4,5},{5,4},{6,7},{7,6},{8,9},{9,8},{10,11... | collective-permute-start | bytes 1769480 | tf_op jit(solution)/shard_map/core01/ppermute | solution.py:150
  55.4 23.4 %collective-permute-start.11 = (bf16[2048]{0:T(1024)(128)(2,1)S(1)}, bf16[2048]{0:T(1024)(128)(2,1)S(1)}, u32[]{:S(2)}, u32[]{:S(2)}) collective-permute-start(bf16[2048]{0:T(1024)(128)(2,1)S(1)} %copy-done.5), channel_id=1, source_target_pairs={{0,0},{1,4},{2,8},{3,12},{4,1},{5,5},{6,9},{7,13},{8,2},{9,6},{10,... | collective-permute-start | bytes 12296 | tf_op jit(solution)/shard_map/head/ppermute | solution.py:150
  57.3 17.6 %collective-permute-start.5 = (bf16[144,2048]{1,0:T(8,128)(2,1)S(1)}, bf16[144,2048]{1,0:T(8,128)(2,1)S(1)}, u32[]{:S(2)}, u32[]{:S(2)}) collective-permute-start(bf16[144,2048]{1,0:T(8,128)(2,1)S(1)} %collective-permute-done.4), channel_id=1, source_target_pairs={{0,4},{4,8},{8,12},{12,0},{1,5},{5,9},{9,13},{13,1},{2,6},{6,10},{... | collective-permute-start | bytes 1769480 | tf_op jit(solution)/shard_map/heads/ppermute | solution.py:104
  57.7 17.2 %collective-permute-start.7 = (bf16[144,2048]{1,0:T(8,128)(2,1)S(1)}, bf16[144,2048]{1,0:T(8,128)(2,1)S(1)}, u32[]{:S(2)}, u32[]{:S(2)}) collective-permute-start(bf16[144,2048]{1,0:T(8,128)(2,1)S(1)} %add_convert_fusion.3), channel_id=1, source_target_pairs={{1,3},{2,0},{4,6},{7,5},{8,10},{11,9},{13,15},{14,12},{17,19},{18,... | collective-permute-start | bytes 1769480 | tf_op jit(solution)/shard_map/x01/ppermute | solution.py:150
  64.6 12.6 %copy-start.1 = (bf16[144,2048]{1,0:T(8,128)(2,1)S(1)}, bf16[144,2048]{1,0:T(8,128)(2,1)}, u32[]{:S(2)}) copy-start(bf16[144,2048]{1,0:T(8,128)(2,1)} %param.12) | copy-start | bytes 1769476
  64.6 12.9 %copy-start.4 = (s32[144]{0:T(256)S(1)}, s32[144]{0:T(256)}, u32[]{:S(2)}) copy-start(s32[144]{0:T(256)} %param.16) | copy-start | bytes 1732
  77.2 2.4 %collective-permute-start.8 = (bf16[144,2048]{1,0:T(8,128)(2,1)}, bf16[144,2048]{1,0:T(8,128)(2,1)S(1)}, u32[]{:S(2)}, u32[]{:S(2)}) collective-permute-start(bf16[144,2048]{1,0:T(8,128)(2,1)} %get-tuple-element.32), channel_id=1, source_target_pairs={{0,1},{1,0},{2,3},{3,2},{4,5},{5,4},{6,7},{7,6},{8,9},{9,8},{10,11... | collective-permute-start | bytes 1769480 | tf_op jit(solution)/shard_map/core23/ppermute | solution.py:150
  79.6 4.9 %copy-start.2 = (f32[16,2048]{1,0:T(8,128)S(1)}, f32[16,2048]{1,0:T(8,128)}, u32[]{:S(2)}) copy-start(f32[16,2048]{1,0:T(8,128)} %add.182) | copy-start | bytes 393220
  79.6 5.0 %copy-start.7 = (f32[16]{0:T(128)S(1)}, f32[16]{0:T(128)}, u32[]{:S(2)}) copy-start(f32[16]{0:T(128)} %multiply_reduce_fusion.1) | copy-start | bytes 196
  79.6 25.1 %copy-start.6 = (f32[16]{0:T(128)S(1)}, f32[16]{0:T(128)}, u32[]{:S(2)}) copy-start(f32[16]{0:T(128)} %convert_reduce_fusion.3) | copy-start | bytes 196
  80.1 25.1 %collective-permute-start.9 = (bf16[144,2048]{1,0:T(8,128)(2,1)S(1)}, bf16[144,2048]{1,0:T(8,128)(2,1)S(1)}, u32[]{:S(2)}, u32[]{:S(2)}) collective-permute-start(bf16[144,2048]{1,0:T(8,128)(2,1)S(1)} %get-tuple-element.30), channel_id=1, source_target_pairs={{0,4},{1,8},{3,12},{4,13},{5,9},{6,1},{9,6},{10,14},{11,2},{12,11}... | collective-permute-start | bytes 1769480 | tf_op jit(solution)/shard_map/home/ppermute | solution.py:150
  81.4 27.8 %collective-permute-start.10 = (bf16[144,2048]{1,0:T(8,128)(2,1)S(1)}, bf16[144,2048]{1,0:T(8,128)(2,1)S(1)}, u32[]{:S(2)}, u32[]{:S(2)}) collective-permute-start(bf16[144,2048]{1,0:T(8,128)(2,1)S(1)} %get-tuple-element.31), channel_id=1, source_target_pairs={{2,4},{3,8},{6,13},{7,9},{8,14},{9,2},{12,7},{13,3},{18,20},{19,24... | collective-permute-start | bytes 1769480 | tf_op jit(solution)/shard_map/home2/ppermute | solution.py:150
  84.7 1.2 %collective-permute-start.12 = (f32[16]{0:T(128)S(1)}, f32[16]{0:T(128)S(1)}, u32[]{:S(2)}, u32[]{:S(2)}) collective-permute-start(f32[16]{0:T(128)S(1)} %add.189), channel_id=1, source_target_pairs={{0,1},{1,0},{2,3},{3,2},{4,5},{5,4},{6,7},{7,6},{8,9},{9,8},{10,11... | collective-permute-start | bytes 200 | tf_op jit(solution)/shard_map/turns_tp/ppermute | solution.py:213
  85.9 3.5 %collective-permute-start.13 = (f32[16]{0:T(128)S(1)}, f32[16]{0:T(128)S(1)}, u32[]{:S(2)}, u32[]{:S(2)}) collective-permute-start(f32[16]{0:T(128)S(1)} %add.190), channel_id=1, source_target_pairs={{0,2},{1,3},{2,0},{3,1},{4,6},{5,7},{6,4},{7,5},{8,10},{9,11},{10,... | collective-permute-start | bytes 200 | tf_op jit(solution)/shard_map/turns_tp/ppermute | solution.py:213
  89.4 15.3 %collective-permute-start.16 = (f32[16]{0:T(128)S(1)}, f32[16]{0:T(128)S(1)}, u32[]{:S(2)}, u32[]{:S(2)}) collective-permute-start(f32[16]{0:T(128)S(1)} %add.191), channel_id=1, source_target_pairs={{0,12},{4,0},{8,4},{12,8},{1,13},{5,1},{9,5},{13,9},{2,14},{6,2},{... | collective-permute-start | bytes 200 | tf_op jit(solution)/shard_map/turns_ctx/ppermute | solution.py:104
  92.3 12.5 %collective-permute-start.15 = (f32[16]{0:T(128)S(1)}, f32[16]{0:T(128)S(1)}, u32[]{:S(2)}, u32[]{:S(2)}) collective-permute-start(f32[16]{0:T(128)S(1)} %add.191), channel_id=1, source_target_pairs={{0,8},{4,12},{8,0},{12,4},{1,9},{5,13},{9,1},{13,5},{2,10},{6,14},... | collective-permute-start | bytes 200 | tf_op jit(solution)/shard_map/turns_ctx/ppermute | solution.py:104
  92.3 12.5 %collective-permute-start.14 = (f32[16]{0:T(128)S(1)}, f32[16]{0:T(128)S(1)}, u32[]{:S(2)}, u32[]{:S(2)}) collective-permute-start(f32[16]{0:T(128)S(1)} %add.191), channel_id=1, source_target_pairs={{0,4},{4,8},{8,12},{12,0},{1,5},{5,9},{9,13},{13,1},{2,6},{6,10},{... | collective-permute-start | bytes 200 | tf_op jit(solution)/shard_map/turns_ctx/ppermute | solution.py:104

commit v4 on v3

--- a/solution.py
+++ b/solution.py
@@ -157,6 +157,7 @@
     near, own_core = (tp ^ ctx) & 2 == 0, (tp ^ ctx) & 1 == 0
 
     head_block = send("head", value_head, lambda c, t: (t, c))
+    piece, head_block = barrier((piece, head_block))
     token_score = jnp.dot(residual, value_head, preferred_element_type=wide)
     sums = jnp.sum(one_hot(turn_ids).astype(wide) * token_score[None, :], axis=1)
     turns = [block[tok_rows : tok_rows + per_number, :width].reshape(-1)[:tok_rows] for block in packed]
@@ -177,7 +178,7 @@
     following = ring_on(piece)
     zero = project(piece)
     through = through + per_turn(0, zero)
-    piece, zero, through = barrier((following, zero, through))
+    piece, zero, through, hots, counts, sums = barrier((following, zero, through, hots, counts, sums))
 
     following = ring_on(piece)
     one = project(piece)
@@ -199,19 +200,22 @@
     sums = sums + jnp.sum(through * head_block.astype(wide)[None, :], axis=1)
     arrived = send("core23", jnp.where(own_core, two, part), lambda c, t: (c, t ^ 1))
     chip = add(jnp.where(own_core, part, two), arrived)
+    mixed = jnp.where(tp ^ ctx == 3, settled, chip)
+    with jax.named_scope("turns_core"):
+        sums = sums + lax.ppermute(sums, "tp", [(t, t ^ 1) for t in range(n_tp)])
+    chip, mixed, sums = barrier((chip, mixed, sums))
+    with jax.named_scope("turns_chip"):
+        sums = sums + lax.ppermute(sums, "tp", [(t, t ^ 2) for t in range(n_tp)])
+    arrived = send("x2", chip, lambda c, t: (c, t ^ 2) if t ^ c == 3 else None)
+    arrived, sums = barrier((arrived, sums))
     returned = [
+        send("home13", mixed, lambda c, t: {0: (c + 1, c), 3: (c - 1, c)}.get(t ^ c)),
         send(
-            "home",
-            jnp.where(tp ^ ctx == 3, settled, chip),
-            lambda c, t: {0: (c + 1, c), 1: (c - 2, c), 3: (c - 1, c)}.get(t ^ c),
+            "home23",
+            jnp.where(own_core, chip, add(chip, arrived)),
+            lambda c, t: {2: (c + 1, c), 1: (c - 2, c)}.get(t ^ c),
         ),
-        send("home2", chip, lambda c, t: {2: (c + 1, c), 3: (c - 2, c)}.get(t ^ c)),
     ]
-    bit = 1
-    while bit < n_tp:
-        with jax.named_scope("turns_tp"):
-            sums = sums + lax.ppermute(sums, "tp", [(t, t ^ bit) for t in range(n_tp)])
-        bit *= 2
     with jax.named_scope("turns_ctx"):
         sums = sum([ring(sums, step) for step in range(1, n_ctx)], sums)
     mine = jnp.where(tp == ctx, settled, 0.0)

time: 112 us -> 109 us (0.973)
  waiting for transfers between devices: 65.3 us -> 57.8 us
  starting transfers between devices: 20.1 us -> 24.8 us
    ppermute x9, waiting for transfers between devices: 57.1 us -> 46.7 us  [ring(): lax.ppermute(x, 'ctx', [(i, (i + step) % n_ctx) for i in range(n_ctx)])]
    ppermute x6 -> x7, starting transfers between devices: 10.7 us -> 15.9 us  [send(): return lax.ppermute(x, both, pairs)]
    ppermute x6 -> x7, waiting for transfers between devices: 3.93 us -> 7.77 us  [send(): return lax.ppermute(x, both, pairs)]
    ppermute x9, starting transfers between devices: 9.12 us -> 7.73 us  [ring(): lax.ppermute(x, 'ctx', [(i, (i + step) % n_ctx) for i in range(n_ctx)])]
  transfers between devices with their start and end apart: 17 -> 18, of which waited for: 9 -> 10; matrix products, arithmetic and copies ran while one was open for 16% -> 14% of each run, Pallas kernels for 0% -> 3%
where the time goes in v4:
time: 109 us; the launch traced here: 108 us
  waiting for transfers between devices  57.8 us (53%)
  starting transfers between devices  24.8 us (23%)
  matrix products  11.5 us (11%)
  other arithmetic  5.6 us (5%)
  Pallas kernels  4.41 us (4%)
  local copies, waits for them, and re-layouts  2.62 us (2%)
    ppermute x9, waiting for transfers between devices, ring(): lax.ppermute(x, 'ctx', [(i, (i + step) % n_ctx) for i in range(n_ctx)])  46.7 us
    ppermute x7, starting transfers between devices, send(): return lax.ppermute(x, both, pairs)  15.9 us
    dot_general x4, matrix products, project(): jnp.dot(piece, out_weight, preferred_element_type=wide).astype(jnp.bfloat16)  9.44 us
    ppermute x7, waiting for transfers between devices, send(): return lax.ppermute(x, both, pairs)  7.77 us
    ppermute x9, starting transfers between devices, ring(): lax.ppermute(x, 'ctx', [(i, (i + step) % n_ctx) for i in range(n_ctx)])  7.73 us
    pallas_call x1, Pallas kernels, attend(): pl.pallas_call(attention, out_shape=jax.ShapeDtypeStruct(queries.shape, j...  2.81 us
    convert_element_type x2, other arithmetic, add(): return sum((term.astype(wide) for term in terms)).astype(jnp.bfloat16)  2.64 us
    ppermute x1, waiting for transfers between devices, shards(): sums = sums + lax.ppermute(sums, 'tp', [(t, t ^ 2) for t in range(n_tp)])  2.27 us
  transfers between devices with their start and end apart: 18, of which 10 were waited for; matrix products, arithmetic and copies ran while one was open for 14% of the time, Pallas kernels for 3%

profile of v4, /device:TPU:2, one launch (start us, length us, event | category | flops | bytes accessed | tf_op | source)
XLA Modules:
  0.0 107.8 jit_solution(3326732807308996420)
XLA Ops:
  0.6 1.6 %pack.1 = bf16[160,512]{1,0:T(8,128)(2,1)} custom-call(bf16[144,256]{1,0:T(8,128)(2,1)} %key_ref.1, bf16[144,256]{1,0:T(8,128)(2,1)} %value_ref.1, s32[1,144]{1,0:T(1,128)} %bitcast.22), custom_call_target="tpu_custom_call" | custom-call | tf_op jit(solution)/shard_map/pack/pallas_call | solution.py:78
  2.2 3.6 %collective-permute-start.2 = (bf16[160,512]{1,0:T(8,128)(2,1)}, bf16[160,512]{1,0:T(8,128)(2,1)S(1)}, u32[]{:S(2)}, u32[]{:S(2)}) collective-permute-start(bf16[160,512]{1,0:T(8,128)(2,1)} %pack.1), channel_id=1, source_target_pairs={{0,12},{4,0},{8,4},{12,8},{1,13},{5,1},{9,5},{13,9},{2,14},{6,2},{... | collective-permute-start | bytes 491528 | tf_op jit(solution)/shard_map/kv/ppermute | solution.py:104
  5.9 1.0 collective-permute-start
  6.9 3.8 %collective-permute-start.3 = (bf16[2048]{0:T(1024)(128)(2,1)}, bf16[2048]{0:T(1024)(128)(2,1)S(1)}, u32[]{:S(2)}, u32[]{:S(2)}) collective-permute-start(bf16[2048]{0:T(1024)(128)(2,1)} %param.14), channel_id=1, source_target_pairs={{0,0},{1,4},{2,8},{3,12},{4,1},{5,5},{6,9},{7,13},{8,2},{9,6},{10,... | collective-permute-start | bytes 12296 | tf_op jit(solution)/shard_map/head/ppermute | solution.py:150
  10.7 0.7 reshape.34
  11.4 0.7 slice_reduce_fusion.3
  12.2 0.7 select_subtract_fusion
  12.9 0.1 convert_reduce_fusion.3
  13.0 1.3 %fusion.5 = f32[1,144]{1,0:T(1,128)S(1)} fusion(bf16[144,2048]{1,0:T(8,128)(2,1)} %param.12, bf16[2048,1]{0,1:T(2,128)(2,1)S(1)} %reshape.34), kind=kOutput, calls=%fused_computation.44 | convolution fusion | flops 589824 | bytes 594496 | tf_op jit(solution)/shard_map/dot_general | solution.py:161
  14.4 1.0 slice.32
  15.6 0.1 multiply_reduce_fusion.1
  15.7 4.2 %collective-permute-done.1 = bf16[160,512]{1,0:T(8,128)(2,1)S(1)} collective-permute-done((bf16[160,512]{1,0:T(8,128)(2,1)}, bf16[160,512]{1,0:T(8,128)(2,1)S(1)}, u32[]{:S(2)}, u32[]{:S(2)}) %collective-permute-start.1) | collective-permute-done | bytes 163872 | tf_op jit(solution)/shard_map/kv/ppermute | solution.py:104
  20.0 0.1 convert_reduce_fusion
  20.2 0.1 convert_reduce_fusion.1
  20.3 2.8 %attention.1 = bf16[144,2048]{1,0:T(8,128)(2,1)S(1)} custom-call(bf16[144,2048]{1,0:T(8,128)(2,1)S(1)} %copy-done, bf16[576,512]{1,0:T(8,128)(2,1)S(1)} %pad_maximum_fusion.kv_ref, s32[1,576]{1,0:T(1,128)S(1)} %broadcast_in_dim.5.token_ref, s32[144,2]{1,0:T(8,128)S(1)} %copy.12.span_ref), custom_call_target="tpu_custom_call" | custom-call | tf_op jit(solution)/shard_map/attention/pallas_call | solution.py:49
  23.2 0.1 convert_reduce_fusion.2
  23.3 1.0 collective-permute-start.4
  24.3 5.1 %convolution_convert_fusion.3 = bf16[144,2048]{1,0:T(8,128)(2,1)S(1)} fusion(bf16[144,2048]{1,0:T(8,128)(2,1)S(1)} %attention.1, bf16[2048,2048]{1,0:T(8,128)(2,1)} %param.13), kind=kOutput, calls=%fused_computation.3 | convolution fusion | flops 1208254464 | bytes 9568256 | tf_op jit(solution)/shard_map/dot_general | solution.py:169
  29.4 0.2 fusion.3
  29.6 10.4 %collective-permute-done.4 = bf16[144,2048]{1,0:T(8,128)(2,1)S(1)} collective-permute-done((bf16[144,2048]{1,0:T(8,128)(2,1)S(1)}, bf16[144,2048]{1,0:T(8,128)(2,1)S(1)}, u32[]{:S(2)}, u32[]{:S(2)}) %collective-permute-start.4) | collective-permute-done | bytes 589856 | tf_op jit(solution)/shard_map/heads/ppermute | solution.py:104
  40.0 1.4 %convolution_convert_fusion.2 = bf16[144,2048]{1,0:T(8,128)(2,1)S(1)} fusion(bf16[144,2048]{1,0:T(8,128)(2,1)S(1)} %collective-permute-done.4, bf16[2048,2048]{1,0:T(8,128)(2,1)S(1)} %bitcast.21), kind=kOutput, calls=%fused_computation.2 | convolution fusion | flops 1208254464 | bytes 9568256 | tf_op jit(solution)/shard_map/dot_general | solution.py:169
  41.5 0.2 fusion.6
  41.7 14.0 %collective-permute-done.5 = bf16[144,2048]{1,0:T(8,128)(2,1)S(1)} collective-permute-done((bf16[144,2048]{1,0:T(8,128)(2,1)S(1)}, bf16[144,2048]{1,0:T(8,128)(2,1)S(1)}, u32[]{:S(2)}, u32[]{:S(2)}) %collective-permute-start.5) | collective-permute-done | bytes 589856 | tf_op jit(solution)/shard_map/heads/ppermute | solution.py:104
  55.9 1.9 %collective-permute-done.7 = bf16[144,2048]{1,0:T(8,128)(2,1)S(1)} collective-permute-done((bf16[144,2048]{1,0:T(8,128)(2,1)S(1)}, bf16[144,2048]{1,0:T(8,128)(2,1)S(1)}, u32[]{:S(2)}, u32[]{:S(2)}) %collective-permute-start.7) | collective-permute-done | bytes 589856 | tf_op jit(solution)/shard_map/core01/ppermute | solution.py:150
  57.8 0.3 add_convert_fusion.4
  58.1 2.5 %collective-permute-start.8 = (bf16[144,2048]{1,0:T(8,128)(2,1)S(1)}, bf16[144,2048]{1,0:T(8,128)(2,1)S(1)}, u32[]{:S(2)}, u32[]{:S(2)}) collective-permute-start(bf16[144,2048]{1,0:T(8,128)(2,1)S(1)} %add_convert_fusion.4), channel_id=1, source_target_pairs={{1,3},{2,0},{4,6},{7,5},{8,10},{11,9},{13,15},{14,12},{17,19},{18,... | collective-permute-start | bytes 1769480 | tf_op jit(solution)/shard_map/x01/ppermute | solution.py:150
  60.6 1.4 %convolution_convert_fusion.1 = bf16[144,2048]{1,0:T(8,128)(2,1)S(1)} fusion(bf16[144,2048]{1,0:T(8,128)(2,1)S(1)} %collective-permute-done.5, bf16[2048,2048]{1,0:T(8,128)(2,1)S(1)} %bitcast.21), kind=kOutput, calls=%fused_computation.1 | convolution fusion | flops 1208254464 | bytes 9568256 | tf_op jit(solution)/shard_map/dot_general | solution.py:169
  62.1 0.2 fusion.7
  62.3 11.1 %collective-permute-done.6 = bf16[144,2048]{1,0:T(8,128)(2,1)S(1)} collective-permute-done((bf16[144,2048]{1,0:T(8,128)(2,1)S(1)}, bf16[144,2048]{1,0:T(8,128)(2,1)S(1)}, u32[]{:S(2)}, u32[]{:S(2)}) %collective-permute-start.6) | collective-permute-done | bytes 589856 | tf_op jit(solution)/shard_map/heads/ppermute | solution.py:104
  73.3 1.5 %broadcast_select_fusion.1 = (bf16[144,2048]{1,0:T(8,128)(2,1)S(1)}, bf16[144,2048]{1,0:T(8,128)(2,1)S(1)}) fusion(bf16[144,2048]{1,0:T(8,128)(2,1)S(1)} %convolution_convert_fusion.1, pred[]{:T(512)S(6)} %eq.107, bf16[144,2048]{1,0:T(8,128)(2,1)S(1)} %collective-permute-done.6, bf16[2048,2048]{1,0:T(8,128)(2,1)S(1)} %bitcast.21), kind=kOutput, calls=%fused_computation.12 | convolution fusion | flops 1208549376 | bytes 10747905 | tf_op jit(solution)/shard_map/dot_general | solution.py:169
  74.9 0.2 fusion.8
  75.1 0.1 multiply_reduce_fusion
  75.3 0.6 collective-permute-start.10
  75.8 1.1 %collective-permute-done.10 = f32[16]{0:T(128)S(1)} collective-permute-done((f32[16]{0:T(128)S(1)}, f32[16]{0:T(128)S(1)}, u32[]{:S(2)}, u32[]{:S(2)}) %collective-permute-start.10) | collective-permute-done | bytes 96 | tf_op jit(solution)/shard_map/turns_core/ppermute | solution.py:205
  76.9 0.5 broadcast_select_fusion
  77.4 0.8 collective-permute-start.12
  78.3 0.6 collective-permute-start.13
  78.9 0.7 collective-permute-start.11
  79.6 2.3 %collective-permute-done.13 = f32[16]{0:T(128)S(1)} collective-permute-done((f32[16]{0:T(128)S(1)}, f32[16]{0:T(128)S(1)}, u32[]{:S(2)}, u32[]{:S(2)}) %collective-permute-start.13) | collective-permute-done | bytes 96 | tf_op jit(solution)/shard_map/turns_chip/ppermute | solution.py:208
  81.9 0.2 fusion
  82.1 7.9 %collective-permute-start.14 = (bf16[144,2048]{1,0:T(8,128)(2,1)S(1)}, bf16[144,2048]{1,0:T(8,128)(2,1)}, u32[]{:S(2)}, u32[]{:S(2)}) collective-permute-start(bf16[144,2048]{1,0:T(8,128)(2,1)S(1)} %fusion), channel_id=1, source_target_pairs={{1,8},{2,4},{4,13},{7,9},{8,14},{11,2},{13,3},{14,7},{17,24},{18,2... | collective-permute-start | bytes 1769480 | tf_op jit(solution)/shard_map/home23/ppermute | solution.py:150
  90.0 1.1 %collective-permute-start.17 = (f32[16]{0:T(128)S(1)}, f32[16]{0:T(128)S(1)}, u32[]{:S(2)}, u32[]{:S(2)}) collective-permute-start(f32[16]{0:T(128)S(1)} %add.196), channel_id=1, source_target_pairs={{0,12},{4,0},{8,4},{12,8},{1,13},{5,1},{9,5},{13,9},{2,14},{6,2},{... | collective-permute-start | bytes 200 | tf_op jit(solution)/shard_map/turns_ctx/ppermute | solution.py:104
  91.1 1.0 collective-permute-start.15
  92.1 6.9 %collective-permute-done.17 = f32[16]{0:T(128)S(1)} collective-permute-done((f32[16]{0:T(128)S(1)}, f32[16]{0:T(128)S(1)}, u32[]{:S(2)}, u32[]{:S(2)}) %collective-permute-start.17) | collective-permute-done | bytes 96 | tf_op jit(solution)/shard_map/turns_ctx/ppermute | solution.py:104
  99.0 0.1 collective-permute-done.16
  99.1 0.5 maximum_divide_fusion
  99.6 5.8 %collective-permute-done.14 = bf16[144,2048]{1,0:T(8,128)(2,1)} collective-permute-done((bf16[144,2048]{1,0:T(8,128)(2,1)S(1)}, bf16[144,2048]{1,0:T(8,128)(2,1)}, u32[]{:S(2)}, u32[]{:S(2)}) %collective-permute-start.14) | collective-permute-done | bytes 589856 | tf_op jit(solution)/shard_map/home23/ppermute | solution.py:150
  105.5 2.4 %add_convert_fusion = bf16[144,2048]{1,0:T(8,128)(2,1)} fusion(bf16[144,2048]{1,0:T(8,128)(2,1)} %collective-permute-done.14, bf16[144,2048]{1,0:T(8,128)(2,1)S(1)} %collective-permute-done.11, bf16[144,2048]{1,0:T(8,128)(2,1)S(1)} %copy-done.1, pred[]{:T(512)S(6)} %eq.87, bf16[144,2048]{1,0:T(8,128)(2,1)S(1)} %collective-permute-done.8, ...), kind=kLoop, calls=%fused_computation.4 | loop fusion | flops 3833856 | bytes 3538945 | tf_op jit(solution)/shard_map/convert_element_type | solution.py:153
  (50 shorter events, 0.8 us)
Async XLA Ops:
  0.6 14.9 %copy-start.2 = (s32[144]{0:T(256)S(1)}, s32[144]{0:T(256)}, u32[]{:S(2)}) copy-start(s32[144]{0:T(256)} %param.16) | copy-start | bytes 1732
  2.2 13.4 %collective-permute-start.2 = (bf16[160,512]{1,0:T(8,128)(2,1)}, bf16[160,512]{1,0:T(8,128)(2,1)S(1)}, u32[]{:S(2)}, u32[]{:S(2)}) collective-permute-start(bf16[160,512]{1,0:T(8,128)(2,1)} %pack.1), channel_id=1, source_target_pairs={{0,12},{4,0},{8,4},{12,8},{1,13},{5,1},{9,5},{13,9},{2,14},{6,2},{... | collective-permute-start | bytes 491528 | tf_op jit(solution)/shard_map/kv/ppermute | solution.py:104
  5.8 14.1 %collective-permute-start.1 = (bf16[160,512]{1,0:T(8,128)(2,1)}, bf16[160,512]{1,0:T(8,128)(2,1)S(1)}, u32[]{:S(2)}, u32[]{:S(2)}) collective-permute-start(bf16[160,512]{1,0:T(8,128)(2,1)} %pack.1), channel_id=1, source_target_pairs={{0,8},{4,12},{8,0},{12,4},{1,9},{5,13},{9,1},{13,5},{2,10},{6,14},... | collective-permute-start | bytes 491528 | tf_op jit(solution)/shard_map/kv/ppermute | solution.py:104
  5.9 14.3 %collective-permute-start = (bf16[160,512]{1,0:T(8,128)(2,1)}, bf16[160,512]{1,0:T(8,128)(2,1)S(1)}, u32[]{:S(2)}, u32[]{:S(2)}) collective-permute-start(bf16[160,512]{1,0:T(8,128)(2,1)} %pack.1), channel_id=1, source_target_pairs={{0,4},{4,8},{8,12},{12,0},{1,5},{5,9},{9,13},{13,1},{2,6},{6,10},{... | collective-permute-start | bytes 491528 | tf_op jit(solution)/shard_map/kv/ppermute | solution.py:104
  6.9 16.3 %collective-permute-start.3 = (bf16[2048]{0:T(1024)(128)(2,1)}, bf16[2048]{0:T(1024)(128)(2,1)S(1)}, u32[]{:S(2)}, u32[]{:S(2)}) collective-permute-start(bf16[2048]{0:T(1024)(128)(2,1)} %param.14), channel_id=1, source_target_pairs={{0,0},{1,4},{2,8},{3,12},{4,1},{5,5},{6,9},{7,13},{8,2},{9,6},{10,... | collective-permute-start | bytes 12296 | tf_op jit(solution)/shard_map/head/ppermute | solution.py:150
  14.4 5.9 %copy-start = (bf16[144,2048]{1,0:T(8,128)(2,1)S(1)}, bf16[144,2048]{1,0:T(8,128)(2,1)}, u32[]{:S(2)}) copy-start(bf16[144,2048]{1,0:T(8,128)(2,1)} %q_ref.1) | copy-start | bytes 1769476
  20.3 19.6 %slice-start = ((s8[8388608]{0:T(1024)(128)(4,1)}), s8[4194304]{0:T(1024)(128)(4,1)S(1)}, s32[]{:S(2)}) async-start(s8[8388608]{0:T(1024)(128)(4,1)} %bitcast.20), calls=%async_computation | async-start | bytes 8388608
  23.3 16.7 %slice-start.1 = ((s8[8388608]{0:T(1024)(128)(4,1)}), s8[4194304]{0:T(1024)(128)(4,1)S(1)}, s32[]{:S(2)}) async-start(s8[8388608]{0:T(1024)(128)(4,1)} %bitcast.20), calls=%async_computation.1 | async-start | bytes 8388608
  23.3 16.7 %collective-permute-start.4 = (bf16[144,2048]{1,0:T(8,128)(2,1)S(1)}, bf16[144,2048]{1,0:T(8,128)(2,1)S(1)}, u32[]{:S(2)}, u32[]{:S(2)}) collective-permute-start(bf16[144,2048]{1,0:T(8,128)(2,1)S(1)} %attention.1), channel_id=1, source_target_pairs={{0,4},{4,8},{8,12},{12,0},{1,5},{5,9},{9,13},{13,1},{2,6},{6,10},{... | collective-permute-start | bytes 1769480 | tf_op jit(solution)/shard_map/heads/ppermute | solution.py:104
  40.0 15.7 %collective-permute-start.5 = (bf16[144,2048]{1,0:T(8,128)(2,1)S(1)}, bf16[144,2048]{1,0:T(8,128)(2,1)S(1)}, u32[]{:S(2)}, u32[]{:S(2)}) collective-permute-start(bf16[144,2048]{1,0:T(8,128)(2,1)S(1)} %collective-permute-done.4), channel_id=1, source_target_pairs={{0,4},{4,8},{8,12},{12,0},{1,5},{5,9},{9,13},{13,1},{2,6},{6,10},{... | collective-permute-start | bytes 1769480 | tf_op jit(solution)/shard_map/heads/ppermute | solution.py:104
  55.7 2.1 %collective-permute-start.7 = (bf16[144,2048]{1,0:T(8,128)(2,1)S(1)}, bf16[144,2048]{1,0:T(8,128)(2,1)S(1)}, u32[]{:S(2)}, u32[]{:S(2)}) collective-permute-start(bf16[144,2048]{1,0:T(8,128)(2,1)S(1)} %broadcast_select_fusion.2), channel_id=1, source_target_pairs={{0,1},{1,0},{2,3},{3,2},{4,5},{5,4},{6,7},{7,6},{8,9},{9,8},{10,11... | collective-permute-start | bytes 1769480 | tf_op jit(solution)/shard_map/core01/ppermute | solution.py:150
  55.8 17.5 %collective-permute-start.6 = (bf16[144,2048]{1,0:T(8,128)(2,1)S(1)}, bf16[144,2048]{1,0:T(8,128)(2,1)S(1)}, u32[]{:S(2)}, u32[]{:S(2)}) collective-permute-start(bf16[144,2048]{1,0:T(8,128)(2,1)S(1)} %collective-permute-done.5), channel_id=1, source_target_pairs={{0,4},{4,8},{8,12},{12,0},{1,5},{5,9},{9,13},{13,1},{2,6},{6,10},{... | collective-permute-start | bytes 1769480 | tf_op jit(solution)/shard_map/heads/ppermute | solution.py:104
  58.1 15.3 %collective-permute-start.8 = (bf16[144,2048]{1,0:T(8,128)(2,1)S(1)}, bf16[144,2048]{1,0:T(8,128)(2,1)S(1)}, u32[]{:S(2)}, u32[]{:S(2)}) collective-permute-start(bf16[144,2048]{1,0:T(8,128)(2,1)S(1)} %add_convert_fusion.4), channel_id=1, source_target_pairs={{1,3},{2,0},{4,6},{7,5},{8,10},{11,9},{13,15},{14,12},{17,19},{18,... | collective-permute-start | bytes 1769480 | tf_op jit(solution)/shard_map/x01/ppermute | solution.py:150
  74.8 2.1 %collective-permute-start.9 = (bf16[144,2048]{1,0:T(8,128)(2,1)S(1)}, bf16[144,2048]{1,0:T(8,128)(2,1)S(1)}, u32[]{:S(2)}, u32[]{:S(2)}) collective-permute-start(bf16[144,2048]{1,0:T(8,128)(2,1)S(1)} %get-tuple-element.56), channel_id=1, source_target_pairs={{0,1},{1,0},{2,3},{3,2},{4,5},{5,4},{6,7},{7,6},{8,9},{9,8},{10,11... | collective-permute-start | bytes 1769480 | tf_op jit(solution)/shard_map/core23/ppermute | solution.py:150
  75.3 1.6 %collective-permute-start.10 = (f32[16]{0:T(128)S(1)}, f32[16]{0:T(128)S(1)}, u32[]{:S(2)}, u32[]{:S(2)}) collective-permute-start(f32[16]{0:T(128)S(1)} %add.193), channel_id=1, source_target_pairs={{0,1},{1,0},{2,3},{3,2},{4,5},{5,4},{6,7},{7,6},{8,9},{9,8},{10,11... | collective-permute-start | bytes 200 | tf_op jit(solution)/shard_map/turns_core/ppermute | solution.py:205
  77.4 28.0 %copy-start.1 = (bf16[144,2048]{1,0:T(8,128)(2,1)S(1)}, bf16[144,2048]{1,0:T(8,128)(2,1)}, u32[]{:S(2)}) copy-start(bf16[144,2048]{1,0:T(8,128)(2,1)} %param.12) | copy-start | bytes 1769476
  77.4 4.5 %collective-permute-start.12 = (bf16[144,2048]{1,0:T(8,128)(2,1)S(1)}, bf16[144,2048]{1,0:T(8,128)(2,1)S(1)}, u32[]{:S(2)}, u32[]{:S(2)}) collective-permute-start(bf16[144,2048]{1,0:T(8,128)(2,1)S(1)} %get-tuple-element.49), channel_id=1, source_target_pairs={{3,1},{6,4},{9,11},{12,14},{19,17},{22,20},{25,27},{28,30}} | collective-permute-start | bytes 1769480 | tf_op jit(solution)/shard_map/x2/ppermute | solution.py:150
  78.3 3.6 %collective-permute-start.13 = (f32[16]{0:T(128)S(1)}, f32[16]{0:T(128)S(1)}, u32[]{:S(2)}, u32[]{:S(2)}) collective-permute-start(f32[16]{0:T(128)S(1)} %add.194), channel_id=1, source_target_pairs={{0,2},{1,3},{2,0},{3,1},{4,6},{5,7},{6,4},{7,5},{8,10},{9,11},{10,... | collective-permute-start | bytes 200 | tf_op jit(solution)/shard_map/turns_chip/ppermute | solution.py:208
  78.9 20.7 %collective-permute-start.11 = (bf16[144,2048]{1,0:T(8,128)(2,1)S(1)}, bf16[144,2048]{1,0:T(8,128)(2,1)S(1)}, u32[]{:S(2)}, u32[]{:S(2)}) collective-permute-start(bf16[144,2048]{1,0:T(8,128)(2,1)S(1)} %get-tuple-element.48), channel_id=1, source_target_pairs={{0,4},{3,12},{5,9},{6,1},{9,6},{10,14},{12,11},{15,3},{16,20},{19,... | collective-permute-start | bytes 1769480 | tf_op jit(solution)/shard_map/home13/ppermute | solution.py:150
  82.1 23.4 %collective-permute-start.14 = (bf16[144,2048]{1,0:T(8,128)(2,1)S(1)}, bf16[144,2048]{1,0:T(8,128)(2,1)}, u32[]{:S(2)}, u32[]{:S(2)}) collective-permute-start(bf16[144,2048]{1,0:T(8,128)(2,1)S(1)} %fusion), channel_id=1, source_target_pairs={{1,8},{2,4},{4,13},{7,9},{8,14},{11,2},{13,3},{14,7},{17,24},{18,2... | collective-permute-start | bytes 1769480 | tf_op jit(solution)/shard_map/home23/ppermute | solution.py:150
  90.0 8.9 %collective-permute-start.17 = (f32[16]{0:T(128)S(1)}, f32[16]{0:T(128)S(1)}, u32[]{:S(2)}, u32[]{:S(2)}) collective-permute-start(f32[16]{0:T(128)S(1)} %add.196), channel_id=1, source_target_pairs={{0,12},{4,0},{8,4},{12,8},{1,13},{5,1},{9,5},{13,9},{2,14},{6,2},{... | collective-permute-start | bytes 200 | tf_op jit(solution)/shard_map/turns_ctx/ppermute | solution.py:104
  91.1 7.9 %collective-permute-start.16 = (f32[16]{0:T(128)S(1)}, f32[16]{0:T(128)S(1)}, u32[]{:S(2)}, u32[]{:S(2)}) collective-permute-start(f32[16]{0:T(128)S(1)} %add.196), channel_id=1, source_target_pairs={{0,8},{4,12},{8,0},{12,4},{1,9},{5,13},{9,1},{13,5},{2,10},{6,14},... | collective-permute-start | bytes 200 | tf_op jit(solution)/shard_map/turns_ctx/ppermute | solution.py:104
  91.1 7.9 %collective-permute-start.15 = (f32[16]{0:T(128)S(1)}, f32[16]{0:T(128)S(1)}, u32[]{:S(2)}, u32[]{:S(2)}) collective-permute-start(f32[16]{0:T(128)S(1)} %add.196), channel_id=1, source_target_pairs={{0,4},{4,8},{8,12},{12,0},{1,5},{5,9},{9,13},{13,1},{2,6},{6,10},{... | collective-permute-start | bytes 200 | tf_op jit(solution)/shard_map/turns_ctx/ppermute | solution.py:104

commit v5 on v4

--- a/solution.py
+++ b/solution.py
@@ -198,22 +198,22 @@
     part = project(piece)
     through = through + per_turn(3, part)
     sums = sums + jnp.sum(through * head_block.astype(wide)[None, :], axis=1)
-    arrived = send("core23", jnp.where(own_core, two, part), lambda c, t: (c, t ^ 1))
-    chip = add(jnp.where(own_core, part, two), arrived)
+    arrived = send("core23", jnp.where(own_core, part, two), lambda c, t: (c, t ^ 1))
+    chip = add(jnp.where(own_core, two, part), arrived)
     mixed = jnp.where(tp ^ ctx == 3, settled, chip)
     with jax.named_scope("turns_core"):
         sums = sums + lax.ppermute(sums, "tp", [(t, t ^ 1) for t in range(n_tp)])
     chip, mixed, sums = barrier((chip, mixed, sums))
     with jax.named_scope("turns_chip"):
         sums = sums + lax.ppermute(sums, "tp", [(t, t ^ 2) for t in range(n_tp)])
-    arrived = send("x2", chip, lambda c, t: (c, t ^ 2) if t ^ c == 3 else None)
+    arrived = send("x2", chip, lambda c, t: (c, c) if t ^ c == 2 else None)
     arrived, sums = barrier((arrived, sums))
     returned = [
-        send("home13", mixed, lambda c, t: {0: (c + 1, c), 3: (c - 1, c)}.get(t ^ c)),
+        send("home13", mixed, lambda c, t: {1: (c + 1, c), 3: (c - 1, c)}.get(t ^ c)),
         send(
             "home23",
-            jnp.where(own_core, chip, add(chip, arrived)),
-            lambda c, t: {2: (c + 1, c), 1: (c - 2, c)}.get(t ^ c),
+            jnp.where(own_core, add(chip, arrived), chip),
+            lambda c, t: {3: (c + 1, c), 0: (c - 2, c)}.get(t ^ c),
         ),
     ]
     with jax.named_scope("turns_ctx"):

time: 109 us -> 108 us (level)
    ppermute x7, waiting for transfers between devices: 7.77 us -> 1.94 us  [send(): return lax.ppermute(x, both, pairs)]
    ppermute x1, waiting for transfers between devices: 2.27 us -> 7.61 us  [shards(): sums = sums + lax.ppermute(sums, 'tp', [(t, t ^ 2) for t in range(n_tp)])]
    ppermute x7, starting transfers between devices: 15.9 us -> 11.1 us  [send(): return lax.ppermute(x, both, pairs)]
    ppermute x9, starting transfers between devices: 7.73 us -> 12.3 us  [ring(): lax.ppermute(x, 'ctx', [(i, (i + step) % n_ctx) for i in range(n_ctx)])]
    ppermute x9, waiting for transfers between devices: 46.7 us -> 47.8 us  [ring(): lax.ppermute(x, 'ctx', [(i, (i + step) % n_ctx) for i in range(n_ctx)])]
  transfers between devices with their start and end apart: 18 -> 18, of which waited for: 10 -> 9; matrix products, arithmetic and copies ran while one was open for 14% -> 14% of each run, Pallas kernels for 3% -> 3%
where the time goes in v5:
time: 108 us
  waiting for transfers between devices  58.5 us (54%)
  starting transfers between devices  24 us (22%)
  matrix products  11.5 us (11%)
  other arithmetic  5.6 us (5%)
  Pallas kernels  4.41 us (4%)
  local copies, waits for them, and re-layouts  2.62 us (2%)
  between operations  1.09 us (1%)
    ppermute x9, waiting for transfers between devices, ring(): lax.ppermute(x, 'ctx', [(i, (i + step) % n_ctx) for i in range(n_ctx)])  47.8 us
    ppermute x9, starting transfers between devices, ring(): lax.ppermute(x, 'ctx', [(i, (i + step) % n_ctx) for i in range(n_ctx)])  12.3 us
    ppermute x7, starting transfers between devices, send(): return lax.ppermute(x, both, pairs)  11.1 us
    dot_general x4, matrix products, project(): jnp.dot(piece, out_weight, preferred_element_type=wide).astype(jnp.bfloat16)  9.44 us
    ppermute x1, waiting for transfers between devices, shards(): sums = sums + lax.ppermute(sums, 'tp', [(t, t ^ 2) for t in range(n_tp)])  7.61 us
    pallas_call x1, Pallas kernels, attend(): pl.pallas_call(attention, out_shape=jax.ShapeDtypeStruct(queries.shape, j...  2.81 us
    convert_element_type x2, other arithmetic, add(): return sum((term.astype(wide) for term in terms)).astype(jnp.bfloat16)  2.65 us
  transfers between devices with their start and end apart: 18, of which 9 were waited for; matrix products, arithmetic and copies ran while one was open for 14% of the time, Pallas kernels for 3%

profile of v5, /device:TPU:2, one launch (start us, length us, event | category | flops | bytes accessed | tf_op | source)
XLA Modules:
  0.0 107.7 jit_solution(9546453753975500427)
XLA Ops:
  0.6 1.6 %pack.1 = bf16[160,512]{1,0:T(8,128)(2,1)} custom-call(bf16[144,256]{1,0:T(8,128)(2,1)} %key_ref.1, bf16[144,256]{1,0:T(8,128)(2,1)} %value_ref.1, s32[1,144]{1,0:T(1,128)} %bitcast.22), custom_call_target="tpu_custom_call" | custom-call | tf_op jit(solution)/shard_map/pack/pallas_call | solution.py:78
  2.2 3.6 %collective-permute-start.2 = (bf16[160,512]{1,0:T(8,128)(2,1)}, bf16[160,512]{1,0:T(8,128)(2,1)S(1)}, u32[]{:S(2)}, u32[]{:S(2)}) collective-permute-start(bf16[160,512]{1,0:T(8,128)(2,1)} %pack.1), channel_id=1, source_target_pairs={{0,12},{4,0},{8,4},{12,8},{1,13},{5,1},{9,5},{13,9},{2,14},{6,2},{... | collective-permute-start | bytes 491528 | tf_op jit(solution)/shard_map/kv/ppermute | solution.py:104
  5.9 1.0 collective-permute-start
  6.9 3.8 %collective-permute-start.3 = (bf16[2048]{0:T(1024)(128)(2,1)}, bf16[2048]{0:T(1024)(128)(2,1)S(1)}, u32[]{:S(2)}, u32[]{:S(2)}) collective-permute-start(bf16[2048]{0:T(1024)(128)(2,1)} %param.14), channel_id=1, source_target_pairs={{0,0},{1,4},{2,8},{3,12},{4,1},{5,5},{6,9},{7,13},{8,2},{9,6},{10,... | collective-permute-start | bytes 12296 | tf_op jit(solution)/shard_map/head/ppermute | solution.py:150
  10.7 0.7 reshape.34
  11.4 0.7 slice_reduce_fusion.3
  12.2 0.7 select_subtract_fusion
  12.9 0.1 convert_reduce_fusion.3
  13.0 1.3 %fusion.5 = f32[1,144]{1,0:T(1,128)S(1)} fusion(bf16[144,2048]{1,0:T(8,128)(2,1)} %param.12, bf16[2048,1]{0,1:T(2,128)(2,1)S(1)} %reshape.34), kind=kOutput, calls=%fused_computation.44 | convolution fusion | flops 589824 | bytes 594496 | tf_op jit(solution)/shard_map/dot_general | solution.py:161
  14.3 0.1 pad_add_fusion
  14.4 1.0 slice.32
  15.4 0.1 copy.12.span_ref
  15.6 0.1 multiply_reduce_fusion.1
  15.7 4.2 %collective-permute-done.1 = bf16[160,512]{1,0:T(8,128)(2,1)S(1)} collective-permute-done((bf16[160,512]{1,0:T(8,128)(2,1)}, bf16[160,512]{1,0:T(8,128)(2,1)S(1)}, u32[]{:S(2)}, u32[]{:S(2)}) %collective-permute-start.1) | collective-permute-done | bytes 163872 | tf_op jit(solution)/shard_map/kv/ppermute | solution.py:104
  20.0 0.1 convert_reduce_fusion
  20.2 0.1 convert_reduce_fusion.1
  20.3 2.8 %attention.1 = bf16[144,2048]{1,0:T(8,128)(2,1)S(1)} custom-call(bf16[144,2048]{1,0:T(8,128)(2,1)S(1)} %copy-done, bf16[576,512]{1,0:T(8,128)(2,1)S(1)} %pad_maximum_fusion.kv_ref, s32[1,576]{1,0:T(1,128)S(1)} %broadcast_in_dim.5.token_ref, s32[144,2]{1,0:T(8,128)S(1)} %copy.12.span_ref), custom_call_target="tpu_custom_call" | custom-call | tf_op jit(solution)/shard_map/attention/pallas_call | solution.py:49
  23.2 0.1 convert_reduce_fusion.2
  23.3 1.0 collective-permute-start.4
  24.3 5.1 %convolution_convert_fusion.3 = bf16[144,2048]{1,0:T(8,128)(2,1)S(1)} fusion(bf16[144,2048]{1,0:T(8,128)(2,1)S(1)} %attention.1, bf16[2048,2048]{1,0:T(8,128)(2,1)} %param.13), kind=kOutput, calls=%fused_computation.3 | convolution fusion | flops 1208254464 | bytes 9568256 | tf_op jit(solution)/shard_map/dot_general | solution.py:169
  29.4 0.2 fusion.3
  29.6 10.4 %collective-permute-done.4 = bf16[144,2048]{1,0:T(8,128)(2,1)S(1)} collective-permute-done((bf16[144,2048]{1,0:T(8,128)(2,1)S(1)}, bf16[144,2048]{1,0:T(8,128)(2,1)S(1)}, u32[]{:S(2)}, u32[]{:S(2)}) %collective-permute-start.4) | collective-permute-done | bytes 589856 | tf_op jit(solution)/shard_map/heads/ppermute | solution.py:104
  40.0 1.4 %convolution_convert_fusion.2 = bf16[144,2048]{1,0:T(8,128)(2,1)S(1)} fusion(bf16[144,2048]{1,0:T(8,128)(2,1)S(1)} %collective-permute-done.4, bf16[2048,2048]{1,0:T(8,128)(2,1)S(1)} %bitcast.21), kind=kOutput, calls=%fused_computation.2 | convolution fusion | flops 1208254464 | bytes 9568256 | tf_op jit(solution)/shard_map/dot_general | solution.py:169
  41.5 0.2 fusion.6
  41.7 14.0 %collective-permute-done.5 = bf16[144,2048]{1,0:T(8,128)(2,1)S(1)} collective-permute-done((bf16[144,2048]{1,0:T(8,128)(2,1)S(1)}, bf16[144,2048]{1,0:T(8,128)(2,1)S(1)}, u32[]{:S(2)}, u32[]{:S(2)}) %collective-permute-start.5) | collective-permute-done | bytes 589856 | tf_op jit(solution)/shard_map/heads/ppermute | solution.py:104
  55.9 1.9 %collective-permute-done.7 = bf16[144,2048]{1,0:T(8,128)(2,1)S(1)} collective-permute-done((bf16[144,2048]{1,0:T(8,128)(2,1)S(1)}, bf16[144,2048]{1,0:T(8,128)(2,1)S(1)}, u32[]{:S(2)}, u32[]{:S(2)}) %collective-permute-start.7) | collective-permute-done | bytes 589856 | tf_op jit(solution)/shard_map/core01/ppermute | solution.py:150
  57.8 0.3 add_convert_fusion.4
  58.1 2.5 %collective-permute-start.8 = (bf16[144,2048]{1,0:T(8,128)(2,1)S(1)}, bf16[144,2048]{1,0:T(8,128)(2,1)S(1)}, u32[]{:S(2)}, u32[]{:S(2)}) collective-permute-start(bf16[144,2048]{1,0:T(8,128)(2,1)S(1)} %add_convert_fusion.4), channel_id=1, source_target_pairs={{1,3},{2,0},{4,6},{7,5},{8,10},{11,9},{13,15},{14,12},{17,19},{18,... | collective-permute-start | bytes 1769480 | tf_op jit(solution)/shard_map/x01/ppermute | solution.py:150
  60.6 1.4 %convolution_convert_fusion.1 = bf16[144,2048]{1,0:T(8,128)(2,1)S(1)} fusion(bf16[144,2048]{1,0:T(8,128)(2,1)S(1)} %collective-permute-done.5, bf16[2048,2048]{1,0:T(8,128)(2,1)S(1)} %bitcast.21), kind=kOutput, calls=%fused_computation.1 | convolution fusion | flops 1208254464 | bytes 9568256 | tf_op jit(solution)/shard_map/dot_general | solution.py:169
  62.1 0.2 fusion.7
  62.3 11.1 %collective-permute-done.6 = bf16[144,2048]{1,0:T(8,128)(2,1)S(1)} collective-permute-done((bf16[144,2048]{1,0:T(8,128)(2,1)S(1)}, bf16[144,2048]{1,0:T(8,128)(2,1)S(1)}, u32[]{:S(2)}, u32[]{:S(2)}) %collective-permute-start.6) | collective-permute-done | bytes 589856 | tf_op jit(solution)/shard_map/heads/ppermute | solution.py:104
  73.3 1.5 %broadcast_select_fusion.1 = (bf16[144,2048]{1,0:T(8,128)(2,1)S(1)}, bf16[144,2048]{1,0:T(8,128)(2,1)S(1)}) fusion(bf16[144,2048]{1,0:T(8,128)(2,1)S(1)} %convolution_convert_fusion.1, pred[]{:T(512)S(6)} %eq.107, bf16[144,2048]{1,0:T(8,128)(2,1)S(1)} %collective-permute-done.6, bf16[2048,2048]{1,0:T(8,128)(2,1)S(1)} %bitcast.21), kind=kOutput, calls=%fused_computation.12 | convolution fusion | flops 1208549376 | bytes 10747905 | tf_op jit(solution)/shard_map/dot_general | solution.py:169
  74.9 0.2 fusion.8
  75.1 0.1 multiply_reduce_fusion
  75.3 0.6 collective-permute-start.10
  75.8 1.1 %collective-permute-done.10 = f32[16]{0:T(128)S(1)} collective-permute-done((f32[16]{0:T(128)S(1)}, f32[16]{0:T(128)S(1)}, u32[]{:S(2)}, u32[]{:S(2)}) %collective-permute-start.10) | collective-permute-done | bytes 96 | tf_op jit(solution)/shard_map/turns_core/ppermute | solution.py:205
  76.9 0.5 broadcast_select_fusion
  77.4 2.6 %collective-permute-start.12 = (bf16[144,2048]{1,0:T(8,128)(2,1)S(1)}, bf16[144,2048]{1,0:T(8,128)(2,1)S(1)}, u32[]{:S(2)}, u32[]{:S(2)}) collective-permute-start(bf16[144,2048]{1,0:T(8,128)(2,1)S(1)} %get-tuple-element.49), channel_id=1, source_target_pairs={{2,0},{7,5},{8,10},{13,15},{18,16},{23,21},{24,26},{29,31}} | collective-permute-start | bytes 1769480 | tf_op jit(solution)/shard_map/x2/ppermute | solution.py:150
  80.2 0.7 collective-permute-start.11
  80.9 7.6 %collective-permute-done.13 = f32[16]{0:T(128)S(1)} collective-permute-done((f32[16]{0:T(128)S(1)}, f32[16]{0:T(128)S(1)}, u32[]{:S(2)}, u32[]{:S(2)}) %collective-permute-start.13) | collective-permute-done | bytes 96 | tf_op jit(solution)/shard_map/turns_chip/ppermute | solution.py:208
  88.5 0.2 fusion
  88.7 1.3 %collective-permute-start.14 = (bf16[144,2048]{1,0:T(8,128)(2,1)S(1)}, bf16[144,2048]{1,0:T(8,128)(2,1)}, u32[]{:S(2)}, u32[]{:S(2)}) collective-permute-start(bf16[144,2048]{1,0:T(8,128)(2,1)S(1)} %fusion), channel_id=1, source_target_pairs={{0,8},{3,4},{5,13},{6,9},{9,14},{10,2},{12,3},{15,7},{16,24},{19,2... | collective-permute-start | bytes 1769480 | tf_op jit(solution)/shard_map/home23/ppermute | solution.py:150
  90.1 4.5 %collective-permute-start.16 = (f32[16]{0:T(128)S(1)}, f32[16]{0:T(128)S(1)}, u32[]{:S(2)}, u32[]{:S(2)}) collective-permute-start(f32[16]{0:T(128)S(1)} %add.196), channel_id=1, source_target_pairs={{0,8},{4,12},{8,0},{12,4},{1,9},{5,13},{9,1},{13,5},{2,10},{6,14},... | collective-permute-start | bytes 200 | tf_op jit(solution)/shard_map/turns_ctx/ppermute | solution.py:104
  94.6 2.0 %collective-permute-start.15 = (f32[16]{0:T(128)S(1)}, f32[16]{0:T(128)S(1)}, u32[]{:S(2)}, u32[]{:S(2)}) collective-permute-start(f32[16]{0:T(128)S(1)} %add.196), channel_id=1, source_target_pairs={{0,4},{4,8},{8,12},{12,0},{1,5},{5,9},{9,13},{13,1},{2,6},{6,10},{... | collective-permute-start | bytes 200 | tf_op jit(solution)/shard_map/turns_ctx/ppermute | solution.py:104
  96.6 0.8 collective-permute-done.17
  97.4 7.3 %collective-permute-done.16 = f32[16]{0:T(128)S(1)} collective-permute-done((f32[16]{0:T(128)S(1)}, f32[16]{0:T(128)S(1)}, u32[]{:S(2)}, u32[]{:S(2)}) %collective-permute-start.16) | collective-permute-done | bytes 96 | tf_op jit(solution)/shard_map/turns_ctx/ppermute | solution.py:104
  104.8 0.5 maximum_divide_fusion
  105.3 2.4 %add_convert_fusion = bf16[144,2048]{1,0:T(8,128)(2,1)} fusion(bf16[144,2048]{1,0:T(8,128)(2,1)} %collective-permute-done.14, bf16[144,2048]{1,0:T(8,128)(2,1)S(1)} %collective-permute-done.11, bf16[144,2048]{1,0:T(8,128)(2,1)S(1)} %copy-done.1, pred[]{:T(512)S(6)} %eq.87, bf16[144,2048]{1,0:T(8,128)(2,1)S(1)} %collective-permute-done.8, ...), kind=kLoop, calls=%fused_computation.4 | loop fusion | flops 3833856 | bytes 3538945 | tf_op jit(solution)/shard_map/convert_element_type | solution.py:153
  (50 shorter events, 0.7 us)
Async XLA Ops:
  0.6 14.9 %copy-start.2 = (s32[144]{0:T(256)S(1)}, s32[144]{0:T(256)}, u32[]{:S(2)}) copy-start(s32[144]{0:T(256)} %param.16) | copy-start | bytes 1732
  2.2 13.4 %collective-permute-start.2 = (bf16[160,512]{1,0:T(8,128)(2,1)}, bf16[160,512]{1,0:T(8,128)(2,1)S(1)}, u32[]{:S(2)}, u32[]{:S(2)}) collective-permute-start(bf16[160,512]{1,0:T(8,128)(2,1)} %pack.1), channel_id=1, source_target_pairs={{0,12},{4,0},{8,4},{12,8},{1,13},{5,1},{9,5},{13,9},{2,14},{6,2},{... | collective-permute-start | bytes 491528 | tf_op jit(solution)/shard_map/kv/ppermute | solution.py:104
  5.8 14.1 %collective-permute-start.1 = (bf16[160,512]{1,0:T(8,128)(2,1)}, bf16[160,512]{1,0:T(8,128)(2,1)S(1)}, u32[]{:S(2)}, u32[]{:S(2)}) collective-permute-start(bf16[160,512]{1,0:T(8,128)(2,1)} %pack.1), channel_id=1, source_target_pairs={{0,8},{4,12},{8,0},{12,4},{1,9},{5,13},{9,1},{13,5},{2,10},{6,14},... | collective-permute-start | bytes 491528 | tf_op jit(solution)/shard_map/kv/ppermute | solution.py:104
  5.9 14.3 %collective-permute-start = (bf16[160,512]{1,0:T(8,128)(2,1)}, bf16[160,512]{1,0:T(8,128)(2,1)S(1)}, u32[]{:S(2)}, u32[]{:S(2)}) collective-permute-start(bf16[160,512]{1,0:T(8,128)(2,1)} %pack.1), channel_id=1, source_target_pairs={{0,4},{4,8},{8,12},{12,0},{1,5},{5,9},{9,13},{13,1},{2,6},{6,10},{... | collective-permute-start | bytes 491528 | tf_op jit(solution)/shard_map/kv/ppermute | solution.py:104
  6.9 16.3 %collective-permute-start.3 = (bf16[2048]{0:T(1024)(128)(2,1)}, bf16[2048]{0:T(1024)(128)(2,1)S(1)}, u32[]{:S(2)}, u32[]{:S(2)}) collective-permute-start(bf16[2048]{0:T(1024)(128)(2,1)} %param.14), channel_id=1, source_target_pairs={{0,0},{1,4},{2,8},{3,12},{4,1},{5,5},{6,9},{7,13},{8,2},{9,6},{10,... | collective-permute-start | bytes 12296 | tf_op jit(solution)/shard_map/head/ppermute | solution.py:150
  14.4 5.9 %copy-start = (bf16[144,2048]{1,0:T(8,128)(2,1)S(1)}, bf16[144,2048]{1,0:T(8,128)(2,1)}, u32[]{:S(2)}) copy-start(bf16[144,2048]{1,0:T(8,128)(2,1)} %q_ref.1) | copy-start | bytes 1769476
  20.3 19.6 %slice-start = ((s8[8388608]{0:T(1024)(128)(4,1)}), s8[4194304]{0:T(1024)(128)(4,1)S(1)}, s32[]{:S(2)}) async-start(s8[8388608]{0:T(1024)(128)(4,1)} %bitcast.20), calls=%async_computation | async-start | bytes 8388608
  23.3 16.7 %slice-start.1 = ((s8[8388608]{0:T(1024)(128)(4,1)}), s8[4194304]{0:T(1024)(128)(4,1)S(1)}, s32[]{:S(2)}) async-start(s8[8388608]{0:T(1024)(128)(4,1)} %bitcast.20), calls=%async_computation.1 | async-start | bytes 8388608
  23.3 16.7 %collective-permute-start.4 = (bf16[144,2048]{1,0:T(8,128)(2,1)S(1)}, bf16[144,2048]{1,0:T(8,128)(2,1)S(1)}, u32[]{:S(2)}, u32[]{:S(2)}) collective-permute-start(bf16[144,2048]{1,0:T(8,128)(2,1)S(1)} %attention.1), channel_id=1, source_target_pairs={{0,4},{4,8},{8,12},{12,0},{1,5},{5,9},{9,13},{13,1},{2,6},{6,10},{... | collective-permute-start | bytes 1769480 | tf_op jit(solution)/shard_map/heads/ppermute | solution.py:104
  40.0 15.7 %collective-permute-start.5 = (bf16[144,2048]{1,0:T(8,128)(2,1)S(1)}, bf16[144,2048]{1,0:T(8,128)(2,1)S(1)}, u32[]{:S(2)}, u32[]{:S(2)}) collective-permute-start(bf16[144,2048]{1,0:T(8,128)(2,1)S(1)} %collective-permute-done.4), channel_id=1, source_target_pairs={{0,4},{4,8},{8,12},{12,0},{1,5},{5,9},{9,13},{13,1},{2,6},{6,10},{... | collective-permute-start | bytes 1769480 | tf_op jit(solution)/shard_map/heads/ppermute | solution.py:104
  55.7 2.1 %collective-permute-start.7 = (bf16[144,2048]{1,0:T(8,128)(2,1)S(1)}, bf16[144,2048]{1,0:T(8,128)(2,1)S(1)}, u32[]{:S(2)}, u32[]{:S(2)}) collective-permute-start(bf16[144,2048]{1,0:T(8,128)(2,1)S(1)} %broadcast_select_fusion.2), channel_id=1, source_target_pairs={{0,1},{1,0},{2,3},{3,2},{4,5},{5,4},{6,7},{7,6},{8,9},{9,8},{10,11... | collective-permute-start | bytes 1769480 | tf_op jit(solution)/shard_map/core01/ppermute | solution.py:150
  55.8 17.5 %collective-permute-start.6 = (bf16[144,2048]{1,0:T(8,128)(2,1)S(1)}, bf16[144,2048]{1,0:T(8,128)(2,1)S(1)}, u32[]{:S(2)}, u32[]{:S(2)}) collective-permute-start(bf16[144,2048]{1,0:T(8,128)(2,1)S(1)} %collective-permute-done.5), channel_id=1, source_target_pairs={{0,4},{4,8},{8,12},{12,0},{1,5},{5,9},{9,13},{13,1},{2,6},{6,10},{... | collective-permute-start | bytes 1769480 | tf_op jit(solution)/shard_map/heads/ppermute | solution.py:104
  58.1 15.3 %collective-permute-start.8 = (bf16[144,2048]{1,0:T(8,128)(2,1)S(1)}, bf16[144,2048]{1,0:T(8,128)(2,1)S(1)}, u32[]{:S(2)}, u32[]{:S(2)}) collective-permute-start(bf16[144,2048]{1,0:T(8,128)(2,1)S(1)} %add_convert_fusion.4), channel_id=1, source_target_pairs={{1,3},{2,0},{4,6},{7,5},{8,10},{11,9},{13,15},{14,12},{17,19},{18,... | collective-permute-start | bytes 1769480 | tf_op jit(solution)/shard_map/x01/ppermute | solution.py:150
  74.8 2.1 %collective-permute-start.9 = (bf16[144,2048]{1,0:T(8,128)(2,1)S(1)}, bf16[144,2048]{1,0:T(8,128)(2,1)S(1)}, u32[]{:S(2)}, u32[]{:S(2)}) collective-permute-start(bf16[144,2048]{1,0:T(8,128)(2,1)S(1)} %get-tuple-element.56), channel_id=1, source_target_pairs={{0,1},{1,0},{2,3},{3,2},{4,5},{5,4},{6,7},{7,6},{8,9},{9,8},{10,11... | collective-permute-start | bytes 1769480 | tf_op jit(solution)/shard_map/core23/ppermute | solution.py:150
  75.3 1.6 %collective-permute-start.10 = (f32[16]{0:T(128)S(1)}, f32[16]{0:T(128)S(1)}, u32[]{:S(2)}, u32[]{:S(2)}) collective-permute-start(f32[16]{0:T(128)S(1)} %add.193), channel_id=1, source_target_pairs={{0,1},{1,0},{2,3},{3,2},{4,5},{5,4},{6,7},{7,6},{8,9},{9,8},{10,11... | collective-permute-start | bytes 200 | tf_op jit(solution)/shard_map/turns_core/ppermute | solution.py:205
  77.4 27.9 %copy-start.1 = (bf16[144,2048]{1,0:T(8,128)(2,1)S(1)}, bf16[144,2048]{1,0:T(8,128)(2,1)}, u32[]{:S(2)}) copy-start(bf16[144,2048]{1,0:T(8,128)(2,1)} %param.12) | copy-start | bytes 1769476
  77.4 11.1 %collective-permute-start.12 = (bf16[144,2048]{1,0:T(8,128)(2,1)S(1)}, bf16[144,2048]{1,0:T(8,128)(2,1)S(1)}, u32[]{:S(2)}, u32[]{:S(2)}) collective-permute-start(bf16[144,2048]{1,0:T(8,128)(2,1)S(1)} %get-tuple-element.49), channel_id=1, source_target_pairs={{2,0},{7,5},{8,10},{13,15},{18,16},{23,21},{24,26},{29,31}} | collective-permute-start | bytes 1769480 | tf_op jit(solution)/shard_map/x2/ppermute | solution.py:150
  80.1 8.4 %collective-permute-start.13 = (f32[16]{0:T(128)S(1)}, f32[16]{0:T(128)S(1)}, u32[]{:S(2)}, u32[]{:S(2)}) collective-permute-start(f32[16]{0:T(128)S(1)} %add.194), channel_id=1, source_target_pairs={{0,2},{1,3},{2,0},{3,1},{4,6},{5,7},{6,4},{7,5},{8,10},{9,11},{10,... | collective-permute-start | bytes 200 | tf_op jit(solution)/shard_map/turns_chip/ppermute | solution.py:208
  80.2 25.1 %collective-permute-start.11 = (bf16[144,2048]{1,0:T(8,128)(2,1)S(1)}, bf16[144,2048]{1,0:T(8,128)(2,1)S(1)}, u32[]{:S(2)}, u32[]{:S(2)}) collective-permute-start(bf16[144,2048]{1,0:T(8,128)(2,1)S(1)} %get-tuple-element.48), channel_id=1, source_target_pairs={{1,4},{3,12},{4,9},{6,1},{9,6},{11,14},{12,11},{14,3},{17,20},{19,... | collective-permute-start | bytes 1769480 | tf_op jit(solution)/shard_map/home13/ppermute | solution.py:150
  88.7 16.6 %collective-permute-start.14 = (bf16[144,2048]{1,0:T(8,128)(2,1)S(1)}, bf16[144,2048]{1,0:T(8,128)(2,1)}, u32[]{:S(2)}, u32[]{:S(2)}) collective-permute-start(bf16[144,2048]{1,0:T(8,128)(2,1)S(1)} %fusion), channel_id=1, source_target_pairs={{0,8},{3,4},{5,13},{6,9},{9,14},{10,2},{12,3},{15,7},{16,24},{19,2... | collective-permute-start | bytes 1769480 | tf_op jit(solution)/shard_map/home23/ppermute | solution.py:150
  90.0 7.4 %collective-permute-start.17 = (f32[16]{0:T(128)S(1)}, f32[16]{0:T(128)S(1)}, u32[]{:S(2)}, u32[]{:S(2)}) collective-permute-start(f32[16]{0:T(128)S(1)} %add.196), channel_id=1, source_target_pairs={{0,12},{4,0},{8,4},{12,8},{1,13},{5,1},{9,5},{13,9},{2,14},{6,2},{... | collective-permute-start | bytes 200 | tf_op jit(solution)/shard_map/turns_ctx/ppermute | solution.py:104
  90.1 14.7 %collective-permute-start.16 = (f32[16]{0:T(128)S(1)}, f32[16]{0:T(128)S(1)}, u32[]{:S(2)}, u32[]{:S(2)}) collective-permute-start(f32[16]{0:T(128)S(1)} %add.196), channel_id=1, source_target_pairs={{0,8},{4,12},{8,0},{12,4},{1,9},{5,13},{9,1},{13,5},{2,10},{6,14},... | collective-permute-start | bytes 200 | tf_op jit(solution)/shard_map/turns_ctx/ppermute | solution.py:104
  94.6 10.2 %collective-permute-start.15 = (f32[16]{0:T(128)S(1)}, f32[16]{0:T(128)S(1)}, u32[]{:S(2)}, u32[]{:S(2)}) collective-permute-start(f32[16]{0:T(128)S(1)} %add.196), channel_id=1, source_target_pairs={{0,4},{4,8},{8,12},{12,0},{1,5},{5,9},{9,13},{13,1},{2,6},{6,10},{... | collective-permute-start | bytes 200 | tf_op jit(solution)/shard_map/turns_ctx/ppermute | solution.py:104

commit v6 on v5

--- a/solution.py
+++ b/solution.py
@@ -203,7 +203,8 @@
     mixed = jnp.where(tp ^ ctx == 3, settled, chip)
     with jax.named_scope("turns_core"):
         sums = sums + lax.ppermute(sums, "tp", [(t, t ^ 1) for t in range(n_tp)])
-    chip, mixed, sums = barrier((chip, mixed, sums))
+    base = residual.astype(wide) + jnp.where(tp == ctx, settled, 0.0).astype(wide)
+    chip, mixed, sums, base = barrier((chip, mixed, sums, base))
     with jax.named_scope("turns_chip"):
         sums = sums + lax.ppermute(sums, "tp", [(t, t ^ 2) for t in range(n_tp)])
     arrived = send("x2", chip, lambda c, t: (c, c) if t ^ c == 2 else None)
@@ -218,8 +219,7 @@
     ]
     with jax.named_scope("turns_ctx"):
         sums = sum([ring(sums, step) for step in range(1, n_ctx)], sums)
-    mine = jnp.where(tp == ctx, settled, 0.0)
-    return (add(residual, mine, *returned), sums / jnp.maximum(counts, 1.0))
+    return (add(base, *returned), sums / jnp.maximum(counts, 1.0))
 
 
 def solution(mesh):

time: 108 us -> 107 us (level)
  waiting for transfers between devices: 58.5 us -> 55.1 us
  matrix products: 11.5 us -> 14.8 us
    dot_general x4, matrix products: 9.44 us -> 12.7 us  [project(): jnp.dot(piece, out_weight, preferred_element_type=wide).astype(jnp.bfloat16)]
    ppermute x9, waiting for transfers between devices: 47.8 us -> 44.9 us  [ring(): lax.ppermute(x, 'ctx', [(i, (i + step) % n_ctx) for i in range(n_ctx)])]
    convert_element_type x2, other arithmetic: 2.65 us -> 1.37 us  [add(): return sum((term.astype(wide) for term in terms)).astype(jnp.bfloat16)]
  transfers between devices with their start and end apart: 18 -> 18, of which waited for: 9 -> 9; matrix products, arithmetic and copies ran while one was open for 14% -> 18% of each run, Pallas kernels for 3% -> 3%
where the time goes in v6:
time: 107 us; the launch traced here: 106 us
  waiting for transfers between devices  55.1 us (51%)
  starting transfers between devices  23.4 us (22%)
  matrix products  14.8 us (14%)
  other arithmetic  4.6 us (4%)
  Pallas kernels  4.41 us (4%)
  local copies, waits for them, and re-layouts  2.7 us (3%)
  between operations  1.11 us (1%)
    ppermute x9, waiting for transfers between devices, ring(): lax.ppermute(x, 'ctx', [(i, (i + step) % n_ctx) for i in range(n_ctx)])  44.9 us
    dot_general x4, matrix products, project(): jnp.dot(piece, out_weight, preferred_element_type=wide).astype(jnp.bfloat16)  12.7 us
    ppermute x9, starting transfers between devices, ring(): lax.ppermute(x, 'ctx', [(i, (i + step) % n_ctx) for i in range(n_ctx)])  11.6 us
    ppermute x7, starting transfers between devices, send(): return lax.ppermute(x, both, pairs)  11.2 us
    ppermute x1, waiting for transfers between devices, shards(): sums = sums + lax.ppermute(sums, 'tp', [(t, t ^ 2) for t in range(n_tp)])  7.61 us
    pallas_call x1, Pallas kernels, attend(): pl.pallas_call(attention, out_shape=jax.ShapeDtypeStruct(queries.shape, j...  2.81 us
  transfers between devices with their start and end apart: 18, of which 9 were waited for; matrix products, arithmetic and copies ran while one was open for 18% of the time, Pallas kernels for 3%

profile of v6, /device:TPU:2, one launch (start us, length us, event | category | flops | bytes accessed | tf_op | source)
XLA Modules:
  0.0 106.2 jit_solution(9026796477847201515)
XLA Ops:
  0.6 1.6 %pack.1 = bf16[160,512]{1,0:T(8,128)(2,1)} custom-call(bf16[144,256]{1,0:T(8,128)(2,1)} %key_ref.1, bf16[144,256]{1,0:T(8,128)(2,1)} %value_ref.1, s32[1,144]{1,0:T(1,128)} %bitcast.24), custom_call_target="tpu_custom_call" | custom-call | tf_op jit(solution)/shard_map/pack/pallas_call | solution.py:78
  2.2 3.6 %collective-permute-start.2 = (bf16[160,512]{1,0:T(8,128)(2,1)}, bf16[160,512]{1,0:T(8,128)(2,1)S(1)}, u32[]{:S(2)}, u32[]{:S(2)}) collective-permute-start(bf16[160,512]{1,0:T(8,128)(2,1)} %pack.1), channel_id=1, source_target_pairs={{0,12},{4,0},{8,4},{12,8},{1,13},{5,1},{9,5},{13,9},{2,14},{6,2},{... | collective-permute-start | bytes 491528 | tf_op jit(solution)/shard_map/kv/ppermute | solution.py:104
  5.9 1.0 collective-permute-start
  6.9 3.8 %collective-permute-start.3 = (bf16[2048]{0:T(1024)(128)(2,1)}, bf16[2048]{0:T(1024)(128)(2,1)S(1)}, u32[]{:S(2)}, u32[]{:S(2)}) collective-permute-start(bf16[2048]{0:T(1024)(128)(2,1)} %param.14), channel_id=1, source_target_pairs={{0,0},{1,4},{2,8},{3,12},{4,1},{5,5},{6,9},{7,13},{8,2},{9,6},{10,... | collective-permute-start | bytes 12296 | tf_op jit(solution)/shard_map/head/ppermute | solution.py:150
  10.7 0.7 reshape.34
  11.4 0.7 slice_reduce_fusion.3
  12.2 0.7 select_subtract_fusion
  12.9 0.1 convert_reduce_fusion.3
  13.0 1.3 %fusion.5 = f32[1,144]{1,0:T(1,128)S(1)} fusion(bf16[144,2048]{1,0:T(8,128)(2,1)} %param.12, bf16[2048,1]{0,1:T(2,128)(2,1)S(1)} %reshape.34), kind=kOutput, calls=%fused_computation.45 | convolution fusion | flops 589824 | bytes 594496 | tf_op jit(solution)/shard_map/dot_general | solution.py:161
  14.4 1.0 slice.32
  15.4 0.1 copy.12.span_ref
  15.6 0.1 multiply_reduce_fusion.1
  15.7 4.2 %collective-permute-done.1 = bf16[160,512]{1,0:T(8,128)(2,1)S(1)} collective-permute-done((bf16[160,512]{1,0:T(8,128)(2,1)}, bf16[160,512]{1,0:T(8,128)(2,1)S(1)}, u32[]{:S(2)}, u32[]{:S(2)}) %collective-permute-start.1) | collective-permute-done | bytes 163872 | tf_op jit(solution)/shard_map/kv/ppermute | solution.py:104
  20.0 0.1 convert_reduce_fusion
  20.2 0.1 convert_reduce_fusion.1
  20.3 2.8 %attention.1 = bf16[144,2048]{1,0:T(8,128)(2,1)S(1)} custom-call(bf16[144,2048]{1,0:T(8,128)(2,1)S(1)} %copy-done, bf16[576,512]{1,0:T(8,128)(2,1)S(1)} %pad_maximum_fusion.kv_ref, s32[1,576]{1,0:T(1,128)S(1)} %broadcast_in_dim.5.token_ref, s32[144,2]{1,0:T(8,128)S(1)} %copy.12.span_ref), custom_call_target="tpu_custom_call" | custom-call | tf_op jit(solution)/shard_map/attention/pallas_call | solution.py:49
  23.2 0.1 convert_reduce_fusion.2
  23.3 1.0 collective-permute-start.4
  24.3 5.1 %convolution_convert_fusion.3 = bf16[144,2048]{1,0:T(8,128)(2,1)S(1)} fusion(bf16[144,2048]{1,0:T(8,128)(2,1)S(1)} %attention.1, bf16[2048,2048]{1,0:T(8,128)(2,1)} %param.13), kind=kOutput, calls=%fused_computation.3 | convolution fusion | flops 1208254464 | bytes 9568256 | tf_op jit(solution)/shard_map/dot_general | solution.py:169
  29.4 0.2 fusion.3
  29.6 10.4 %collective-permute-done.4 = bf16[144,2048]{1,0:T(8,128)(2,1)S(1)} collective-permute-done((bf16[144,2048]{1,0:T(8,128)(2,1)S(1)}, bf16[144,2048]{1,0:T(8,128)(2,1)S(1)}, u32[]{:S(2)}, u32[]{:S(2)}) %collective-permute-start.4) | collective-permute-done | bytes 589856 | tf_op jit(solution)/shard_map/heads/ppermute | solution.py:104
  40.0 1.4 %convolution_convert_fusion.2 = bf16[144,2048]{1,0:T(8,128)(2,1)S(1)} fusion(bf16[144,2048]{1,0:T(8,128)(2,1)S(1)} %collective-permute-done.4, bf16[2048,2048]{1,0:T(8,128)(2,1)S(1)} %bitcast.21), kind=kOutput, calls=%fused_computation.2 | convolution fusion | flops 1208254464 | bytes 9568256 | tf_op jit(solution)/shard_map/dot_general | solution.py:169
  41.5 0.2 fusion.6
  41.7 14.0 %collective-permute-done.5 = bf16[144,2048]{1,0:T(8,128)(2,1)S(1)} collective-permute-done((bf16[144,2048]{1,0:T(8,128)(2,1)S(1)}, bf16[144,2048]{1,0:T(8,128)(2,1)S(1)}, u32[]{:S(2)}, u32[]{:S(2)}) %collective-permute-start.5) | collective-permute-done | bytes 589856 | tf_op jit(solution)/shard_map/heads/ppermute | solution.py:104
  55.9 1.9 %collective-permute-done.7 = bf16[144,2048]{1,0:T(8,128)(2,1)S(1)} collective-permute-done((bf16[144,2048]{1,0:T(8,128)(2,1)S(1)}, bf16[144,2048]{1,0:T(8,128)(2,1)S(1)}, u32[]{:S(2)}, u32[]{:S(2)}) %collective-permute-start.7) | collective-permute-done | bytes 589856 | tf_op jit(solution)/shard_map/core01/ppermute | solution.py:150
  57.8 0.3 add_convert_fusion.4
  58.2 2.8 %collective-permute-start.8 = (bf16[144,2048]{1,0:T(8,128)(2,1)S(1)}, bf16[144,2048]{1,0:T(8,128)(2,1)S(1)}, u32[]{:S(2)}, u32[]{:S(2)}) collective-permute-start(bf16[144,2048]{1,0:T(8,128)(2,1)S(1)} %add_convert_fusion.4), channel_id=1, source_target_pairs={{1,3},{2,0},{4,6},{7,5},{8,10},{11,9},{13,15},{14,12},{17,19},{18,... | collective-permute-start | bytes 1769480 | tf_op jit(solution)/shard_map/x01/ppermute | solution.py:150
  60.9 4.8 %convolution_convert_fusion.1 = bf16[144,2048]{1,0:T(8,128)(2,1)S(1)} fusion(bf16[144,2048]{1,0:T(8,128)(2,1)S(1)} %collective-permute-done.5, bf16[2048,2048]{1,0:T(8,128)(2,1)} %param.13), kind=kOutput, calls=%fused_computation.1 | convolution fusion | flops 1208254464 | bytes 9568256 | tf_op jit(solution)/shard_map/dot_general | solution.py:169
  65.7 0.2 fusion.7
  65.9 7.4 %collective-permute-done.6 = bf16[144,2048]{1,0:T(8,128)(2,1)S(1)} collective-permute-done((bf16[144,2048]{1,0:T(8,128)(2,1)S(1)}, bf16[144,2048]{1,0:T(8,128)(2,1)S(1)}, u32[]{:S(2)}, u32[]{:S(2)}) %collective-permute-start.6) | collective-permute-done | bytes 589856 | tf_op jit(solution)/shard_map/heads/ppermute | solution.py:104
  73.4 1.5 %broadcast_select_fusion.1 = (bf16[144,2048]{1,0:T(8,128)(2,1)S(1)}, bf16[144,2048]{1,0:T(8,128)(2,1)S(1)}) fusion(bf16[144,2048]{1,0:T(8,128)(2,1)S(1)} %convolution_convert_fusion.1, pred[]{:T(512)S(6)} %eq.87, bf16[144,2048]{1,0:T(8,128)(2,1)S(1)} %collective-permute-done.6, bf16[2048,2048]{1,0:T(8,128)(2,1)S(1)} %bitcast.23), kind=kOutput, calls=%fused_computation.13 | convolution fusion | flops 1208549376 | bytes 10747905 | tf_op jit(solution)/shard_map/dot_general | solution.py:169
  74.9 0.2 fusion.8
  75.1 0.1 multiply_reduce_fusion
  75.3 0.6 collective-permute-start.10
  75.9 0.3 convert_add_fusion
  76.2 0.7 collective-permute-done.10
  76.9 0.5 broadcast_select_fusion
  77.5 2.5 %collective-permute-start.12 = (bf16[144,2048]{1,0:T(8,128)(2,1)S(1)}, bf16[144,2048]{1,0:T(8,128)(2,1)S(1)}, u32[]{:S(2)}, u32[]{:S(2)}) collective-permute-start(bf16[144,2048]{1,0:T(8,128)(2,1)S(1)} %get-tuple-element.51), channel_id=1, source_target_pairs={{2,0},{7,5},{8,10},{13,15},{18,16},{23,21},{24,26},{29,31}} | collective-permute-start | bytes 1769480 | tf_op jit(solution)/shard_map/x2/ppermute | solution.py:150
  80.1 0.7 collective-permute-start.11
  80.8 7.6 %collective-permute-done.13 = f32[16]{0:T(128)S(1)} collective-permute-done((f32[16]{0:T(128)S(1)}, f32[16]{0:T(128)S(1)}, u32[]{:S(2)}, u32[]{:S(2)}) %collective-permute-start.13) | collective-permute-done | bytes 96 | tf_op jit(solution)/shard_map/turns_chip/ppermute | solution.py:209
  88.4 0.2 fusion
  88.6 1.3 %collective-permute-start.14 = (bf16[144,2048]{1,0:T(8,128)(2,1)S(1)}, bf16[144,2048]{1,0:T(8,128)(2,1)S(1)}, u32[]{:S(2)}, u32[]{:S(2)}) collective-permute-start(bf16[144,2048]{1,0:T(8,128)(2,1)S(1)} %fusion), channel_id=1, source_target_pairs={{0,8},{3,4},{5,13},{6,9},{9,14},{10,2},{12,3},{15,7},{16,24},{19,2... | collective-permute-start | bytes 1769480 | tf_op jit(solution)/shard_map/home23/ppermute | solution.py:150
  89.9 3.9 %collective-permute-start.16 = (f32[16]{0:T(128)S(1)}, f32[16]{0:T(128)S(1)}, u32[]{:S(2)}, u32[]{:S(2)}) collective-permute-start(f32[16]{0:T(128)S(1)} %add.196), channel_id=1, source_target_pairs={{0,8},{4,12},{8,0},{12,4},{1,9},{5,13},{9,1},{13,5},{2,10},{6,14},... | collective-permute-start | bytes 200 | tf_op jit(solution)/shard_map/turns_ctx/ppermute | solution.py:104
  93.8 1.9 %collective-permute-start.15 = (f32[16]{0:T(128)S(1)}, f32[16]{0:T(128)S(1)}, u32[]{:S(2)}, u32[]{:S(2)}) collective-permute-start(f32[16]{0:T(128)S(1)} %add.196), channel_id=1, source_target_pairs={{0,4},{4,8},{8,12},{12,0},{1,5},{5,9},{9,13},{13,1},{2,6},{6,10},{... | collective-permute-start | bytes 200 | tf_op jit(solution)/shard_map/turns_ctx/ppermute | solution.py:104
  95.8 1.5 %collective-permute-done.17 = f32[16]{0:T(128)S(1)} collective-permute-done((f32[16]{0:T(128)S(1)}, f32[16]{0:T(128)S(1)}, u32[]{:S(2)}, u32[]{:S(2)}) %collective-permute-start.17) | collective-permute-done | bytes 96 | tf_op jit(solution)/shard_map/turns_ctx/ppermute | solution.py:104
  97.3 7.3 %collective-permute-done.16 = f32[16]{0:T(128)S(1)} collective-permute-done((f32[16]{0:T(128)S(1)}, f32[16]{0:T(128)S(1)}, u32[]{:S(2)}, u32[]{:S(2)}) %collective-permute-start.16) | collective-permute-done | bytes 96 | tf_op jit(solution)/shard_map/turns_ctx/ppermute | solution.py:104
  104.6 0.5 maximum_divide_fusion
  105.1 1.0 add_convert_fusion
  (56 shorter events, 0.9 us)
Async XLA Ops:
  0.6 14.9 %copy-start.2 = (s32[144]{0:T(256)S(1)}, s32[144]{0:T(256)}, u32[]{:S(2)}) copy-start(s32[144]{0:T(256)} %param.16) | copy-start | bytes 1732
  2.2 13.4 %collective-permute-start.2 = (bf16[160,512]{1,0:T(8,128)(2,1)}, bf16[160,512]{1,0:T(8,128)(2,1)S(1)}, u32[]{:S(2)}, u32[]{:S(2)}) collective-permute-start(bf16[160,512]{1,0:T(8,128)(2,1)} %pack.1), channel_id=1, source_target_pairs={{0,12},{4,0},{8,4},{12,8},{1,13},{5,1},{9,5},{13,9},{2,14},{6,2},{... | collective-permute-start | bytes 491528 | tf_op jit(solution)/shard_map/kv/ppermute | solution.py:104
  5.8 14.1 %collective-permute-start.1 = (bf16[160,512]{1,0:T(8,128)(2,1)}, bf16[160,512]{1,0:T(8,128)(2,1)S(1)}, u32[]{:S(2)}, u32[]{:S(2)}) collective-permute-start(bf16[160,512]{1,0:T(8,128)(2,1)} %pack.1), channel_id=1, source_target_pairs={{0,8},{4,12},{8,0},{12,4},{1,9},{5,13},{9,1},{13,5},{2,10},{6,14},... | collective-permute-start | bytes 491528 | tf_op jit(solution)/shard_map/kv/ppermute | solution.py:104
  5.9 14.3 %collective-permute-start = (bf16[160,512]{1,0:T(8,128)(2,1)}, bf16[160,512]{1,0:T(8,128)(2,1)S(1)}, u32[]{:S(2)}, u32[]{:S(2)}) collective-permute-start(bf16[160,512]{1,0:T(8,128)(2,1)} %pack.1), channel_id=1, source_target_pairs={{0,4},{4,8},{8,12},{12,0},{1,5},{5,9},{9,13},{13,1},{2,6},{6,10},{... | collective-permute-start | bytes 491528 | tf_op jit(solution)/shard_map/kv/ppermute | solution.py:104
  6.9 16.3 %collective-permute-start.3 = (bf16[2048]{0:T(1024)(128)(2,1)}, bf16[2048]{0:T(1024)(128)(2,1)S(1)}, u32[]{:S(2)}, u32[]{:S(2)}) collective-permute-start(bf16[2048]{0:T(1024)(128)(2,1)} %param.14), channel_id=1, source_target_pairs={{0,0},{1,4},{2,8},{3,12},{4,1},{5,5},{6,9},{7,13},{8,2},{9,6},{10,... | collective-permute-start | bytes 12296 | tf_op jit(solution)/shard_map/head/ppermute | solution.py:150
  14.4 5.9 %copy-start = (bf16[144,2048]{1,0:T(8,128)(2,1)S(1)}, bf16[144,2048]{1,0:T(8,128)(2,1)}, u32[]{:S(2)}) copy-start(bf16[144,2048]{1,0:T(8,128)(2,1)} %q_ref.1) | copy-start | bytes 1769476
  20.3 19.6 %slice-start = ((s8[8388608]{0:T(1024)(128)(4,1)}), s8[4194304]{0:T(1024)(128)(4,1)S(1)}, s32[]{:S(2)}) async-start(s8[8388608]{0:T(1024)(128)(4,1)} %bitcast.20), calls=%async_computation | async-start | bytes 8388608
  23.3 16.7 %slice-start.1 = ((s8[8388608]{0:T(1024)(128)(4,1)}), s8[4194304]{0:T(1024)(128)(4,1)S(1)}, s32[]{:S(2)}) async-start(s8[8388608]{0:T(1024)(128)(4,1)} %bitcast.20), calls=%async_computation.1 | async-start | bytes 8388608
  23.3 16.7 %collective-permute-start.4 = (bf16[144,2048]{1,0:T(8,128)(2,1)S(1)}, bf16[144,2048]{1,0:T(8,128)(2,1)S(1)}, u32[]{:S(2)}, u32[]{:S(2)}) collective-permute-start(bf16[144,2048]{1,0:T(8,128)(2,1)S(1)} %attention.1), channel_id=1, source_target_pairs={{0,4},{4,8},{8,12},{12,0},{1,5},{5,9},{9,13},{13,1},{2,6},{6,10},{... | collective-permute-start | bytes 1769480 | tf_op jit(solution)/shard_map/heads/ppermute | solution.py:104
  40.0 15.7 %collective-permute-start.5 = (bf16[144,2048]{1,0:T(8,128)(2,1)S(1)}, bf16[144,2048]{1,0:T(8,128)(2,1)S(1)}, u32[]{:S(2)}, u32[]{:S(2)}) collective-permute-start(bf16[144,2048]{1,0:T(8,128)(2,1)S(1)} %collective-permute-done.4), channel_id=1, source_target_pairs={{0,4},{4,8},{8,12},{12,0},{1,5},{5,9},{9,13},{13,1},{2,6},{6,10},{... | collective-permute-start | bytes 1769480 | tf_op jit(solution)/shard_map/heads/ppermute | solution.py:104
  55.7 2.1 %collective-permute-start.7 = (bf16[144,2048]{1,0:T(8,128)(2,1)S(1)}, bf16[144,2048]{1,0:T(8,128)(2,1)S(1)}, u32[]{:S(2)}, u32[]{:S(2)}) collective-permute-start(bf16[144,2048]{1,0:T(8,128)(2,1)S(1)} %broadcast_select_fusion.2), channel_id=1, source_target_pairs={{0,1},{1,0},{2,3},{3,2},{4,5},{5,4},{6,7},{7,6},{8,9},{9,8},{10,11... | collective-permute-start | bytes 1769480 | tf_op jit(solution)/shard_map/core01/ppermute | solution.py:150
  55.8 17.5 %collective-permute-start.6 = (bf16[144,2048]{1,0:T(8,128)(2,1)S(1)}, bf16[144,2048]{1,0:T(8,128)(2,1)S(1)}, u32[]{:S(2)}, u32[]{:S(2)}) collective-permute-start(bf16[144,2048]{1,0:T(8,128)(2,1)S(1)} %collective-permute-done.5), channel_id=1, source_target_pairs={{0,4},{4,8},{8,12},{12,0},{1,5},{5,9},{9,13},{13,1},{2,6},{6,10},{... | collective-permute-start | bytes 1769480 | tf_op jit(solution)/shard_map/heads/ppermute | solution.py:104
  57.8 15.6 %slice-start.2 = ((s8[8388608]{0:T(1024)(128)(4,1)}), s8[4194304]{0:T(1024)(128)(4,1)S(1)}, s32[]{:S(2)}) async-start(s8[8388608]{0:T(1024)(128)(4,1)} %bitcast.22), calls=%async_computation.2 | async-start | bytes 8388608
  58.1 15.2 %slice-start.3 = ((s8[8388608]{0:T(1024)(128)(4,1)}), s8[4194304]{0:T(1024)(128)(4,1)S(1)}, s32[]{:S(2)}) async-start(s8[8388608]{0:T(1024)(128)(4,1)} %bitcast.22), calls=%async_computation.3 | async-start | bytes 8388608
  58.2 15.2 %collective-permute-start.8 = (bf16[144,2048]{1,0:T(8,128)(2,1)S(1)}, bf16[144,2048]{1,0:T(8,128)(2,1)S(1)}, u32[]{:S(2)}, u32[]{:S(2)}) collective-permute-start(bf16[144,2048]{1,0:T(8,128)(2,1)S(1)} %add_convert_fusion.4), channel_id=1, source_target_pairs={{1,3},{2,0},{4,6},{7,5},{8,10},{11,9},{13,15},{14,12},{17,19},{18,... | collective-permute-start | bytes 1769480 | tf_op jit(solution)/shard_map/x01/ppermute | solution.py:150
  74.8 1.1 %copy-start.1 = (bf16[144,2048]{1,0:T(8,128)(2,1)S(1)}, bf16[144,2048]{1,0:T(8,128)(2,1)}, u32[]{:S(2)}) copy-start(bf16[144,2048]{1,0:T(8,128)(2,1)} %param.12) | copy-start | bytes 1769476
  74.9 2.1 %collective-permute-start.9 = (bf16[144,2048]{1,0:T(8,128)(2,1)S(1)}, bf16[144,2048]{1,0:T(8,128)(2,1)S(1)}, u32[]{:S(2)}, u32[]{:S(2)}) collective-permute-start(bf16[144,2048]{1,0:T(8,128)(2,1)S(1)} %get-tuple-element.58), channel_id=1, source_target_pairs={{0,1},{1,0},{2,3},{3,2},{4,5},{5,4},{6,7},{7,6},{8,9},{9,8},{10,11... | collective-permute-start | bytes 1769480 | tf_op jit(solution)/shard_map/core23/ppermute | solution.py:150
  75.3 1.7 %collective-permute-start.10 = (f32[16]{0:T(128)S(1)}, f32[16]{0:T(128)S(1)}, u32[]{:S(2)}, u32[]{:S(2)}) collective-permute-start(f32[16]{0:T(128)S(1)} %add.192), channel_id=1, source_target_pairs={{0,1},{1,0},{2,3},{3,2},{4,5},{5,4},{6,7},{7,6},{8,9},{9,8},{10,11... | collective-permute-start | bytes 200 | tf_op jit(solution)/shard_map/turns_core/ppermute | solution.py:205
  77.5 10.9 %collective-permute-start.12 = (bf16[144,2048]{1,0:T(8,128)(2,1)S(1)}, bf16[144,2048]{1,0:T(8,128)(2,1)S(1)}, u32[]{:S(2)}, u32[]{:S(2)}) collective-permute-start(bf16[144,2048]{1,0:T(8,128)(2,1)S(1)} %get-tuple-element.51), channel_id=1, source_target_pairs={{2,0},{7,5},{8,10},{13,15},{18,16},{23,21},{24,26},{29,31}} | collective-permute-start | bytes 1769480 | tf_op jit(solution)/shard_map/x2/ppermute | solution.py:150
  80.0 8.4 %collective-permute-start.13 = (f32[16]{0:T(128)S(1)}, f32[16]{0:T(128)S(1)}, u32[]{:S(2)}, u32[]{:S(2)}) collective-permute-start(f32[16]{0:T(128)S(1)} %add.193), channel_id=1, source_target_pairs={{0,2},{1,3},{2,0},{3,1},{4,6},{5,7},{6,4},{7,5},{8,10},{9,11},{10,... | collective-permute-start | bytes 200 | tf_op jit(solution)/shard_map/turns_chip/ppermute | solution.py:209
  80.1 25.1 %collective-permute-start.11 = (bf16[144,2048]{1,0:T(8,128)(2,1)S(1)}, bf16[144,2048]{1,0:T(8,128)(2,1)S(1)}, u32[]{:S(2)}, u32[]{:S(2)}) collective-permute-start(bf16[144,2048]{1,0:T(8,128)(2,1)S(1)} %get-tuple-element.50), channel_id=1, source_target_pairs={{1,4},{3,12},{4,9},{6,1},{9,6},{11,14},{12,11},{14,3},{17,20},{19,... | collective-permute-start | bytes 1769480 | tf_op jit(solution)/shard_map/home13/ppermute | solution.py:150
  88.6 16.6 %collective-permute-start.14 = (bf16[144,2048]{1,0:T(8,128)(2,1)S(1)}, bf16[144,2048]{1,0:T(8,128)(2,1)S(1)}, u32[]{:S(2)}, u32[]{:S(2)}) collective-permute-start(bf16[144,2048]{1,0:T(8,128)(2,1)S(1)} %fusion), channel_id=1, source_target_pairs={{0,8},{3,4},{5,13},{6,9},{9,14},{10,2},{12,3},{15,7},{16,24},{19,2... | collective-permute-start | bytes 1769480 | tf_op jit(solution)/shard_map/home23/ppermute | solution.py:150
  89.9 7.4 %collective-permute-start.17 = (f32[16]{0:T(128)S(1)}, f32[16]{0:T(128)S(1)}, u32[]{:S(2)}, u32[]{:S(2)}) collective-permute-start(f32[16]{0:T(128)S(1)} %add.196), channel_id=1, source_target_pairs={{0,12},{4,0},{8,4},{12,8},{1,13},{5,1},{9,5},{13,9},{2,14},{6,2},{... | collective-permute-start | bytes 200 | tf_op jit(solution)/shard_map/turns_ctx/ppermute | solution.py:104
  89.9 14.7 %collective-permute-start.16 = (f32[16]{0:T(128)S(1)}, f32[16]{0:T(128)S(1)}, u32[]{:S(2)}, u32[]{:S(2)}) collective-permute-start(f32[16]{0:T(128)S(1)} %add.196), channel_id=1, source_target_pairs={{0,8},{4,12},{8,0},{12,4},{1,9},{5,13},{9,1},{13,5},{2,10},{6,14},... | collective-permute-start | bytes 200 | tf_op jit(solution)/shard_map/turns_ctx/ppermute | solution.py:104
  93.8 10.8 %collective-permute-start.15 = (f32[16]{0:T(128)S(1)}, f32[16]{0:T(128)S(1)}, u32[]{:S(2)}, u32[]{:S(2)}) collective-permute-start(f32[16]{0:T(128)S(1)} %add.196), channel_id=1, source_target_pairs={{0,4},{4,8},{8,12},{12,0},{1,5},{5,9},{9,13},{13,1},{2,6},{6,10},{... | collective-permute-start | bytes 200 | tf_op jit(solution)/shard_map/turns_ctx/ppermute | solution.py:104

commit v7 on v6

--- a/solution.py
+++ b/solution.py
@@ -107,11 +107,21 @@
     per_number = -(-tok_rows // width)
     lines = jnp.pad(turn_ids, (0, per_number * width - tok_rows)).reshape(per_number, width)
     packed = pack(keys, values, lines)
+    swaps = n_ctx == 4
     with jax.named_scope("kv"):
-        packed = [packed] + [ring(packed, s) for s in range(1, n_ctx)]
+        if swaps:
+            packed = [packed] + [
+                lax.ppermute(packed, "ctx", [(c, c ^ s) for c in range(n_ctx)])
+                for s in range(1, n_ctx)
+            ]
+        else:
+            packed = [packed] + [ring(packed, s) for s in range(1, n_ctx)]
     kv = jnp.concatenate([block[:tok_rows] for block in packed], axis=0)
     key_tokens = jnp.concatenate(
-        [row_tokens((ctx - s) % n_ctx, n_ctx, tok_rows) for s in range(n_ctx)]
+        [
+            row_tokens(ctx ^ s if swaps else (ctx - s) % n_ctx, n_ctx, tok_rows)
+            for s in range(n_ctx)
+        ]
     )
     tokens = row_tokens(ctx, n_ctx, tok_rows)
     span = jnp.stack([tokens - positions, tokens], axis=1)
@@ -161,6 +171,8 @@
     token_score = jnp.dot(residual, value_head, preferred_element_type=wide)
     sums = jnp.sum(one_hot(turn_ids).astype(wide) * token_score[None, :], axis=1)
     turns = [block[tok_rows : tok_rows + per_number, :width].reshape(-1)[:tok_rows] for block in packed]
+    odd = ctx % 2 == 1
+    turns[1], turns[3] = jnp.where(odd, turns[1], turns[3]), jnp.where(odd, turns[3], turns[1])
     hots = [one_hot(block) for block in turns]
     counts = sum(jnp.sum(hot.astype(wide), axis=1) for hot in hots)
     through = jnp.zeros((TURNS, out_weight.shape[1]), wide)

time: 107 us -> 106 us (level)
  starting transfers between devices: 23.4 us -> 22.3 us
    ppermute x9 -> x6, starting transfers between devices: 11.6 us -> 5.83 us  [ring(): lax.ppermute(x, 'ctx', [(i, (i + step) % n_ctx) for i in range(n_ctx)])]
    ppermute x0 -> x3, starting transfers between devices: none -> 4.39 us  [shards(): lax.ppermute(packed, 'ctx', [(c, c ^ s) for c in range(n_ctx)])]
    ppermute x9 -> x6, waiting for transfers between devices: 44.9 us -> 40.8 us  [ring(): lax.ppermute(x, 'ctx', [(i, (i + step) % n_ctx) for i in range(n_ctx)])]
    ppermute x0 -> x3, waiting for transfers between devices: none -> 3.64 us  [shards(): lax.ppermute(packed, 'ctx', [(c, c ^ s) for c in range(n_ctx)])]
where the time goes in v7:
time: 106 us; the launch traced here: 105 us
  waiting for transfers between devices  54.8 us (52%)
  starting transfers between devices  22.3 us (21%)
  matrix products  14.7 us (14%)
  other arithmetic  5.18 us (5%)
  Pallas kernels  4.41 us (4%)
  local copies, waits for them, and re-layouts  2.69 us (3%)
    ppermute x6, waiting for transfers between devices, ring(): lax.ppermute(x, 'ctx', [(i, (i + step) % n_ctx) for i in range(n_ctx)])  40.8 us
    dot_general x4, matrix products, project(): jnp.dot(piece, out_weight, preferred_element_type=wide).astype(jnp.bfloat16)  12.6 us
    ppermute x7, starting transfers between devices, send(): return lax.ppermute(x, both, pairs)  11.5 us
    ppermute x1, waiting for transfers between devices, shards(): sums = sums + lax.ppermute(sums, 'tp', [(t, t ^ 2) for t in range(n_tp)])  7.63 us
    ppermute x6, starting transfers between devices, ring(): lax.ppermute(x, 'ctx', [(i, (i + step) % n_ctx) for i in range(n_ctx)])  5.83 us
    ppermute x3, starting transfers between devices, shards(): lax.ppermute(packed, 'ctx', [(c, c ^ s) for c in range(n_ctx)])  4.39 us
    ppermute x3, waiting for transfers between devices, shards(): lax.ppermute(packed, 'ctx', [(c, c ^ s) for c in range(n_ctx)])  3.64 us
    pallas_call x1, Pallas kernels, attend(): pl.pallas_call(attention, out_shape=jax.ShapeDtypeStruct(queries.shape, j...  2.81 us
  transfers between devices with their start and end apart: 18, of which 9 were waited for; matrix products, arithmetic and copies ran while one was open for 18% of the time, Pallas kernels for 3%

profile of v7, /device:TPU:2, one launch (start us, length us, event | category | flops | bytes accessed | tf_op | source)
XLA Modules:
  0.0 105.1 jit_solution(8839228375696771696)
XLA Ops:
  0.6 1.6 %pack.1 = bf16[160,512]{1,0:T(8,128)(2,1)} custom-call(bf16[144,256]{1,0:T(8,128)(2,1)} %key_ref.1, bf16[144,256]{1,0:T(8,128)(2,1)} %value_ref.1, s32[1,144]{1,0:T(1,128)} %bitcast.24), custom_call_target="tpu_custom_call" | custom-call | tf_op jit(solution)/shard_map/pack/pallas_call | solution.py:78
  2.2 3.6 %collective-permute-start.2 = (bf16[160,512]{1,0:T(8,128)(2,1)}, bf16[160,512]{1,0:T(8,128)(2,1)S(1)}, u32[]{:S(2)}, u32[]{:S(2)}) collective-permute-start(bf16[160,512]{1,0:T(8,128)(2,1)} %pack.1), channel_id=1, source_target_pairs={{0,12},{4,8},{8,4},{12,0},{1,13},{5,9},{9,5},{13,1},{2,14},{6,10},... | collective-permute-start | bytes 491528 | tf_op jit(solution)/shard_map/kv/ppermute | solution.py:114
  5.8 0.8 collective-permute-start
  6.6 4.0 %collective-permute-start.3 = (bf16[2048]{0:T(1024)(128)(2,1)}, bf16[2048]{0:T(1024)(128)(2,1)S(1)}, u32[]{:S(2)}, u32[]{:S(2)}) collective-permute-start(bf16[2048]{0:T(1024)(128)(2,1)} %param.14), channel_id=1, source_target_pairs={{0,0},{1,4},{2,8},{3,12},{4,1},{5,5},{6,9},{7,13},{8,2},{9,6},{10,... | collective-permute-start | bytes 12296 | tf_op jit(solution)/shard_map/head/ppermute | solution.py:160
  10.7 0.7 reshape.35
  11.4 0.7 slice_reduce_fusion.1
  12.1 1.3 %fusion.8 = f32[1,144]{1,0:T(1,128)S(1)} fusion(bf16[144,2048]{1,0:T(8,128)(2,1)} %param.12, bf16[2048,1]{0,1:T(2,128)(2,1)S(1)} %reshape.35), kind=kOutput, calls=%fused_computation.47 | convolution fusion | flops 589824 | bytes 594496 | tf_op jit(solution)/shard_map/dot_general | solution.py:171
  13.4 0.8 multiply_reduce_fusion.1
  14.2 0.1 convert_reduce_fusion.3
  14.4 0.7 add_select_fusion.3
  15.1 0.1 pad_add_fusion
  15.2 1.0 slice.32
  16.2 0.1 copy.12.span_ref
  16.3 3.6 %collective-permute-done.1 = bf16[160,512]{1,0:T(8,128)(2,1)S(1)} collective-permute-done((bf16[160,512]{1,0:T(8,128)(2,1)}, bf16[160,512]{1,0:T(8,128)(2,1)S(1)}, u32[]{:S(2)}, u32[]{:S(2)}) %collective-permute-start.1) | collective-permute-done | bytes 163872 | tf_op jit(solution)/shard_map/kv/ppermute | solution.py:114
  20.1 0.1 convert_reduce_fusion.1
  20.2 2.8 %attention.1 = bf16[144,2048]{1,0:T(8,128)(2,1)S(1)} custom-call(bf16[144,2048]{1,0:T(8,128)(2,1)S(1)} %copy-done, bf16[576,512]{1,0:T(8,128)(2,1)S(1)} %pad_maximum_fusion.kv_ref, s32[1,576]{1,0:T(1,128)S(1)} %broadcast_in_dim.5.token_ref, s32[144,2]{1,0:T(8,128)S(1)} %copy.12.span_ref), custom_call_target="tpu_custom_call" | custom-call | tf_op jit(solution)/shard_map/attention/pallas_call | solution.py:49
  23.1 4.9 %convolution_convert_fusion.3 = bf16[144,2048]{1,0:T(8,128)(2,1)S(1)} fusion(bf16[144,2048]{1,0:T(8,128)(2,1)S(1)} %attention.1, bf16[2048,2048]{1,0:T(8,128)(2,1)} %param.13), kind=kOutput, calls=%fused_computation.3 | convolution fusion | flops 1208254464 | bytes 9568256 | tf_op jit(solution)/shard_map/dot_general | solution.py:181
  28.1 0.1 convert_reduce_fusion
  28.3 0.2 fusion.3
  28.4 10.9 %collective-permute-done.4 = bf16[144,2048]{1,0:T(8,128)(2,1)S(1)} collective-permute-done((bf16[144,2048]{1,0:T(8,128)(2,1)S(1)}, bf16[144,2048]{1,0:T(8,128)(2,1)S(1)}, u32[]{:S(2)}, u32[]{:S(2)}) %collective-permute-start.4) | collective-permute-done | bytes 589856 | tf_op jit(solution)/shard_map/heads/ppermute | solution.py:104
  39.3 1.4 %convolution_convert_fusion.2 = bf16[144,2048]{1,0:T(8,128)(2,1)S(1)} fusion(bf16[144,2048]{1,0:T(8,128)(2,1)S(1)} %collective-permute-done.4, bf16[2048,2048]{1,0:T(8,128)(2,1)S(1)} %bitcast.21), kind=kOutput, calls=%fused_computation.2 | convolution fusion | flops 1208254464 | bytes 9568256 | tf_op jit(solution)/shard_map/dot_general | solution.py:181
  40.8 0.2 fusion.9
  41.0 13.6 %collective-permute-done.5 = bf16[144,2048]{1,0:T(8,128)(2,1)S(1)} collective-permute-done((bf16[144,2048]{1,0:T(8,128)(2,1)S(1)}, bf16[144,2048]{1,0:T(8,128)(2,1)S(1)}, u32[]{:S(2)}, u32[]{:S(2)}) %collective-permute-start.5) | collective-permute-done | bytes 589856 | tf_op jit(solution)/shard_map/heads/ppermute | solution.py:104
  54.8 1.9 %collective-permute-done.7 = bf16[144,2048]{1,0:T(8,128)(2,1)S(1)} collective-permute-done((bf16[144,2048]{1,0:T(8,128)(2,1)S(1)}, bf16[144,2048]{1,0:T(8,128)(2,1)S(1)}, u32[]{:S(2)}, u32[]{:S(2)}) %collective-permute-start.7) | collective-permute-done | bytes 589856 | tf_op jit(solution)/shard_map/core01/ppermute | solution.py:160
  56.7 0.3 add_convert_fusion.4
  57.0 2.8 %collective-permute-start.8 = (bf16[144,2048]{1,0:T(8,128)(2,1)S(1)}, bf16[144,2048]{1,0:T(8,128)(2,1)S(1)}, u32[]{:S(2)}, u32[]{:S(2)}) collective-permute-start(bf16[144,2048]{1,0:T(8,128)(2,1)S(1)} %add_convert_fusion.4), channel_id=1, source_target_pairs={{1,3},{2,0},{4,6},{7,5},{8,10},{11,9},{13,15},{14,12},{17,19},{18,... | collective-permute-start | bytes 1769480 | tf_op jit(solution)/shard_map/x01/ppermute | solution.py:160
  59.8 4.8 %convolution_convert_fusion.1 = bf16[144,2048]{1,0:T(8,128)(2,1)S(1)} fusion(bf16[144,2048]{1,0:T(8,128)(2,1)S(1)} %collective-permute-done.5, bf16[2048,2048]{1,0:T(8,128)(2,1)} %param.13), kind=kOutput, calls=%fused_computation.1 | convolution fusion | flops 1208254464 | bytes 9568256 | tf_op jit(solution)/shard_map/dot_general | solution.py:181
  64.6 0.2 fusion.10
  64.8 7.4 %collective-permute-done.6 = bf16[144,2048]{1,0:T(8,128)(2,1)S(1)} collective-permute-done((bf16[144,2048]{1,0:T(8,128)(2,1)S(1)}, bf16[144,2048]{1,0:T(8,128)(2,1)S(1)}, u32[]{:S(2)}, u32[]{:S(2)}) %collective-permute-start.6) | collective-permute-done | bytes 589856 | tf_op jit(solution)/shard_map/heads/ppermute | solution.py:104
  72.3 1.5 %broadcast_select_fusion.1 = (bf16[144,2048]{1,0:T(8,128)(2,1)S(1)}, bf16[144,2048]{1,0:T(8,128)(2,1)S(1)}) fusion(bf16[144,2048]{1,0:T(8,128)(2,1)S(1)} %convolution_convert_fusion.1, pred[]{:T(512)S(6)} %eq.87, bf16[144,2048]{1,0:T(8,128)(2,1)S(1)} %collective-permute-done.6, bf16[2048,2048]{1,0:T(8,128)(2,1)S(1)} %bitcast.23), kind=kOutput, calls=%fused_computation.13 | convolution fusion | flops 1208549376 | bytes 10747905 | tf_op jit(solution)/shard_map/dot_general | solution.py:181
  73.8 0.2 fusion.11
  74.0 0.1 multiply_reduce_fusion
  74.2 0.6 collective-permute-start.10
  74.7 0.1 copy-done.1
  74.8 0.3 convert_add_fusion
  75.1 0.7 collective-permute-done.10
  75.8 0.5 broadcast_select_fusion
  76.3 2.5 %collective-permute-start.12 = (bf16[144,2048]{1,0:T(8,128)(2,1)S(1)}, bf16[144,2048]{1,0:T(8,128)(2,1)S(1)}, u32[]{:S(2)}, u32[]{:S(2)}) collective-permute-start(bf16[144,2048]{1,0:T(8,128)(2,1)S(1)} %get-tuple-element.51), channel_id=1, source_target_pairs={{2,0},{7,5},{8,10},{13,15},{18,16},{23,21},{24,26},{29,31}} | collective-permute-start | bytes 1769480 | tf_op jit(solution)/shard_map/x2/ppermute | solution.py:160
  78.9 0.7 collective-permute-start.11
  79.7 7.6 %collective-permute-done.13 = f32[16]{0:T(128)S(1)} collective-permute-done((f32[16]{0:T(128)S(1)}, f32[16]{0:T(128)S(1)}, u32[]{:S(2)}, u32[]{:S(2)}) %collective-permute-start.13) | collective-permute-done | bytes 96 | tf_op jit(solution)/shard_map/turns_chip/ppermute | solution.py:221
  87.3 0.2 fusion
  87.5 1.3 %collective-permute-start.14 = (bf16[144,2048]{1,0:T(8,128)(2,1)S(1)}, bf16[144,2048]{1,0:T(8,128)(2,1)S(1)}, u32[]{:S(2)}, u32[]{:S(2)}) collective-permute-start(bf16[144,2048]{1,0:T(8,128)(2,1)S(1)} %fusion), channel_id=1, source_target_pairs={{0,8},{3,4},{5,13},{6,9},{9,14},{10,2},{12,3},{15,7},{16,24},{19,2... | collective-permute-start | bytes 1769480 | tf_op jit(solution)/shard_map/home23/ppermute | solution.py:160
  88.8 3.7 %collective-permute-start.16 = (f32[16]{0:T(128)S(1)}, f32[16]{0:T(128)S(1)}, u32[]{:S(2)}, u32[]{:S(2)}) collective-permute-start(f32[16]{0:T(128)S(1)} %add.169), channel_id=1, source_target_pairs={{0,8},{4,12},{8,0},{12,4},{1,9},{5,13},{9,1},{13,5},{2,10},{6,14},... | collective-permute-start | bytes 200 | tf_op jit(solution)/shard_map/turns_ctx/ppermute | solution.py:104
  92.5 1.9 %collective-permute-start.15 = (f32[16]{0:T(128)S(1)}, f32[16]{0:T(128)S(1)}, u32[]{:S(2)}, u32[]{:S(2)}) collective-permute-start(f32[16]{0:T(128)S(1)} %add.169), channel_id=1, source_target_pairs={{0,4},{4,8},{8,12},{12,0},{1,5},{5,9},{9,13},{13,1},{2,6},{6,10},{... | collective-permute-start | bytes 200 | tf_op jit(solution)/shard_map/turns_ctx/ppermute | solution.py:104
  94.5 1.7 %collective-permute-done.17 = f32[16]{0:T(128)S(1)} collective-permute-done((f32[16]{0:T(128)S(1)}, f32[16]{0:T(128)S(1)}, u32[]{:S(2)}, u32[]{:S(2)}) %collective-permute-start.17) | collective-permute-done | bytes 96 | tf_op jit(solution)/shard_map/turns_ctx/ppermute | solution.py:104
  96.2 7.3 %collective-permute-done.16 = f32[16]{0:T(128)S(1)} collective-permute-done((f32[16]{0:T(128)S(1)}, f32[16]{0:T(128)S(1)}, u32[]{:S(2)}, u32[]{:S(2)}) %collective-permute-start.16) | collective-permute-done | bytes 96 | tf_op jit(solution)/shard_map/turns_ctx/ppermute | solution.py:104
  103.5 0.5 maximum_divide_fusion
  104.0 1.0 add_convert_fusion
  (51 shorter events, 0.8 us)
Async XLA Ops:
  2.2 17.7 %collective-permute-start.2 = (bf16[160,512]{1,0:T(8,128)(2,1)}, bf16[160,512]{1,0:T(8,128)(2,1)S(1)}, u32[]{:S(2)}, u32[]{:S(2)}) collective-permute-start(bf16[160,512]{1,0:T(8,128)(2,1)} %pack.1), channel_id=1, source_target_pairs={{0,12},{4,8},{8,4},{12,0},{1,13},{5,9},{9,5},{13,1},{2,14},{6,10},... | collective-permute-start | bytes 491528 | tf_op jit(solution)/shard_map/kv/ppermute | solution.py:114
  5.8 14.1 %collective-permute-start.1 = (bf16[160,512]{1,0:T(8,128)(2,1)}, bf16[160,512]{1,0:T(8,128)(2,1)S(1)}, u32[]{:S(2)}, u32[]{:S(2)}) collective-permute-start(bf16[160,512]{1,0:T(8,128)(2,1)} %pack.1), channel_id=1, source_target_pairs={{0,8},{4,12},{8,0},{12,4},{1,9},{5,13},{9,1},{13,5},{2,10},{6,14},... | collective-permute-start | bytes 491528 | tf_op jit(solution)/shard_map/kv/ppermute | solution.py:114
  5.8 14.2 %collective-permute-start = (bf16[160,512]{1,0:T(8,128)(2,1)}, bf16[160,512]{1,0:T(8,128)(2,1)S(1)}, u32[]{:S(2)}, u32[]{:S(2)}) collective-permute-start(bf16[160,512]{1,0:T(8,128)(2,1)} %pack.1), channel_id=1, source_target_pairs={{0,4},{4,0},{8,12},{12,8},{1,5},{5,1},{9,13},{13,9},{2,6},{6,2},{1... | collective-permute-start | bytes 491528 | tf_op jit(solution)/shard_map/kv/ppermute | solution.py:114
  6.6 16.4 %collective-permute-start.3 = (bf16[2048]{0:T(1024)(128)(2,1)}, bf16[2048]{0:T(1024)(128)(2,1)S(1)}, u32[]{:S(2)}, u32[]{:S(2)}) collective-permute-start(bf16[2048]{0:T(1024)(128)(2,1)} %param.14), channel_id=1, source_target_pairs={{0,0},{1,4},{2,8},{3,12},{4,1},{5,5},{6,9},{7,13},{8,2},{9,6},{10,... | collective-permute-start | bytes 12296 | tf_op jit(solution)/shard_map/head/ppermute | solution.py:160
  15.2 5.1 %copy-start = (bf16[144,2048]{1,0:T(8,128)(2,1)S(1)}, bf16[144,2048]{1,0:T(8,128)(2,1)}, u32[]{:S(2)}) copy-start(bf16[144,2048]{1,0:T(8,128)(2,1)} %q_ref.1) | copy-start | bytes 1769476
  20.2 19.1 %slice-start = ((s8[8388608]{0:T(1024)(128)(4,1)}), s8[4194304]{0:T(1024)(128)(4,1)S(1)}, s32[]{:S(2)}) async-start(s8[8388608]{0:T(1024)(128)(4,1)} %bitcast.20), calls=%async_computation | async-start | bytes 8388608
  23.0 16.3 %slice-start.1 = ((s8[8388608]{0:T(1024)(128)(4,1)}), s8[4194304]{0:T(1024)(128)(4,1)S(1)}, s32[]{:S(2)}) async-start(s8[8388608]{0:T(1024)(128)(4,1)} %bitcast.20), calls=%async_computation.1 | async-start | bytes 8388608
  23.1 16.2 %collective-permute-start.4 = (bf16[144,2048]{1,0:T(8,128)(2,1)S(1)}, bf16[144,2048]{1,0:T(8,128)(2,1)S(1)}, u32[]{:S(2)}, u32[]{:S(2)}) collective-permute-start(bf16[144,2048]{1,0:T(8,128)(2,1)S(1)} %attention.1), channel_id=1, source_target_pairs={{0,4},{4,8},{8,12},{12,0},{1,5},{5,9},{9,13},{13,1},{2,6},{6,10},{... | collective-permute-start | bytes 1769480 | tf_op jit(solution)/shard_map/heads/ppermute | solution.py:104
  39.3 15.3 %collective-permute-start.5 = (bf16[144,2048]{1,0:T(8,128)(2,1)S(1)}, bf16[144,2048]{1,0:T(8,128)(2,1)S(1)}, u32[]{:S(2)}, u32[]{:S(2)}) collective-permute-start(bf16[144,2048]{1,0:T(8,128)(2,1)S(1)} %collective-permute-done.4), channel_id=1, source_target_pairs={{0,4},{4,8},{8,12},{12,0},{1,5},{5,9},{9,13},{13,1},{2,6},{6,10},{... | collective-permute-start | bytes 1769480 | tf_op jit(solution)/shard_map/heads/ppermute | solution.py:104
  54.6 2.1 %collective-permute-start.7 = (bf16[144,2048]{1,0:T(8,128)(2,1)S(1)}, bf16[144,2048]{1,0:T(8,128)(2,1)S(1)}, u32[]{:S(2)}, u32[]{:S(2)}) collective-permute-start(bf16[144,2048]{1,0:T(8,128)(2,1)S(1)} %broadcast_select_fusion.2), channel_id=1, source_target_pairs={{0,1},{1,0},{2,3},{3,2},{4,5},{5,4},{6,7},{7,6},{8,9},{9,8},{10,11... | collective-permute-start | bytes 1769480 | tf_op jit(solution)/shard_map/core01/ppermute | solution.py:160
  54.7 17.5 %collective-permute-start.6 = (bf16[144,2048]{1,0:T(8,128)(2,1)S(1)}, bf16[144,2048]{1,0:T(8,128)(2,1)S(1)}, u32[]{:S(2)}, u32[]{:S(2)}) collective-permute-start(bf16[144,2048]{1,0:T(8,128)(2,1)S(1)} %collective-permute-done.5), channel_id=1, source_target_pairs={{0,4},{4,8},{8,12},{12,0},{1,5},{5,9},{9,13},{13,1},{2,6},{6,10},{... | collective-permute-start | bytes 1769480 | tf_op jit(solution)/shard_map/heads/ppermute | solution.py:104
  56.7 15.6 %slice-start.2 = ((s8[8388608]{0:T(1024)(128)(4,1)}), s8[4194304]{0:T(1024)(128)(4,1)S(1)}, s32[]{:S(2)}) async-start(s8[8388608]{0:T(1024)(128)(4,1)} %bitcast.22), calls=%async_computation.2 | async-start | bytes 8388608
  57.0 15.2 %slice-start.3 = ((s8[8388608]{0:T(1024)(128)(4,1)}), s8[4194304]{0:T(1024)(128)(4,1)S(1)}, s32[]{:S(2)}) async-start(s8[8388608]{0:T(1024)(128)(4,1)} %bitcast.22), calls=%async_computation.3 | async-start | bytes 8388608
  57.0 15.2 %collective-permute-start.8 = (bf16[144,2048]{1,0:T(8,128)(2,1)S(1)}, bf16[144,2048]{1,0:T(8,128)(2,1)S(1)}, u32[]{:S(2)}, u32[]{:S(2)}) collective-permute-start(bf16[144,2048]{1,0:T(8,128)(2,1)S(1)} %add_convert_fusion.4), channel_id=1, source_target_pairs={{1,3},{2,0},{4,6},{7,5},{8,10},{11,9},{13,15},{14,12},{17,19},{18,... | collective-permute-start | bytes 1769480 | tf_op jit(solution)/shard_map/x01/ppermute | solution.py:160
  73.7 1.1 %copy-start.1 = (bf16[144,2048]{1,0:T(8,128)(2,1)S(1)}, bf16[144,2048]{1,0:T(8,128)(2,1)}, u32[]{:S(2)}) copy-start(bf16[144,2048]{1,0:T(8,128)(2,1)} %param.12) | copy-start | bytes 1769476
  73.7 2.1 %collective-permute-start.9 = (bf16[144,2048]{1,0:T(8,128)(2,1)S(1)}, bf16[144,2048]{1,0:T(8,128)(2,1)S(1)}, u32[]{:S(2)}, u32[]{:S(2)}) collective-permute-start(bf16[144,2048]{1,0:T(8,128)(2,1)S(1)} %get-tuple-element.60), channel_id=1, source_target_pairs={{0,1},{1,0},{2,3},{3,2},{4,5},{5,4},{6,7},{7,6},{8,9},{9,8},{10,11... | collective-permute-start | bytes 1769480 | tf_op jit(solution)/shard_map/core23/ppermute | solution.py:160
  74.2 1.7 %collective-permute-start.10 = (f32[16]{0:T(128)S(1)}, f32[16]{0:T(128)S(1)}, u32[]{:S(2)}, u32[]{:S(2)}) collective-permute-start(f32[16]{0:T(128)S(1)} %add.165), channel_id=1, source_target_pairs={{0,1},{1,0},{2,3},{3,2},{4,5},{5,4},{6,7},{7,6},{8,9},{9,8},{10,11... | collective-permute-start | bytes 200 | tf_op jit(solution)/shard_map/turns_core/ppermute | solution.py:217
  76.3 11.0 %collective-permute-start.12 = (bf16[144,2048]{1,0:T(8,128)(2,1)S(1)}, bf16[144,2048]{1,0:T(8,128)(2,1)S(1)}, u32[]{:S(2)}, u32[]{:S(2)}) collective-permute-start(bf16[144,2048]{1,0:T(8,128)(2,1)S(1)} %get-tuple-element.51), channel_id=1, source_target_pairs={{2,0},{7,5},{8,10},{13,15},{18,16},{23,21},{24,26},{29,31}} | collective-permute-start | bytes 1769480 | tf_op jit(solution)/shard_map/x2/ppermute | solution.py:160
  78.9 8.4 %collective-permute-start.13 = (f32[16]{0:T(128)S(1)}, f32[16]{0:T(128)S(1)}, u32[]{:S(2)}, u32[]{:S(2)}) collective-permute-start(f32[16]{0:T(128)S(1)} %add.166), channel_id=1, source_target_pairs={{0,2},{1,3},{2,0},{3,1},{4,6},{5,7},{6,4},{7,5},{8,10},{9,11},{10,... | collective-permute-start | bytes 200 | tf_op jit(solution)/shard_map/turns_chip/ppermute | solution.py:221
  78.9 25.1 %collective-permute-start.11 = (bf16[144,2048]{1,0:T(8,128)(2,1)S(1)}, bf16[144,2048]{1,0:T(8,128)(2,1)S(1)}, u32[]{:S(2)}, u32[]{:S(2)}) collective-permute-start(bf16[144,2048]{1,0:T(8,128)(2,1)S(1)} %get-tuple-element.50), channel_id=1, source_target_pairs={{1,4},{3,12},{4,9},{6,1},{9,6},{11,14},{12,11},{14,3},{17,20},{19,... | collective-permute-start | bytes 1769480 | tf_op jit(solution)/shard_map/home13/ppermute | solution.py:160
  87.5 16.6 %collective-permute-start.14 = (bf16[144,2048]{1,0:T(8,128)(2,1)S(1)}, bf16[144,2048]{1,0:T(8,128)(2,1)S(1)}, u32[]{:S(2)}, u32[]{:S(2)}) collective-permute-start(bf16[144,2048]{1,0:T(8,128)(2,1)S(1)} %fusion), channel_id=1, source_target_pairs={{0,8},{3,4},{5,13},{6,9},{9,14},{10,2},{12,3},{15,7},{16,24},{19,2... | collective-permute-start | bytes 1769480 | tf_op jit(solution)/shard_map/home23/ppermute | solution.py:160
  88.8 7.4 %collective-permute-start.17 = (f32[16]{0:T(128)S(1)}, f32[16]{0:T(128)S(1)}, u32[]{:S(2)}, u32[]{:S(2)}) collective-permute-start(f32[16]{0:T(128)S(1)} %add.169), channel_id=1, source_target_pairs={{0,12},{4,0},{8,4},{12,8},{1,13},{5,1},{9,5},{13,9},{2,14},{6,2},{... | collective-permute-start | bytes 200 | tf_op jit(solution)/shard_map/turns_ctx/ppermute | solution.py:104
  88.8 14.7 %collective-permute-start.16 = (f32[16]{0:T(128)S(1)}, f32[16]{0:T(128)S(1)}, u32[]{:S(2)}, u32[]{:S(2)}) collective-permute-start(f32[16]{0:T(128)S(1)} %add.169), channel_id=1, source_target_pairs={{0,8},{4,12},{8,0},{12,4},{1,9},{5,13},{9,1},{13,5},{2,10},{6,14},... | collective-permute-start | bytes 200 | tf_op jit(solution)/shard_map/turns_ctx/ppermute | solution.py:104
  92.5 11.0 %collective-permute-start.15 = (f32[16]{0:T(128)S(1)}, f32[16]{0:T(128)S(1)}, u32[]{:S(2)}, u32[]{:S(2)}) collective-permute-start(f32[16]{0:T(128)S(1)} %add.169), channel_id=1, source_target_pairs={{0,4},{4,8},{8,12},{12,0},{1,5},{5,9},{9,13},{13,1},{2,6},{6,10},{... | collective-permute-start | bytes 200 | tf_op jit(solution)/shard_map/turns_ctx/ppermute | solution.py:104

commit v8 on v7

--- a/solution.py
+++ b/solution.py
@@ -230,7 +230,10 @@
         ),
     ]
     with jax.named_scope("turns_ctx"):
-        sums = sum([ring(sums, step) for step in range(1, n_ctx)], sums)
+        swapped = [
+            lax.ppermute(sums, "ctx", [(c, c ^ s) for c in range(n_ctx)]) for s in range(1, n_ctx)
+        ]
+        sums = (sums + swapped[0]) + (swapped[1] + swapped[2])
     return (add(base, *returned), sums / jnp.maximum(counts, 1.0))
 
 

time: 106 us -> 106 us (level)
  starting transfers between devices: 22.3 us -> 21 us
  waiting for transfers between devices: 54.8 us -> 56 us
    ppermute x0 -> x3, waiting for transfers between devices: none -> 10.3 us  [shards(): lax.ppermute(sums, 'ctx', [(c, c ^ s) for c in range(n_ctx)])]
    ppermute x6 -> x3, waiting for transfers between devices: 40.8 us -> 31.8 us  [ring(): lax.ppermute(x, 'ctx', [(i, (i + step) % n_ctx) for i in range(n_ctx)])]
    ppermute x6 -> x3, starting transfers between devices: 5.83 us -> 0.12 us  [ring(): lax.ppermute(x, 'ctx', [(i, (i + step) % n_ctx) for i in range(n_ctx)])]
    ppermute x0 -> x3, starting transfers between devices: none -> 4.45 us  [shards(): lax.ppermute(sums, 'ctx', [(c, c ^ s) for c in range(n_ctx)])]
where the time goes in v8:
time: 106 us; the launch traced here: 105 us
  waiting for transfers between devices  56 us (53%)
  starting transfers between devices  21 us (20%)
  matrix products  14.7 us (14%)
  other arithmetic  5.18 us (5%)
  Pallas kernels  4.41 us (4%)
  local copies, waits for them, and re-layouts  2.69 us (3%)
    ppermute x3, waiting for transfers between devices, ring(): lax.ppermute(x, 'ctx', [(i, (i + step) % n_ctx) for i in range(n_ctx)])  31.8 us
    dot_general x4, matrix products, project(): jnp.dot(piece, out_weight, preferred_element_type=wide).astype(jnp.bfloat16)  12.6 us
    ppermute x7, starting transfers between devices, send(): return lax.ppermute(x, both, pairs)  11.5 us
    ppermute x3, waiting for transfers between devices, shards(): lax.ppermute(sums, 'ctx', [(c, c ^ s) for c in range(n_ctx)])  10.3 us
    ppermute x1, waiting for transfers between devices, shards(): sums = sums + lax.ppermute(sums, 'tp', [(t, t ^ 2) for t in range(n_tp)])  7.63 us
    ppermute x3, starting transfers between devices, shards(): lax.ppermute(sums, 'ctx', [(c, c ^ s) for c in range(n_ctx)])  4.45 us
    ppermute x3, starting transfers between devices, shards(): lax.ppermute(packed, 'ctx', [(c, c ^ s) for c in range(n_ctx)])  4.39 us
    ppermute x3, waiting for transfers between devices, shards(): lax.ppermute(packed, 'ctx', [(c, c ^ s) for c in range(n_ctx)])  3.64 us
  transfers between devices with their start and end apart: 18, of which 9 were waited for; matrix products, arithmetic and copies ran while one was open for 18% of the time, Pallas kernels for 3%

profile of v8, /device:TPU:2, one launch (start us, length us, event | category | flops | bytes accessed | tf_op | source)
XLA Modules:
  0.0 105.1 jit_solution(11049374909216525321)
XLA Ops:
  0.6 1.6 %pack.1 = bf16[160,512]{1,0:T(8,128)(2,1)} custom-call(bf16[144,256]{1,0:T(8,128)(2,1)} %key_ref.1, bf16[144,256]{1,0:T(8,128)(2,1)} %value_ref.1, s32[1,144]{1,0:T(1,128)} %bitcast.24), custom_call_target="tpu_custom_call" | custom-call | tf_op jit(solution)/shard_map/pack/pallas_call | solution.py:78
  2.2 3.6 %collective-permute-start.2 = (bf16[160,512]{1,0:T(8,128)(2,1)}, bf16[160,512]{1,0:T(8,128)(2,1)S(1)}, u32[]{:S(2)}, u32[]{:S(2)}) collective-permute-start(bf16[160,512]{1,0:T(8,128)(2,1)} %pack.1), channel_id=1, source_target_pairs={{0,12},{4,8},{8,4},{12,0},{1,13},{5,9},{9,5},{13,1},{2,14},{6,10},... | collective-permute-start | bytes 491528 | tf_op jit(solution)/shard_map/kv/ppermute | solution.py:114
  5.8 0.8 collective-permute-start
  6.6 4.0 %collective-permute-start.3 = (bf16[2048]{0:T(1024)(128)(2,1)}, bf16[2048]{0:T(1024)(128)(2,1)S(1)}, u32[]{:S(2)}, u32[]{:S(2)}) collective-permute-start(bf16[2048]{0:T(1024)(128)(2,1)} %param.14), channel_id=1, source_target_pairs={{0,0},{1,4},{2,8},{3,12},{4,1},{5,5},{6,9},{7,13},{8,2},{9,6},{10,... | collective-permute-start | bytes 12296 | tf_op jit(solution)/shard_map/head/ppermute | solution.py:160
  10.7 0.7 reshape.35
  11.4 0.7 slice_reduce_fusion.1
  12.1 1.3 %fusion.8 = f32[1,144]{1,0:T(1,128)S(1)} fusion(bf16[144,2048]{1,0:T(8,128)(2,1)} %param.12, bf16[2048,1]{0,1:T(2,128)(2,1)S(1)} %reshape.35), kind=kOutput, calls=%fused_computation.47 | convolution fusion | flops 589824 | bytes 594496 | tf_op jit(solution)/shard_map/dot_general | solution.py:171
  13.4 0.8 multiply_reduce_fusion.1
  14.2 0.1 convert_reduce_fusion.3
  14.4 0.7 add_select_fusion.3
  15.1 0.1 pad_add_fusion
  15.2 1.0 slice.32
  16.2 0.1 copy.12.span_ref
  16.3 3.6 %collective-permute-done.1 = bf16[160,512]{1,0:T(8,128)(2,1)S(1)} collective-permute-done((bf16[160,512]{1,0:T(8,128)(2,1)}, bf16[160,512]{1,0:T(8,128)(2,1)S(1)}, u32[]{:S(2)}, u32[]{:S(2)}) %collective-permute-start.1) | collective-permute-done | bytes 163872 | tf_op jit(solution)/shard_map/kv/ppermute | solution.py:114
  20.1 0.1 convert_reduce_fusion.1
  20.2 2.8 %attention.1 = bf16[144,2048]{1,0:T(8,128)(2,1)S(1)} custom-call(bf16[144,2048]{1,0:T(8,128)(2,1)S(1)} %copy-done, bf16[576,512]{1,0:T(8,128)(2,1)S(1)} %pad_maximum_fusion.kv_ref, s32[1,576]{1,0:T(1,128)S(1)} %broadcast_in_dim.5.token_ref, s32[144,2]{1,0:T(8,128)S(1)} %copy.12.span_ref), custom_call_target="tpu_custom_call" | custom-call | tf_op jit(solution)/shard_map/attention/pallas_call | solution.py:49
  23.1 4.9 %convolution_convert_fusion.3 = bf16[144,2048]{1,0:T(8,128)(2,1)S(1)} fusion(bf16[144,2048]{1,0:T(8,128)(2,1)S(1)} %attention.1, bf16[2048,2048]{1,0:T(8,128)(2,1)} %param.13), kind=kOutput, calls=%fused_computation.3 | convolution fusion | flops 1208254464 | bytes 9568256 | tf_op jit(solution)/shard_map/dot_general | solution.py:181
  28.1 0.1 convert_reduce_fusion
  28.3 0.2 fusion.3
  28.4 10.9 %collective-permute-done.4 = bf16[144,2048]{1,0:T(8,128)(2,1)S(1)} collective-permute-done((bf16[144,2048]{1,0:T(8,128)(2,1)S(1)}, bf16[144,2048]{1,0:T(8,128)(2,1)S(1)}, u32[]{:S(2)}, u32[]{:S(2)}) %collective-permute-start.4) | collective-permute-done | bytes 589856 | tf_op jit(solution)/shard_map/heads/ppermute | solution.py:104
  39.3 1.4 %convolution_convert_fusion.2 = bf16[144,2048]{1,0:T(8,128)(2,1)S(1)} fusion(bf16[144,2048]{1,0:T(8,128)(2,1)S(1)} %collective-permute-done.4, bf16[2048,2048]{1,0:T(8,128)(2,1)S(1)} %bitcast.21), kind=kOutput, calls=%fused_computation.2 | convolution fusion | flops 1208254464 | bytes 9568256 | tf_op jit(solution)/shard_map/dot_general | solution.py:181
  40.8 0.2 fusion.9
  41.0 13.6 %collective-permute-done.5 = bf16[144,2048]{1,0:T(8,128)(2,1)S(1)} collective-permute-done((bf16[144,2048]{1,0:T(8,128)(2,1)S(1)}, bf16[144,2048]{1,0:T(8,128)(2,1)S(1)}, u32[]{:S(2)}, u32[]{:S(2)}) %collective-permute-start.5) | collective-permute-done | bytes 589856 | tf_op jit(solution)/shard_map/heads/ppermute | solution.py:104
  54.8 1.9 %collective-permute-done.7 = bf16[144,2048]{1,0:T(8,128)(2,1)S(1)} collective-permute-done((bf16[144,2048]{1,0:T(8,128)(2,1)S(1)}, bf16[144,2048]{1,0:T(8,128)(2,1)S(1)}, u32[]{:S(2)}, u32[]{:S(2)}) %collective-permute-start.7) | collective-permute-done | bytes 589856 | tf_op jit(solution)/shard_map/core01/ppermute | solution.py:160
  56.7 0.3 add_convert_fusion.4
  57.0 2.8 %collective-permute-start.8 = (bf16[144,2048]{1,0:T(8,128)(2,1)S(1)}, bf16[144,2048]{1,0:T(8,128)(2,1)S(1)}, u32[]{:S(2)}, u32[]{:S(2)}) collective-permute-start(bf16[144,2048]{1,0:T(8,128)(2,1)S(1)} %add_convert_fusion.4), channel_id=1, source_target_pairs={{1,3},{2,0},{4,6},{7,5},{8,10},{11,9},{13,15},{14,12},{17,19},{18,... | collective-permute-start | bytes 1769480 | tf_op jit(solution)/shard_map/x01/ppermute | solution.py:160
  59.8 4.8 %convolution_convert_fusion.1 = bf16[144,2048]{1,0:T(8,128)(2,1)S(1)} fusion(bf16[144,2048]{1,0:T(8,128)(2,1)S(1)} %collective-permute-done.5, bf16[2048,2048]{1,0:T(8,128)(2,1)} %param.13), kind=kOutput, calls=%fused_computation.1 | convolution fusion | flops 1208254464 | bytes 9568256 | tf_op jit(solution)/shard_map/dot_general | solution.py:181
  64.6 0.2 fusion.10
  64.8 7.4 %collective-permute-done.6 = bf16[144,2048]{1,0:T(8,128)(2,1)S(1)} collective-permute-done((bf16[144,2048]{1,0:T(8,128)(2,1)S(1)}, bf16[144,2048]{1,0:T(8,128)(2,1)S(1)}, u32[]{:S(2)}, u32[]{:S(2)}) %collective-permute-start.6) | collective-permute-done | bytes 589856 | tf_op jit(solution)/shard_map/heads/ppermute | solution.py:104
  72.3 1.5 %broadcast_select_fusion.1 = (bf16[144,2048]{1,0:T(8,128)(2,1)S(1)}, bf16[144,2048]{1,0:T(8,128)(2,1)S(1)}) fusion(bf16[144,2048]{1,0:T(8,128)(2,1)S(1)} %convolution_convert_fusion.1, pred[]{:T(512)S(6)} %eq.87, bf16[144,2048]{1,0:T(8,128)(2,1)S(1)} %collective-permute-done.6, bf16[2048,2048]{1,0:T(8,128)(2,1)S(1)} %bitcast.23), kind=kOutput, calls=%fused_computation.13 | convolution fusion | flops 1208549376 | bytes 10747905 | tf_op jit(solution)/shard_map/dot_general | solution.py:181
  73.8 0.2 fusion.11
  74.0 0.1 multiply_reduce_fusion
  74.2 0.6 collective-permute-start.10
  74.7 0.1 copy-done.1
  74.8 0.3 convert_add_fusion
  75.1 0.7 collective-permute-done.10
  75.8 0.5 broadcast_select_fusion
  76.3 2.5 %collective-permute-start.12 = (bf16[144,2048]{1,0:T(8,128)(2,1)S(1)}, bf16[144,2048]{1,0:T(8,128)(2,1)S(1)}, u32[]{:S(2)}, u32[]{:S(2)}) collective-permute-start(bf16[144,2048]{1,0:T(8,128)(2,1)S(1)} %get-tuple-element.51), channel_id=1, source_target_pairs={{2,0},{7,5},{8,10},{13,15},{18,16},{23,21},{24,26},{29,31}} | collective-permute-start | bytes 1769480 | tf_op jit(solution)/shard_map/x2/ppermute | solution.py:160
  78.9 0.7 collective-permute-start.11
  79.7 7.6 %collective-permute-done.13 = f32[16]{0:T(128)S(1)} collective-permute-done((f32[16]{0:T(128)S(1)}, f32[16]{0:T(128)S(1)}, u32[]{:S(2)}, u32[]{:S(2)}) %collective-permute-start.13) | collective-permute-done | bytes 96 | tf_op jit(solution)/shard_map/turns_chip/ppermute | solution.py:221
  87.3 0.2 fusion
  87.5 1.3 %collective-permute-start.14 = (bf16[144,2048]{1,0:T(8,128)(2,1)S(1)}, bf16[144,2048]{1,0:T(8,128)(2,1)S(1)}, u32[]{:S(2)}, u32[]{:S(2)}) collective-permute-start(bf16[144,2048]{1,0:T(8,128)(2,1)S(1)} %fusion), channel_id=1, source_target_pairs={{0,8},{3,4},{5,13},{6,9},{9,14},{10,2},{12,3},{15,7},{16,24},{19,2... | collective-permute-start | bytes 1769480 | tf_op jit(solution)/shard_map/home23/ppermute | solution.py:160
  88.9 3.7 %collective-permute-start.16 = (f32[16]{0:T(128)S(1)}, f32[16]{0:T(128)S(1)}, u32[]{:S(2)}, u32[]{:S(2)}) collective-permute-start(f32[16]{0:T(128)S(1)} %add.169), channel_id=1, source_target_pairs={{0,8},{4,12},{8,0},{12,4},{1,9},{5,13},{9,1},{13,5},{2,10},{6,14},... | collective-permute-start | bytes 200 | tf_op jit(solution)/shard_map/turns_ctx/ppermute | solution.py:234
  92.6 0.7 collective-permute-start.15
  93.2 1.1 %collective-permute-done.17 = f32[16]{0:T(128)S(1)} collective-permute-done((f32[16]{0:T(128)S(1)}, f32[16]{0:T(128)S(1)}, u32[]{:S(2)}, u32[]{:S(2)}) %collective-permute-start.17) | collective-permute-done | bytes 96 | tf_op jit(solution)/shard_map/turns_ctx/ppermute | solution.py:234
  94.4 9.1 %collective-permute-done.16 = f32[16]{0:T(128)S(1)} collective-permute-done((f32[16]{0:T(128)S(1)}, f32[16]{0:T(128)S(1)}, u32[]{:S(2)}, u32[]{:S(2)}) %collective-permute-start.16) | collective-permute-done | bytes 96 | tf_op jit(solution)/shard_map/turns_ctx/ppermute | solution.py:234
  103.5 0.5 maximum_divide_fusion
  104.0 1.0 add_convert_fusion
  (51 shorter events, 0.8 us)
Async XLA Ops:
  2.2 17.7 %collective-permute-start.2 = (bf16[160,512]{1,0:T(8,128)(2,1)}, bf16[160,512]{1,0:T(8,128)(2,1)S(1)}, u32[]{:S(2)}, u32[]{:S(2)}) collective-permute-start(bf16[160,512]{1,0:T(8,128)(2,1)} %pack.1), channel_id=1, source_target_pairs={{0,12},{4,8},{8,4},{12,0},{1,13},{5,9},{9,5},{13,1},{2,14},{6,10},... | collective-permute-start | bytes 491528 | tf_op jit(solution)/shard_map/kv/ppermute | solution.py:114
  5.8 14.1 %collective-permute-start.1 = (bf16[160,512]{1,0:T(8,128)(2,1)}, bf16[160,512]{1,0:T(8,128)(2,1)S(1)}, u32[]{:S(2)}, u32[]{:S(2)}) collective-permute-start(bf16[160,512]{1,0:T(8,128)(2,1)} %pack.1), channel_id=1, source_target_pairs={{0,8},{4,12},{8,0},{12,4},{1,9},{5,13},{9,1},{13,5},{2,10},{6,14},... | collective-permute-start | bytes 491528 | tf_op jit(solution)/shard_map/kv/ppermute | solution.py:114
  5.8 14.2 %collective-permute-start = (bf16[160,512]{1,0:T(8,128)(2,1)}, bf16[160,512]{1,0:T(8,128)(2,1)S(1)}, u32[]{:S(2)}, u32[]{:S(2)}) collective-permute-start(bf16[160,512]{1,0:T(8,128)(2,1)} %pack.1), channel_id=1, source_target_pairs={{0,4},{4,0},{8,12},{12,8},{1,5},{5,1},{9,13},{13,9},{2,6},{6,2},{1... | collective-permute-start | bytes 491528 | tf_op jit(solution)/shard_map/kv/ppermute | solution.py:114
  6.6 16.4 %collective-permute-start.3 = (bf16[2048]{0:T(1024)(128)(2,1)}, bf16[2048]{0:T(1024)(128)(2,1)S(1)}, u32[]{:S(2)}, u32[]{:S(2)}) collective-permute-start(bf16[2048]{0:T(1024)(128)(2,1)} %param.14), channel_id=1, source_target_pairs={{0,0},{1,4},{2,8},{3,12},{4,1},{5,5},{6,9},{7,13},{8,2},{9,6},{10,... | collective-permute-start | bytes 12296 | tf_op jit(solution)/shard_map/head/ppermute | solution.py:160
  15.2 5.1 %copy-start = (bf16[144,2048]{1,0:T(8,128)(2,1)S(1)}, bf16[144,2048]{1,0:T(8,128)(2,1)}, u32[]{:S(2)}) copy-start(bf16[144,2048]{1,0:T(8,128)(2,1)} %q_ref.1) | copy-start | bytes 1769476
  20.2 19.1 %slice-start = ((s8[8388608]{0:T(1024)(128)(4,1)}), s8[4194304]{0:T(1024)(128)(4,1)S(1)}, s32[]{:S(2)}) async-start(s8[8388608]{0:T(1024)(128)(4,1)} %bitcast.20), calls=%async_computation | async-start | bytes 8388608
  23.0 16.3 %slice-start.1 = ((s8[8388608]{0:T(1024)(128)(4,1)}), s8[4194304]{0:T(1024)(128)(4,1)S(1)}, s32[]{:S(2)}) async-start(s8[8388608]{0:T(1024)(128)(4,1)} %bitcast.20), calls=%async_computation.1 | async-start | bytes 8388608
  23.1 16.2 %collective-permute-start.4 = (bf16[144,2048]{1,0:T(8,128)(2,1)S(1)}, bf16[144,2048]{1,0:T(8,128)(2,1)S(1)}, u32[]{:S(2)}, u32[]{:S(2)}) collective-permute-start(bf16[144,2048]{1,0:T(8,128)(2,1)S(1)} %attention.1), channel_id=1, source_target_pairs={{0,4},{4,8},{8,12},{12,0},{1,5},{5,9},{9,13},{13,1},{2,6},{6,10},{... | collective-permute-start | bytes 1769480 | tf_op jit(solution)/shard_map/heads/ppermute | solution.py:104
  39.3 15.3 %collective-permute-start.5 = (bf16[144,2048]{1,0:T(8,128)(2,1)S(1)}, bf16[144,2048]{1,0:T(8,128)(2,1)S(1)}, u32[]{:S(2)}, u32[]{:S(2)}) collective-permute-start(bf16[144,2048]{1,0:T(8,128)(2,1)S(1)} %collective-permute-done.4), channel_id=1, source_target_pairs={{0,4},{4,8},{8,12},{12,0},{1,5},{5,9},{9,13},{13,1},{2,6},{6,10},{... | collective-permute-start | bytes 1769480 | tf_op jit(solution)/shard_map/heads/ppermute | solution.py:104
  54.6 2.1 %collective-permute-start.7 = (bf16[144,2048]{1,0:T(8,128)(2,1)S(1)}, bf16[144,2048]{1,0:T(8,128)(2,1)S(1)}, u32[]{:S(2)}, u32[]{:S(2)}) collective-permute-start(bf16[144,2048]{1,0:T(8,128)(2,1)S(1)} %broadcast_select_fusion.2), channel_id=1, source_target_pairs={{0,1},{1,0},{2,3},{3,2},{4,5},{5,4},{6,7},{7,6},{8,9},{9,8},{10,11... | collective-permute-start | bytes 1769480 | tf_op jit(solution)/shard_map/core01/ppermute | solution.py:160
  54.7 17.5 %collective-permute-start.6 = (bf16[144,2048]{1,0:T(8,128)(2,1)S(1)}, bf16[144,2048]{1,0:T(8,128)(2,1)S(1)}, u32[]{:S(2)}, u32[]{:S(2)}) collective-permute-start(bf16[144,2048]{1,0:T(8,128)(2,1)S(1)} %collective-permute-done.5), channel_id=1, source_target_pairs={{0,4},{4,8},{8,12},{12,0},{1,5},{5,9},{9,13},{13,1},{2,6},{6,10},{... | collective-permute-start | bytes 1769480 | tf_op jit(solution)/shard_map/heads/ppermute | solution.py:104
  56.7 15.6 %slice-start.2 = ((s8[8388608]{0:T(1024)(128)(4,1)}), s8[4194304]{0:T(1024)(128)(4,1)S(1)}, s32[]{:S(2)}) async-start(s8[8388608]{0:T(1024)(128)(4,1)} %bitcast.22), calls=%async_computation.2 | async-start | bytes 8388608
  57.0 15.2 %slice-start.3 = ((s8[8388608]{0:T(1024)(128)(4,1)}), s8[4194304]{0:T(1024)(128)(4,1)S(1)}, s32[]{:S(2)}) async-start(s8[8388608]{0:T(1024)(128)(4,1)} %bitcast.22), calls=%async_computation.3 | async-start | bytes 8388608
  57.0 15.2 %collective-permute-start.8 = (bf16[144,2048]{1,0:T(8,128)(2,1)S(1)}, bf16[144,2048]{1,0:T(8,128)(2,1)S(1)}, u32[]{:S(2)}, u32[]{:S(2)}) collective-permute-start(bf16[144,2048]{1,0:T(8,128)(2,1)S(1)} %add_convert_fusion.4), channel_id=1, source_target_pairs={{1,3},{2,0},{4,6},{7,5},{8,10},{11,9},{13,15},{14,12},{17,19},{18,... | collective-permute-start | bytes 1769480 | tf_op jit(solution)/shard_map/x01/ppermute | solution.py:160
  73.7 1.1 %copy-start.1 = (bf16[144,2048]{1,0:T(8,128)(2,1)S(1)}, bf16[144,2048]{1,0:T(8,128)(2,1)}, u32[]{:S(2)}) copy-start(bf16[144,2048]{1,0:T(8,128)(2,1)} %param.12) | copy-start | bytes 1769476
  73.7 2.1 %collective-permute-start.9 = (bf16[144,2048]{1,0:T(8,128)(2,1)S(1)}, bf16[144,2048]{1,0:T(8,128)(2,1)S(1)}, u32[]{:S(2)}, u32[]{:S(2)}) collective-permute-start(bf16[144,2048]{1,0:T(8,128)(2,1)S(1)} %get-tuple-element.60), channel_id=1, source_target_pairs={{0,1},{1,0},{2,3},{3,2},{4,5},{5,4},{6,7},{7,6},{8,9},{9,8},{10,11... | collective-permute-start | bytes 1769480 | tf_op jit(solution)/shard_map/core23/ppermute | solution.py:160
  74.2 1.7 %collective-permute-start.10 = (f32[16]{0:T(128)S(1)}, f32[16]{0:T(128)S(1)}, u32[]{:S(2)}, u32[]{:S(2)}) collective-permute-start(f32[16]{0:T(128)S(1)} %add.165), channel_id=1, source_target_pairs={{0,1},{1,0},{2,3},{3,2},{4,5},{5,4},{6,7},{7,6},{8,9},{9,8},{10,11... | collective-permute-start | bytes 200 | tf_op jit(solution)/shard_map/turns_core/ppermute | solution.py:217
  76.3 11.0 %collective-permute-start.12 = (bf16[144,2048]{1,0:T(8,128)(2,1)S(1)}, bf16[144,2048]{1,0:T(8,128)(2,1)S(1)}, u32[]{:S(2)}, u32[]{:S(2)}) collective-permute-start(bf16[144,2048]{1,0:T(8,128)(2,1)S(1)} %get-tuple-element.51), channel_id=1, source_target_pairs={{2,0},{7,5},{8,10},{13,15},{18,16},{23,21},{24,26},{29,31}} | collective-permute-start | bytes 1769480 | tf_op jit(solution)/shard_map/x2/ppermute | solution.py:160
  78.9 8.4 %collective-permute-start.13 = (f32[16]{0:T(128)S(1)}, f32[16]{0:T(128)S(1)}, u32[]{:S(2)}, u32[]{:S(2)}) collective-permute-start(f32[16]{0:T(128)S(1)} %add.166), channel_id=1, source_target_pairs={{0,2},{1,3},{2,0},{3,1},{4,6},{5,7},{6,4},{7,5},{8,10},{9,11},{10,... | collective-permute-start | bytes 200 | tf_op jit(solution)/shard_map/turns_chip/ppermute | solution.py:221
  78.9 25.1 %collective-permute-start.11 = (bf16[144,2048]{1,0:T(8,128)(2,1)S(1)}, bf16[144,2048]{1,0:T(8,128)(2,1)S(1)}, u32[]{:S(2)}, u32[]{:S(2)}) collective-permute-start(bf16[144,2048]{1,0:T(8,128)(2,1)S(1)} %get-tuple-element.50), channel_id=1, source_target_pairs={{1,4},{3,12},{4,9},{6,1},{9,6},{11,14},{12,11},{14,3},{17,20},{19,... | collective-permute-start | bytes 1769480 | tf_op jit(solution)/shard_map/home13/ppermute | solution.py:160
  87.5 16.6 %collective-permute-start.14 = (bf16[144,2048]{1,0:T(8,128)(2,1)S(1)}, bf16[144,2048]{1,0:T(8,128)(2,1)S(1)}, u32[]{:S(2)}, u32[]{:S(2)}) collective-permute-start(bf16[144,2048]{1,0:T(8,128)(2,1)S(1)} %fusion), channel_id=1, source_target_pairs={{0,8},{3,4},{5,13},{6,9},{9,14},{10,2},{12,3},{15,7},{16,24},{19,2... | collective-permute-start | bytes 1769480 | tf_op jit(solution)/shard_map/home23/ppermute | solution.py:160
  88.8 5.6 %collective-permute-start.17 = (f32[16]{0:T(128)S(1)}, f32[16]{0:T(128)S(1)}, u32[]{:S(2)}, u32[]{:S(2)}) collective-permute-start(f32[16]{0:T(128)S(1)} %add.169), channel_id=1, source_target_pairs={{0,12},{4,8},{8,4},{12,0},{1,13},{5,9},{9,5},{13,1},{2,14},{6,10},... | collective-permute-start | bytes 200 | tf_op jit(solution)/shard_map/turns_ctx/ppermute | solution.py:234
  88.9 14.6 %collective-permute-start.16 = (f32[16]{0:T(128)S(1)}, f32[16]{0:T(128)S(1)}, u32[]{:S(2)}, u32[]{:S(2)}) collective-permute-start(f32[16]{0:T(128)S(1)} %add.169), channel_id=1, source_target_pairs={{0,8},{4,12},{8,0},{12,4},{1,9},{5,13},{9,1},{13,5},{2,10},{6,14},... | collective-permute-start | bytes 200 | tf_op jit(solution)/shard_map/turns_ctx/ppermute | solution.py:234
  92.6 10.9 %collective-permute-start.15 = (f32[16]{0:T(128)S(1)}, f32[16]{0:T(128)S(1)}, u32[]{:S(2)}, u32[]{:S(2)}) collective-permute-start(f32[16]{0:T(128)S(1)} %add.169), channel_id=1, source_target_pairs={{0,4},{4,0},{8,12},{12,8},{1,5},{5,1},{9,13},{13,9},{2,6},{6,2},{1... | collective-permute-start | bytes 200 | tf_op jit(solution)/shard_map/turns_ctx/ppermute | solution.py:234
